TPU v7x, 512 devices: a whole 4x4x16 slice. The times are simulated.
512 devices in a mesh: role: 2 (over x_lo), grp: 16 (over z), tp: 16 (over y, x_hi, core).
Axes of the slice: x: 4 (x_hi: 2, x_lo: 2; x = x_hi * 2 + x_lo), y: 4, z: 16, core: 2. Of those that a mesh axis runs over, the one named last changes fastest.
Arguments:
- prompt_acts: bfloat16 [2, 16, 1024, 8192], P('role', 'grp', None, 'tp'), may hold values from -6 to 6
- kv_weight: bfloat16 [8192, 2048], P('tp'), may hold values from -0.0625 to 0.0625
- cache_kv: bfloat16 [2, 32, 3072, 2048], P('role', 'grp', 'tp'), may hold values from -6 to 6
- cache_len: int32 [2, 32], P('role', 'grp'), may hold values from 1 to 3072, as said below
- block_owner: int32 [2, 32, 16], P('role', 'grp'), may hold values from 0 to 15, each once within a row
- span_row: int32 [2, 16], P('role', 'grp'), may hold values from 0 to 1
- draft_query: bfloat16 [2, 32, 4, 8192], P('role', 'grp')
- draft_kv: bfloat16 [2, 32, 4, 2048], P('role', 'grp'), may hold values from -4 to 4
Outputs:
- attn_out: bfloat16 [2, 32, 4, 8192], P('role', 'grp')
Inputs may be any that keep to these rules, and one draw needn't show every extreme that they name: `cache_len`: some row of each pool has 3072 live positions. `block_owner`: each row's entries are a permutation of the slabs.
All inputs are finite; a program needn't handle non-finite values.
Results may differ from a plain program's by a relative error of at most 0.02.
Values may be sent and summed in bfloat16 or wider, within the bound.
No kernel may reach another device: no remote copies, remote signals or barrier semaphores. Data moves between devices by JAX's collectives and lax.ppermute only.
A program may use at most 64 MiB of HBM per device.

v0:
```python
import math

import jax
import jax.numpy as jnp
from jax import lax
from jax.sharding import PartitionSpec as P

QH = 64
KVH = 8
HD = 128
DRAFT = 4


NEG = -1e30


def partner(x, axis, stride):
    return lax.ppermute(x, axis, [(i, i ^ 1 << stride) for i in range(lax.axis_size(axis))])


def joined(x, axis, combine):
    everything = jax.tree.map(lambda part: lax.all_gather(part, axis), x)
    initial = jax.tree.map(lambda part: part[0], everything)

    def lap(k, so_far):
        return combine(so_far, jax.tree.map(lambda part: part[k], everything))

    return lax.fori_loop(1, lax.axis_size(axis), lap, initial)


def combine(first, second):
    top = jnp.maximum(first[0], second[0])
    scale_a = jnp.exp(first[0] - top)
    scale_b = jnp.exp(second[0] - top)
    return (
        top,
        first[1] * scale_a + second[1] * scale_b,
        first[2] * scale_a[..., None] + second[2] * scale_b[..., None],
    )


def shards(
    prompt_acts, kv_weight, cache_kv, cache_len, block_owner, span_row, draft_query, draft_kv
):
    acts = prompt_acts[0, 0]
    n_tp = lax.axis_size("tp")
    span = acts.shape[0]
    block_rows = span // n_tp
    partial_value = jnp.dot(acts, kv_weight, preferred_element_type=jnp.float32)
    columns = lax.psum_scatter(
        partial_value.astype(jnp.bfloat16), "tp", scatter_dimension=1, tiled=True
    )
    pieces = lax.all_to_all(columns, "tp", split_axis=0, concat_axis=1, tiled=True)
    fresh = partner(pieces, "role", 0)
    cache = cache_kv[0]
    rows_here = cache.shape[0]
    slab = cache.shape[1]
    head_cols = KVH * HD
    qgroup = QH // KVH
    scale = 1.0 / math.sqrt(HD)
    me = lax.axis_index("tp")
    slabs = jnp.arange(n_tp, dtype=jnp.int32)
    first = jnp.sum(slabs[None, :] * (block_owner[0] == me).astype(jnp.int32), axis=1)
    position = first[:, None] * slab + jnp.arange(slab, dtype=jnp.int32)[None, :]
    live = position < cache_len[0][:, None]
    chosen = span_row[0, 0] == jnp.arange(rows_here, dtype=jnp.int32)
    taken = jnp.broadcast_to(chosen[:, None], (rows_here, block_rows))
    query = draft_query[0].reshape(rows_here, DRAFT, KVH, qgroup, HD)
    cache_keys = cache[..., :head_cols].reshape(rows_here, slab, KVH, HD)
    cache_vals = cache[..., head_cols:].reshape(rows_here, slab, KVH, HD)
    fresh_keys = fresh[:, :head_cols].reshape(-1, KVH, HD)
    fresh_vals = fresh[:, head_cols:].reshape(-1, KVH, HD)
    live_mask = live[:, None, None, None, :]
    taken_mask = taken[:, None, None, None, :]
    cache_score = (
        jnp.einsum("rtkgd,rlkd->rkgtl", query, cache_keys, preferred_element_type=jnp.float32)
        * scale
    )
    fresh_score = (
        jnp.einsum("rtkgd,fkd->rkgtf", query, fresh_keys, preferred_element_type=jnp.float32)
        * scale
    )
    cache_score = jnp.where(live_mask, cache_score, NEG)
    fresh_score = jnp.where(taken_mask, fresh_score, NEG)
    top = jnp.maximum(jnp.max(cache_score, axis=-1), jnp.max(fresh_score, axis=-1))
    cache_weight = jnp.where(live_mask, jnp.exp(cache_score - top[..., None]), 0.0)
    fresh_weight = jnp.where(taken_mask, jnp.exp(fresh_score - top[..., None]), 0.0)
    total = jnp.sum(cache_weight, axis=-1) + jnp.sum(fresh_weight, axis=-1)
    summed = jnp.einsum(
        "rkgtl,rlkd->rkgtd",
        cache_weight.astype(jnp.bfloat16),
        cache_vals,
        preferred_element_type=jnp.float32,
    )
    summed = summed + jnp.einsum(
        "rkgtf,fkd->rkgtd",
        fresh_weight.astype(jnp.bfloat16),
        fresh_vals,
        preferred_element_type=jnp.float32,
    )
    top, total, summed = joined((top, total, summed), "tp", combine)
    drafts = draft_kv[0]
    draft_keys = drafts[..., :head_cols].reshape(rows_here, DRAFT, KVH, HD)
    draft_vals = drafts[..., head_cols:].reshape(rows_here, DRAFT, KVH, HD)
    causal = (jnp.arange(DRAFT)[:, None] >= jnp.arange(DRAFT)[None, :])[None, None, None]
    draft_score = (
        jnp.einsum("rtkgd,rukd->rkgtu", query, draft_keys, preferred_element_type=jnp.float32)
        * scale
    )
    draft_score = jnp.where(causal, draft_score, NEG)
    newtop = jnp.maximum(top, jnp.max(draft_score, axis=-1))
    factor = jnp.exp(top - newtop)
    draft_weight = jnp.where(causal, jnp.exp(draft_score - newtop[..., None]), 0.0)
    total = total * factor + jnp.sum(draft_weight, axis=-1)
    summed = summed * factor[..., None] + jnp.einsum(
        "rkgtu,rukd->rkgtd",
        draft_weight.astype(jnp.bfloat16),
        draft_vals,
        preferred_element_type=jnp.float32,
    )
    output = summed / total[..., None]
    output = output.transpose(0, 3, 1, 2, 4).reshape(rows_here, DRAFT, QH * HD).astype(jnp.bfloat16)
    return output[None]


def solution(mesh):
    placed = (
        P("role", "grp", None, "tp"),
        P("tp", None),
        P("role", "grp", "tp", None),
        P("role", "grp"),
        P("role", "grp", None),
        P("role", "grp"),
        P("role", "grp", None, None),
        P("role", "grp", None, None),
    )
    return jax.shard_map(
        shards, mesh=mesh, in_specs=placed, out_specs=P("role", "grp", None, None), check_vma=False
    )
```

profile of v0, /device:TPU:1, one launch (start us, length us, event | category | flops | bytes accessed | tf_op | source)
XLA Modules:
  0.0 281.3 jit_solution(15156590023573540150)
XLA Ops:
  6.5 1.6 copy-done
  8.1 5.5 %convolution_convert_fusion = bf16[1024,2048]{1,0:T(8,128)(2,1)} fusion(bf16[512,2048]{1,0:T(8,128)(2,1)S(1)} %copy-done, bf16[1,1,1024,512]{3,2,1,0:T(8,128)(2,1)} %param.10), kind=kOutput, calls=%fused_computation.13 | convolution fusion | flops 2149580800 | bytes 7340032 | tf_op jit(solution)/shard_map/dot_general | solution.py:49
  13.7 6.4 %copy.120 = bf16[1024,2048]{0,1:T(8,128)(2,1)} copy(bf16[1024,2048]{1,0:T(8,128)(2,1)} %convolution_convert_fusion) | data formatting | bytes 8388608
  20.8 2.4 fusion.43
  23.2 1.1 copy.126
  24.2 1.3 copy.128
  25.8 2.1 bitcast_bitcast_fusion.1
  27.8 100.0 %reduce-scatter.4.cloned.1.call-done = bf16[128,1024]{1,0:T(8,128)(2,1)} async-done(((bf16[2048,1024]{1,0:T(8,128)(2,1)}), bf16[128,1024]{1,0:T(8,128)(2,1)}) %reduce-scatter.4.cloned.1.call-update) | async-done | bytes 262160
  127.8 1.8 copy.121
  129.6 6.0 %all-to-all-start = ((bf16[16,64,128]{2,1,0:T(8,128)(2,1)}), bf16[16,64,128]{2,1,0:T(8,128)(2,1)S(1)}, u32[]{:S(2)}, u32[]{:S(2)}) async-start(bf16[16,64,128]{2,1,0:T(8,128)(2,1)} %bitcast.10), calls=%async_computation | async-start | bytes 524288 | tf_op jit(solution)/shard_map/all_to_all | solution.py:53
  136.6 7.7 %all-to-all-done = bf16[16,64,128]{2,1,0:T(8,128)(2,1)S(1)} async-done(((bf16[16,64,128]{2,1,0:T(8,128)(2,1)}), bf16[16,64,128]{2,1,0:T(8,128)(2,1)S(1)}, u32[]{:S(2)}, u32[]{:S(2)}) %all-to-all-start) | async-done | bytes 262176 | tf_op jit(solution)/shard_map/all_to_all | solution.py:53
  145.1 2.8 %collective-permute-start = (bf16[64,2048]{1,0:T(8,128)(2,1)}, bf16[64,2048]{1,0:T(8,128)(2,1)S(1)}, u32[]{:S(2)}, u32[]{:S(2)}) collective-permute-start(bf16[64,2048]{1,0:T(8,128)(2,1)} %copy_bitcast_fusion.3), channel_id=1, source_target_pairs={{0,256},{256,0},{1,257},{257,1},{2,258},{258,2},{3,259},{259,3},{4... | collective-permute-start | bytes 786440 | tf_op jit(solution)/shard_map/ppermute | solution.py:18
  148.1 1.8 fusion.45
  149.9 4.1 %collective-permute-done = bf16[64,2048]{1,0:T(8,128)(2,1)S(1)} collective-permute-done((bf16[64,2048]{1,0:T(8,128)(2,1)}, bf16[64,2048]{1,0:T(8,128)(2,1)S(1)}, u32[]{:S(2)}, u32[]{:S(2)}) %collective-permute-start) | collective-permute-done | bytes 262176 | tf_op jit(solution)/shard_map/ppermute | solution.py:18
  156.1 2.7 fusion.46
  158.7 25.0 %all-gather = f32[32,8,8,4]{2,1,3,0:T(8,128)S(1)} all-gather(f32[2,8,8,4]{2,1,3,0:T(8,128)S(1)} %copy_maximum_fusion), channel_id=2, replica_groups=mesh['role'=2,'grp'=16,'tp'=16] {'tp'}, dimensions={0}, use_global_device_ids=true | all-gather | bytes 34816 | tf_op jit(solution)/shard_map/all_gather | solution.py:22
  183.8 1.3 fusion.20
  185.1 22.8 %all-gather.1 = f32[32,8,8,4]{2,1,3,0:T(8,128)S(1)} all-gather(f32[2,8,8,4]{2,1,3,0:T(8,128)S(1)} %copy_add_fusion), channel_id=3, replica_groups=mesh['role'=2,'grp'=16,'tp'=16] {'tp'}, dimensions={0}, use_global_device_ids=true | all-gather | bytes 34816 | tf_op jit(solution)/shard_map/all_gather | solution.py:22
  208.8 17.5 %all-gather.5.cloned.1.call-done = f32[32,8,8,4,128]{4,2,3,1,0:T(8,128)} async-done(((f32[2,8,8,4,128]{4,2,3,1,0:T(8,128)}), f32[32,8,8,4,128]{4,2,3,1,0:T(8,128)}) %all-gather.5.cloned.1.call-update) | async-done | bytes 4194320 | tf_op jit(solution)/shard_map/all_gather | solution.py:22
  227.4 44.3 %while.19 = (s32[]{:T(128)}, f32[2,8,8,4]{2,3,1,0:T(4,128)S(1)}, f32[2,8,8,4]{2,3,1,0:T(4,128)S(1)}, f32[2,8,8,4,128]{4,3,2,1,0:T(4,128)S(1)}, f32[16,2,8,8,4]{3...) while((s32[]{:T(128)}, f32[2,8,8,4]{2,3,1,0:T(4,128)S(1)}, ...), condition=%wide.region_7.8_spmd, body=%wide.region_6.7_spmd.sunk | while | flops 199685 | bytes 1347735 | solution.py:28
  228.3 1.0 constant_dynamic-slice_fusion.6
  231.2 1.0 constant_dynamic-slice_fusion.6
  234.2 1.0 constant_dynamic-slice_fusion.6
  272.6 1.1 fusion.12
  (136 shorter events, 48.7 us)
Async XLA Ops:
  6.5 1.6 copy-start
  6.5 121.3 %reduce-scatter.4.cloned.1.call-start = ((), (), s32[]{:S(2)}) async-start(), calls=%async_computation.3 | async-start | bytes 4456448
  20.1 5.5 %copy-start.6 = (s32[1,2,16]{2,1,0:T(2,128)S(1)}, s32[1,2,16]{2,1,0:T(2,128)}, u32[]{:S(2)}) copy-start(s32[1,2,16]{2,1,0:T(2,128)} %param.14) | copy-start | bytes 388
  20.1 5.6 %copy-start.7 = (s32[1,2]{1,0:T(1,128)S(1)}, s32[1,2]{1,0:T(1,128)}, u32[]{:S(2)}) copy-start(s32[1,2]{1,0:T(1,128)} %param.13) | copy-start | bytes 28
  23.2 124.7 %copy-start.5 = (bf16[1,2,4,8192]{3,2,1,0:T(4,128)(2,1)S(1)}, bf16[1,2,4,8192]{3,2,1,0:T(4,128)(2,1)}, u32[]{:S(2)}) copy-start(bf16[1,2,4,8192]{3,2,1,0:T(4,128)(2,1)} %param.16) | copy-start | bytes 393220
  129.6 14.7 %all-to-all-start = ((bf16[16,64,128]{2,1,0:T(8,128)(2,1)}), bf16[16,64,128]{2,1,0:T(8,128)(2,1)S(1)}, u32[]{:S(2)}, u32[]{:S(2)}) async-start(bf16[16,64,128]{2,1,0:T(8,128)(2,1)} %bitcast.10), calls=%async_computation | async-start | bytes 524288 | tf_op jit(solution)/shard_map/all_to_all | solution.py:53
  135.7 90.7 %all-gather.5.cloned.1.call-start = ((), (), s32[]{:S(2)}) async-start(), calls=%async_computation.2 | async-start | bytes 4456448 | tf_op jit(solution)/shard_map/all_gather | solution.py:22
  136.6 18.1 %copy-start.2 = (bf16[2,192,8,128,1]{3,2,1,0,4:T(8,128)(2,1)S(1)}, bf16[2,192,8,128,1]{3,2,1,0,4:T(8,128)(2,1)}, u32[]{:S(2)}) copy-start(bf16[2,192,8,128,1]{3,2,1,0,4:T(8,128)(2,1)} %bitcast_bitcast_fusion) | copy-start | bytes 2359300
  145.1 8.9 %collective-permute-start = (bf16[64,2048]{1,0:T(8,128)(2,1)}, bf16[64,2048]{1,0:T(8,128)(2,1)S(1)}, u32[]{:S(2)}, u32[]{:S(2)}) collective-permute-start(bf16[64,2048]{1,0:T(8,128)(2,1)} %copy_bitcast_fusion.3), channel_id=1, source_target_pairs={{0,256},{256,0},{1,257},{257,1},{2,258},{258,2},{3,259},{259,3},{4... | collective-permute-start | bytes 786440 | tf_op jit(solution)/shard_map/ppermute | solution.py:18
  149.9 5.2 %copy-start.3 = (f32[2,8,8,4,192]{4,2,3,1,0:T(8,128)}, f32[2,8,8,4,192]{4,2,3,1,0:T(8,128)S(1)}, u32[]{:S(2)}) copy-start(f32[2,8,8,4,192]{4,2,3,1,0:T(8,128)S(1)} %get-tuple-element.252) | copy-start | bytes 1179652
  208.0 0.8 copy-start.1
  227.4 45.1 %copy-start.4 = (f32[2,8,8,4,4]{2,4,3,1,0:T(4,128)S(1)}, f32[2,8,8,4,4]{2,4,3,1,0:T(4,128)}, u32[]{:S(2)}) copy-start(f32[2,8,8,4,4]{2,4,3,1,0:T(4,128)} %get-tuple-element.254) | copy-start | bytes 24580
Sparse Core Ops, SparseCore 0:
  20.2 107.5 reduce-scatter.3
  156.2 70.0 all-gather.4
where the time goes:
time: 284 us; the launch traced here: 281 us
  waiting for transfers between devices  129 us (45%)
  local copies, waits for them, and re-layouts  52.3 us (18%)
  blocking collectives  47.8 us (17%)
  other arithmetic  15.5 us (5%)
  between operations  14.3 us (5%)
  matrix products  12.7 us (4%)
  starting transfers between devices  8.89 us (3%)
    unnamed x3, waiting for transfers between devices  100 us
    all_gather x2, blocking collectives, joined(): everything = jax.tree.map(lambda part: lax.all_gather(part, axis), x)  47.8 us
    dynamic_slice x30, local copies, waits for them, and re-layouts, lap(): return combine(so_far, jax.tree.map(lambda part: part[k], everything))  26.2 us
    all_gather x1, waiting for transfers between devices, joined(): everything = jax.tree.map(lambda part: lax.all_gather(part, axis), x)  17.5 us
    unnamed x23, local copies, waits for them, and re-layouts  13.1 us
    add x15, other arithmetic, combine(): first[2] * scale_a[..., None] + second[2] * scale_b[..., None]  11.9 us
    all_to_all x1, waiting for transfers between devices, shards(): lax.all_to_all(columns, 'tp', split_axis=0, concat_axis=1, tiled=True)  7.69 us
    all_to_all x1, starting transfers between devices, shards(): lax.all_to_all(columns, 'tp', split_axis=0, concat_axis=1, tiled=True)  6.04 us
  transfers between devices with their start and end apart: 4, of which 4 were waited for; matrix products, arithmetic and copies ran while one was open for 5% of the time, Pallas kernels for 0%

commit v1 on v0

v1 whole, which is shorter than its diff:
```python
import functools
import math

import jax
import jax.numpy as jnp
from jax import lax
from jax.experimental import pallas as pl
from jax.experimental.pallas import tpu as pltpu
from jax.sharding import Mesh
from jax.sharding import PartitionSpec as P

QH = 64
KVH = 8
HD = 128
DRAFT = 4
GROUP = QH // KVH
QROWS = GROUP * DRAFT
COLS = KVH * HD
NEG = -1e30
SCALE = 1.0 / math.sqrt(HD)

f32 = jnp.float32
bf16 = jnp.bfloat16


def dot_nt(a, b):
    return lax.dot_general(a, b, (((1,), (1,)), ((), ())), preferred_element_type=f32)


def dot_nn(a, b):
    return jnp.dot(a, b, preferred_element_type=f32)


def packed_stat(lse):
    hi = lse.astype(bf16).astype(f32)
    mid = (lse - hi).astype(bf16).astype(f32)
    lo = lse - hi - mid
    lane = lax.broadcasted_iota(jnp.int32, (lse.shape[0], HD), 1)
    return jnp.where(
        lane == 0, hi, jnp.where(lane == 1, mid, jnp.where(lane == 2, lo, 0.0))
    ).astype(bf16)


def stat(tile):
    return jnp.sum(tile.astype(f32), axis=-1, keepdims=True)


def attend(score, value):
    top = jnp.max(score, axis=-1, keepdims=True)
    weight = jnp.where(score > 0.5 * NEG, jnp.exp(score - top), 0.0)
    total = jnp.sum(weight, axis=-1, keepdims=True)
    any_key = total > 0.0
    safe = jnp.where(any_key, total, 1.0)
    out = dot_nn(weight.astype(bf16), value) / safe
    return out, jnp.where(any_key, top + jnp.log(safe), NEG)


def merge(parts):
    top = functools.reduce(jnp.maximum, [lse for _, lse in parts])
    weights = [jnp.where(lse > 0.5 * NEG, jnp.exp(lse - top), 0.0) for _, lse in parts]
    total = functools.reduce(jnp.add, weights)
    safe = jnp.where(total > 0.0, total, 1.0)
    out = functools.reduce(jnp.add, [w * o for w, (o, _) in zip(weights, parts)])
    return out / safe, jnp.where(total > 0.0, top + jnp.log(safe), NEG)


def cache_kernel(owner_ref, len_ref, q_ref, cache_ref, mine_ref, other_ref):
    core = lax.axis_index("core")
    me = lax.axis_index("yx") * 2 + core
    slab = cache_ref.shape[1]
    for which, out_ref in ((0, other_ref), (1, mine_ref)):
        row = core if which == 1 else 1 - core
        first = jnp.int32(0)
        for block in range(owner_ref.shape[1]):
            first = first + jnp.where(owner_ref[row, block] == me, block, 0)
        room = len_ref[0, row] - first * slab
        live = lax.broadcasted_iota(jnp.int32, (QROWS, slab), 1) < room
        for head in range(KVH):
            keys = cache_ref[row, :, head * HD : (head + 1) * HD]
            values = cache_ref[row, :, COLS + head * HD : COLS + (head + 1) * HD]
            score = dot_nt(q_ref[row, head], keys) * SCALE
            out, lse = attend(jnp.where(live, score, NEG), values)
            out_ref[head, :QROWS] = out.astype(bf16)
            out_ref[head, QROWS:] = packed_stat(lse)


def project_kernel(
    acts_ref, acts2_ref, w_ref, w2_ref, q_ref, mine_ref, theirs_ref, out_ref, qw_ref
):
    core = lax.axis_index("core")
    half = acts2_ref.shape[0]
    acts = acts_ref[pl.ds(pl.multiple_of(core * half, half), half), :]
    acts2 = acts2_ref[...]
    for head in range(KVH):
        cols = slice(head * HD, (head + 1) * HD)
        rows = slice(head * QROWS, (head + 1) * QROWS)
        qw_ref[0, rows] = dot_nt(q_ref[head], w_ref[:, cols]).astype(bf16)
        qw_ref[1, rows] = dot_nt(q_ref[head], w2_ref[:, cols]).astype(bf16)
    score = (dot_nt(qw_ref[0], acts) + dot_nt(qw_ref[1], acts2)) * SCALE
    high = score.astype(bf16)
    low = (score - high.astype(f32)).astype(bf16)
    tiles = half // HD
    for head in range(KVH):
        rows = slice(head * QROWS, (head + 1) * QROWS)
        for tile in range(tiles):
            cols = slice(tile * HD, (tile + 1) * HD)
            at = half + tile * QROWS
            out_ref[head, at : at + QROWS] = high[rows, cols]
            at = half + (tiles + tile) * QROWS
            out_ref[head, at : at + QROWS] = low[rows, cols]
        cols = slice(COLS + head * HD, COLS + (head + 1) * HD)
        value = dot_nn(acts, w_ref[:, cols]) + dot_nn(acts2, w2_ref[:, cols])
        out_ref[head, :half] = value.astype(bf16)
        out, lse = merge(
            [
                (ref[head, :QROWS].astype(f32), stat(ref[head, QROWS:]))
                for ref in (mine_ref, theirs_ref)
            ]
        )
        at = half + 2 * tiles * QROWS
        out_ref[head, at : at + QROWS] = out.astype(bf16)
        out_ref[head, at + QROWS : at + 2 * QROWS] = packed_stat(lse)


def span_kernel(got_ref, q_ref, draft_ref, out_ref):
    parts, length, _ = got_ref.shape
    half = (length - 2 * QROWS) * HD // (HD + 2 * QROWS)
    tiles = half // HD
    role = lax.axis_index("role")
    core = lax.axis_index("core")
    head = lax.axis_index("yx")

    def total(start, size):
        acc = got_ref[0, start : start + size].astype(f32)
        for part in range(1, parts):
            acc = acc + got_ref[part, start : start + size].astype(f32)
        return acc

    value = total(0, half).astype(bf16)
    score = jnp.concatenate(
        [
            total(half + tile * QROWS, QROWS) + total(half + (tiles + tile) * QROWS, QROWS)
            for tile in range(tiles)
        ],
        axis=1,
    )
    out, lse = attend(score, value)
    fresh = jnp.concatenate([out.astype(bf16), packed_stat(lse)], axis=0)

    at = half + 2 * tiles * QROWS
    cached = [
        (
            got_ref[part, at : at + QROWS].astype(f32),
            stat(got_ref[part, at + QROWS : at + 2 * QROWS]),
        )
        for part in range(parts)
    ]
    query = q_ref[core, head]
    start = pl.multiple_of(head * HD, HD)
    draft_keys = draft_ref[core, :, pl.ds(start, HD)].astype(f32)
    draft_vals = draft_ref[core, :, pl.ds(start + COLS, HD)].astype(f32)
    token = lax.broadcasted_iota(jnp.int32, (QROWS, 1), 0) % DRAFT
    scores = []
    for u in range(DRAFT):
        one = jnp.sum(query.astype(f32) * draft_keys[u : u + 1], axis=-1, keepdims=True) * SCALE
        scores.append(jnp.where(token >= u, one, NEG))
    top = functools.reduce(jnp.maximum, scores)
    weights = [jnp.where(one > 0.5 * NEG, jnp.exp(one - top), 0.0) for one in scores]
    sums = functools.reduce(jnp.add, weights)
    drafted = functools.reduce(
        jnp.add,
        [w.astype(bf16).astype(f32) * draft_vals[u : u + 1] for u, w in enumerate(weights)],
    )
    out, lse = merge([*cached, (drafted / sums, top + jnp.log(sums))])
    kept = jnp.concatenate([out.astype(bf16), packed_stat(lse)], axis=0)

    chunks = out_ref.shape[1]
    for chunk in range(chunks):
        out_ref[role, chunk] = kept
        out_ref[1 - role, chunk] = fresh


def join_kernel(span_ref, got_ref, out_ref):
    role = lax.axis_index("role")
    for row in range(out_ref.shape[0]):
        taken = span_ref[0, 0] == row
        for head in range(KVH):

            def pair(pool, core):
                tile = got_ref.at[pool, head * 2 + core]
                return tile[:QROWS].astype(f32), stat(tile[QROWS:])

            parts = [pair(role, row)]
            for core in range(2):
                out, lse = pair(1 - role, core)
                parts.append((out, jnp.where(taken, lse, NEG)))
            out_ref[row, head] = merge(parts)[0].astype(bf16)


def call(kernel, out_shapes, spaces, scratch=(), flops=0, moved=0):
    return pl.pallas_call(
        kernel,
        out_shape=out_shapes,
        in_specs=[pl.BlockSpec(memory_space=space) for space in spaces],
        out_specs=jax.tree.map(lambda _: pl.BlockSpec(memory_space=pltpu.VMEM), out_shapes),
        scratch_shapes=list(scratch),
        compiler_params=pltpu.CompilerParams(vmem_limit_bytes=24 << 20),
        cost_estimate=pl.CostEstimate(flops=flops, bytes_accessed=moved, transcendentals=0),
    )


V = pltpu.VMEM
S = pltpu.SMEM


def shards(
    prompt_acts, kv_weight, cache_kv, cache_len, block_owner, span_row, draft_query, draft_kv
):
    swap = [(0, 1), (1, 0)]
    core = lax.axis_index("core")
    acts = prompt_acts[0, 0]
    span, width = acts.shape
    half = span // 2
    rows = cache_kv.shape[1]
    n_yx = lax.axis_size("yx")
    struct = jax.ShapeDtypeStruct

    weight2 = lax.ppermute(kv_weight, "core", swap)
    query = draft_query[0].reshape(rows, DRAFT, KVH, GROUP, HD).transpose(0, 2, 3, 1, 4)
    query = query.reshape(rows, KVH, QROWS, HD)
    chosen = lax.dynamic_index_in_dim(query, span_row[0, 0], 0, keepdims=False)
    asked = lax.ppermute(chosen, "role", swap)
    acts2 = lax.ppermute(
        lax.dynamic_slice_in_dim(acts, (1 - core) * half, half, 0), "core", swap
    )

    block = struct((KVH, 2 * QROWS, HD), bf16)
    mine, other = call(
        cache_kernel, [block, block], [S, S, V, V], flops=400_000_000, moved=2_000_000
    )(block_owner[0], cache_len, query, cache_kv[0])
    theirs = lax.ppermute(other, "core", swap)

    length = half + 2 * (half // HD) * QROWS + 2 * QROWS
    sent = call(
        project_kernel,
        struct((KVH, length, HD), bf16),
        [V] * 7,
        [V((2, KVH * QROWS, width), bf16)],
        flops=1_700_000_000,
        moved=8_000_000,
    )(acts, acts2, kv_weight, weight2, asked, mine, theirs)
    got = lax.all_to_all(sent, "yx", 0, 0, tiled=True)

    parts = call(
        span_kernel,
        struct((2, 2 * n_yx, 2 * QROWS, HD), bf16),
        [V, V, V],
        flops=20_000_000,
        moved=3_000_000,
    )(got, query, draft_kv[0])
    parts = lax.all_to_all(
        parts.reshape(4 * n_yx, 2 * QROWS, HD), ("role", "yx", "core"), 0, 0, tiled=True
    )
    joined = call(
        join_kernel, struct((rows, KVH, QROWS, HD), bf16), [S, V], flops=10_000_000, moved=700_000
    )(span_row, parts.reshape(2, 2 * n_yx, 2 * QROWS, HD))
    output = joined.reshape(rows, KVH, GROUP, DRAFT, HD).transpose(0, 3, 1, 2, 4)
    return output.reshape(1, rows, DRAFT, QH * HD)


def solution(mesh):
    roles, groups, tps = mesh.devices.shape
    fine = Mesh(mesh.devices.reshape(roles, groups, tps // 2, 2), ("role", "grp", "yx", "core"))
    tp = ("yx", "core")
    placed = (
        P("role", "grp", None, tp),
        P(tp, None),
        P("role", "grp", tp, None),
        P("role", "grp"),
        P("role", "grp", None),
        P("role", "grp"),
        P("role", "grp", None, None),
        P("role", "grp", None, None),
    )
    return jax.shard_map(
        shards, mesh=fine, in_specs=placed, out_specs=P("role", "grp", None, None), check_vma=False
    )
```

time: 284 us -> 80.4 us (0.28)
  waiting for transfers between devices: 129 us -> 3.69 us
  local copies, waits for them, and re-layouts: 52.3 us -> 7.14 us
  other arithmetic: 15.5 us -> 0 us
  between operations: 14.3 us -> 0.76 us
  matrix products: 12.7 us -> 0 us
  Pallas kernels: 0 us -> 11.2 us
  starting transfers between devices: 8.89 us -> 15.1 us
  blocking collectives: 47.8 us -> 41.9 us
    unnamed x3 -> x0, waiting for transfers between devices: 100 us -> none
    all_gather x2 -> x0, blocking collectives: 47.8 us -> none  [joined(): everything = jax.tree.map(lambda part: lax.all_gather(part, axis), x)]
    all_to_all x0 -> x2, blocking collectives: none -> 41.9 us  [the longest x1 25.9 us: shards(): got = lax.all_to_all(sent, 'yx', 0, 0, tiled=True)]
    dynamic_slice x30 -> x1, local copies, waits for them, and re-layouts: 26.2 us -> 1.88 us  [shards(): lax.dynamic_slice_in_dim(acts, (1 - core) * half, half, 0)]
    all_gather x1 -> x0, waiting for transfers between devices: 17.5 us -> none  [joined(): everything = jax.tree.map(lambda part: lax.all_gather(part, axis), x)]
    add x32 -> x0, other arithmetic: 12.8 us -> none  [the longest x15 11.9 us: combine(): first[2] * scale_a[..., None] + second[2] * scale_b[..., None]]
    dot_general x7 -> x0, matrix products: 12.7 us -> none  [the longest x1 5.53 us: shards(): partial_value = jnp.dot(acts, kv_weight, preferred_element_type=jnp.float32)]
    ppermute x1 -> x4, starting transfers between devices: 2.81 us -> 15.1 us  [the longest x1 8.91 us: shards(): weight2 = lax.ppermute(kv_weight, 'core', swap)]
  transfers between devices with their start and end apart: 4 -> 4, of which waited for: 4 -> 1; matrix products, arithmetic and copies ran while one was open for 5% -> 2% of each run, Pallas kernels for 0% -> 7%
where the time goes in v1:
time: 80.4 us; the launch traced here: 79.8 us
  blocking collectives  41.9 us (52%)
  starting transfers between devices  15.1 us (19%)
  Pallas kernels  11.2 us (14%)
  local copies, waits for them, and re-layouts  7.14 us (9%)
  waiting for transfers between devices  3.69 us (5%)
    all_to_all x1, blocking collectives, shards(): got = lax.all_to_all(sent, 'yx', 0, 0, tiled=True)  25.9 us
    all_to_all x1, blocking collectives, shards(): lax.all_to_all(parts.reshape(4 * n_yx, 2 * QROWS, HD), ('role', 'yx', 'co...  16 us
    ppermute x1, starting transfers between devices, shards(): weight2 = lax.ppermute(kv_weight, 'core', swap)  8.91 us
    pallas_call x1, Pallas kernels, shards(): call(cache_kernel, [block, block], [S, S, V, V], flops=400000000, moved=2...  5.36 us
    unnamed x16, local copies, waits for them, and re-layouts  5.24 us
    pallas_call x1, Pallas kernels, shards(): call(project_kernel, struct((KVH, length, HD), bf16), [V] * 7, [V((2, KVH...  4.39 us
    ppermute x1, waiting for transfers between devices, shards(): asked = lax.ppermute(chosen, 'role', swap)  3.68 us
    ppermute x1, starting transfers between devices, shards(): theirs = lax.ppermute(other, 'core', swap)  2.39 us
  transfers between devices with their start and end apart: 4, of which 1 were waited for; matrix products, arithmetic and copies ran while one was open for 2% of the time, Pallas kernels for 7%

profile of v1, /device:TPU:1, one launch (start us, length us, event | category | flops | bytes accessed | tf_op | source)
XLA Modules:
  0.0 79.8 jit_solution(11963967563598025945)
XLA Ops:
  0.0 8.9 %collective-permute-start.1 = (bf16[512,2048]{1,0:T(8,128)(2,1)}, bf16[512,2048]{1,0:T(8,128)(2,1)S(1)}, u32[]{:S(2)}, u32[]{:S(2)}) collective-permute-start(bf16[512,2048]{1,0:T(8,128)(2,1)} %w_ref.1), channel_id=1, source_target_pairs={{0,1},{1,0},{2,3},{3,2},{4,5},{5,4},{6,7},{7,6},{8,9},{9,8},{10,11... | collective-permute-start | bytes 6291464 | tf_op jit(solution)/shard_map/ppermute | solution.py:228
  8.9 1.9 %dynamic-slice_bitcast_fusion = bf16[512,512]{1,0:T(8,128)(2,1)} fusion(bf16[1,1,1024,512]{3,2,1,0:T(8,128)(2,1)} %param.8, s32[]{:T(128)S(6)} %select_n.7), kind=kLoop, calls=%fused_computation | loop fusion | bytes 1048580 | tf_op jit(solution)/shard_map/dynamic_slice | solution.py:234
  10.8 1.9 %collective-permute-start = (bf16[512,512]{1,0:T(8,128)(2,1)}, bf16[512,512]{1,0:T(8,128)(2,1)}, u32[]{:S(2)}, u32[]{:S(2)}) collective-permute-start(bf16[512,512]{1,0:T(8,128)(2,1)} %dynamic-slice_bitcast_fusion), channel_id=1, source_target_pairs={{0,1},{1,0},{2,3},{3,2},{4,5},{5,4},{6,7},{7,6},{8,9},{9,8},{10,11... | collective-permute-start | bytes 1572872 | tf_op jit(solution)/shard_map/ppermute | solution.py:233
  12.7 0.0 copy-start.2
  12.7 1.4 %copy-done.2 = bf16[1,2,192,2048]{3,2,1,0:T(8,128)(2,1)S(1)} copy-done((bf16[1,2,192,2048]{3,2,1,0:T(8,128)(2,1)S(1)}, bf16[1,2,192,2048]{3,2,1,0:T(8,128)(2,1)}, u32[]{:S(2)}) %copy-start.2) | copy-done | bytes 1572888
  14.1 0.9 %copy-done.3 = bf16[1,2,4,8192]{3,2,1,0:T(4,128)(2,1)S(1)} copy-done((bf16[1,2,4,8192]{3,2,1,0:T(4,128)(2,1)S(1)}, bf16[1,2,4,8192]{3,2,1,0:T(4,128)(2,1)}, u32[]{:S(2)}) %copy-start.3) | copy-done | bytes 131096
  15.0 0.7 copy-done.6
  15.7 0.7 copy-done.7
  16.4 5.4 %shard_map.82 = (bf16[8,64,128]{2,1,0:T(8,128)(2,1)S(1)}, bf16[8,64,128]{2,1,0:T(8,128)(2,1)}) custom-call(s32[2,16]{1,0:T(2,128)S(1)} %bitcast.32, s32[1,2]{1,0:T(1,128)S(1)} %copy-done.7, bf16[2,8,32,128]{3,2,1,0:T(8,128)(2,1)S(1)} %bitcast.28, bf16[2,192,2048]{2,1,0:T(8,128)(2,1)S(1)} %bitcast.27), custom_call_target="tpu_custom_call" | custom-call | flops 400000000 | bytes 2000000 | tf_op jit(solution)/shard_map/pallas_call | solution.py:238
  21.7 2.4 %collective-permute-start.3 = (bf16[8,64,128]{2,1,0:T(8,128)(2,1)}, bf16[8,64,128]{2,1,0:T(8,128)(2,1)S(1)}, u32[]{:S(2)}, u32[]{:S(2)}) collective-permute-start(bf16[8,64,128]{2,1,0:T(8,128)(2,1)} %get-tuple-element.8), channel_id=1, source_target_pairs={{0,1},{1,0},{2,3},{3,2},{4,5},{5,4},{6,7},{7,6},{8,9},{9,8},{10,11... | collective-permute-start | bytes 393224 | tf_op jit(solution)/shard_map/ppermute | solution.py:241
  24.8 0.0 copy-done.4
  24.8 1.9 %collective-permute-start.2 = (bf16[8,32,128]{2,1,0:T(8,128)(2,1)S(1)}, bf16[8,32,128]{2,1,0:T(8,128)(2,1)S(1)}, u32[]{:S(2)}, u32[]{:S(2)}) collective-permute-start(bf16[8,32,128]{2,1,0:T(8,128)(2,1)S(1)} %dynamic-slice_bitcast_fusion.1), channel_id=1, source_target_pairs={{0,256},{256,0},{1,257},{257,1},{2,258},{258,2},{3,259},{259,3},{4... | collective-permute-start | bytes 196616 | tf_op jit(solution)/shard_map/ppermute | solution.py:232
  26.8 3.7 %collective-permute-done.2.q_ref = bf16[8,32,128]{2,1,0:T(8,128)(2,1)S(1)} collective-permute-done((bf16[8,32,128]{2,1,0:T(8,128)(2,1)S(1)}, bf16[8,32,128]{2,1,0:T(8,128)(2,1)S(1)}, u32[]{:S(2)}, u32[]{:S(2)}) %collective-permute-start.2) | collective-permute-done | bytes 65568 | tf_op jit(solution)/shard_map/ppermute | solution.py:232
  30.4 0.0 collective-permute-done.3.theirs_ref
  30.4 0.0 collective-permute-done.acts2_ref
  30.4 0.0 collective-permute-done.1.w2_ref
  30.5 0.0 copy-start.1
  30.5 1.6 %copy-done.1 = bf16[512,2048]{1,0:T(8,128)(2,1)S(1)} copy-done((bf16[512,2048]{1,0:T(8,128)(2,1)S(1)}, bf16[512,2048]{1,0:T(8,128)(2,1)}, u32[]{:S(2)}) %copy-start.1) | copy-done | bytes 2097176
  32.0 4.4 %shard_map.83 = bf16[8,832,128]{2,1,0:T(8,128)(2,1)S(1)} custom-call(bf16[1024,512]{1,0:T(8,128)(2,1)S(1)} %bitcast.24, bf16[512,512]{1,0:T(8,128)(2,1)} %collective-permute-done.acts2_ref, bf16[512,2048]{1,0:T(8,128)(2,1)S(1)} %copy-done.1, bf16[512,2048]{1,0:T(8,128)(2,1)S(1)} %collective-permute-done.1.w2_ref, ...), custom_call_target="tpu_custom_call" | custom-call | flops 1700000000 | bytes 8000000 | tf_op jit(solution)/shard_map/pallas_call | solution.py:244
  36.4 0.0 copy-start.5
  36.5 25.9 %all_to_all.10.got_ref = bf16[8,832,128]{2,1,0:T(8,128)(2,1)S(1)} all-to-all(bf16[8,832,128]{2,1,0:T(8,128)(2,1)S(1)} %shard_map.83), channel_id=1, replica_groups=mesh['role'=2,'grp'=16,'yx'=8,'core'=2] {'yx'}, dimensions={0} | all-to-all | bytes 3407872 | tf_op jit(solution)/shard_map/all_to_all | solution.py:252
  62.4 0.4 shard_map.84
  62.8 16.0 %all_to_all.11 = bf16[32,64,128]{2,1,0:T(8,128)(2,1)S(1)} all-to-all(bf16[32,64,128]{2,1,0:T(8,128)(2,1)S(1)} %bitcast.26), channel_id=1, replica_groups=mesh['role'=2,'grp'=16,'yx'=8,'core'=2] {'role','yx','core'}, dimensions={0} | all-to-all | bytes 1048576 | tf_op jit(solution)/shard_map/all_to_all | solution.py:261
  78.8 1.1 %shard_map.85 = bf16[2,8,32,128]{3,2,1,0:T(8,128)(2,1)} custom-call(s32[1,1]{1,0:T(1,128)} %copy.11.span_ref, bf16[2,16,64,128]{3,2,1,0:T(8,128)(2,1)S(1)} %bitcast.25), custom_call_target="tpu_custom_call" | custom-call | flops 10000000 | bytes 700000 | tf_op jit(solution)/shard_map/pallas_call | solution.py:264
  (8 shorter events, 0.0 us)
Async XLA Ops:
  0.0 30.4 %copy-start = (bf16[1,1,1024,512]{3,2,1,0:T(8,128)(2,1)S(1)}, bf16[1,1,1024,512]{3,2,1,0:T(8,128)(2,1)}, u32[]{:S(2)}) copy-start(bf16[1,1,1024,512]{3,2,1,0:T(8,128)(2,1)} %param.8) | copy-start | bytes 3145732
  0.0 30.4 %collective-permute-start.1 = (bf16[512,2048]{1,0:T(8,128)(2,1)}, bf16[512,2048]{1,0:T(8,128)(2,1)S(1)}, u32[]{:S(2)}, u32[]{:S(2)}) collective-permute-start(bf16[512,2048]{1,0:T(8,128)(2,1)} %w_ref.1), channel_id=1, source_target_pairs={{0,1},{1,0},{2,3},{3,2},{4,5},{5,4},{6,7},{7,6},{8,9},{9,8},{10,11... | collective-permute-start | bytes 6291464 | tf_op jit(solution)/shard_map/ppermute | solution.py:228
  10.8 19.6 %collective-permute-start = (bf16[512,512]{1,0:T(8,128)(2,1)}, bf16[512,512]{1,0:T(8,128)(2,1)}, u32[]{:S(2)}, u32[]{:S(2)}) collective-permute-start(bf16[512,512]{1,0:T(8,128)(2,1)} %dynamic-slice_bitcast_fusion), channel_id=1, source_target_pairs={{0,1},{1,0},{2,3},{3,2},{4,5},{5,4},{6,7},{7,6},{8,9},{9,8},{10,11... | collective-permute-start | bytes 1572872 | tf_op jit(solution)/shard_map/ppermute | solution.py:233
  12.7 1.4 %copy-start.2 = (bf16[1,2,192,2048]{3,2,1,0:T(8,128)(2,1)S(1)}, bf16[1,2,192,2048]{3,2,1,0:T(8,128)(2,1)}, u32[]{:S(2)}) copy-start(bf16[1,2,192,2048]{3,2,1,0:T(8,128)(2,1)} %param.10) | copy-start | bytes 4718596
  14.1 0.9 %copy-start.3 = (bf16[1,2,4,8192]{3,2,1,0:T(4,128)(2,1)S(1)}, bf16[1,2,4,8192]{3,2,1,0:T(4,128)(2,1)}, u32[]{:S(2)}) copy-start(bf16[1,2,4,8192]{3,2,1,0:T(4,128)(2,1)} %param.14) | copy-start | bytes 393220
  15.0 0.7 copy-start.6
  15.7 0.7 copy-start.7
  16.4 8.4 %copy-start.4 = (bf16[1,2,4,8192]{3,2,1,0:T(4,128)(2,1)S(1)}, bf16[1,2,4,8192]{3,2,1,0:T(4,128)(2,1)}, u32[]{:S(2)}) copy-start(bf16[1,2,4,8192]{3,2,1,0:T(4,128)(2,1)} %param.14) | copy-start | bytes 393220
  21.7 8.7 %collective-permute-start.3 = (bf16[8,64,128]{2,1,0:T(8,128)(2,1)}, bf16[8,64,128]{2,1,0:T(8,128)(2,1)S(1)}, u32[]{:S(2)}, u32[]{:S(2)}) collective-permute-start(bf16[8,64,128]{2,1,0:T(8,128)(2,1)} %get-tuple-element.8), channel_id=1, source_target_pairs={{0,1},{1,0},{2,3},{3,2},{4,5},{5,4},{6,7},{7,6},{8,9},{9,8},{10,11... | collective-permute-start | bytes 393224 | tf_op jit(solution)/shard_map/ppermute | solution.py:241
  24.8 5.6 %collective-permute-start.2 = (bf16[8,32,128]{2,1,0:T(8,128)(2,1)S(1)}, bf16[8,32,128]{2,1,0:T(8,128)(2,1)S(1)}, u32[]{:S(2)}, u32[]{:S(2)}) collective-permute-start(bf16[8,32,128]{2,1,0:T(8,128)(2,1)S(1)} %dynamic-slice_bitcast_fusion.1), channel_id=1, source_target_pairs={{0,256},{256,0},{1,257},{257,1},{2,258},{258,2},{3,259},{259,3},{4... | collective-permute-start | bytes 196616 | tf_op jit(solution)/shard_map/ppermute | solution.py:232
  30.5 1.6 %copy-start.1 = (bf16[512,2048]{1,0:T(8,128)(2,1)S(1)}, bf16[512,2048]{1,0:T(8,128)(2,1)}, u32[]{:S(2)}) copy-start(bf16[512,2048]{1,0:T(8,128)(2,1)} %w_ref.1) | copy-start | bytes 6291460
  36.4 25.9 %copy-start.5 = (bf16[1,2,4,2048]{3,2,1,0:T(4,128)(2,1)S(1)}, bf16[1,2,4,2048]{3,2,1,0:T(4,128)(2,1)}, u32[]{:S(2)}) copy-start(bf16[1,2,4,2048]{3,2,1,0:T(4,128)(2,1)} %param.15) | copy-start | bytes 98308

commit v2 on v1

--- a/solution.py
+++ b/solution.py
@@ -64,62 +64,132 @@
     return out / safe, jnp.where(total > 0.0, top + jnp.log(safe), NEG)
 
 
-def cache_kernel(owner_ref, len_ref, q_ref, cache_ref, mine_ref, other_ref):
+def stacked(parts):
+    return jnp.concatenate(parts, axis=0)
+
+
+def head_cols(head, start=0):
+    return slice(start + head * HD, start + (head + 1) * HD)
+
+
+def put_pair(out_ref, start, out, lse):
+    shape = (KVH, QROWS, HD)
+    out_ref[:, start : start + QROWS] = out.astype(bf16).reshape(shape)
+    out_ref[:, start + QROWS : start + 2 * QROWS] = packed_stat(lse).reshape(shape)
+
+
+def cache_kernel(
+    owner_hbm, len_hbm, q_ref, cache_hbm, mine_ref, other_ref, owner_ref, len_ref, cache_ref, sems
+):
     core = lax.axis_index("core")
     me = lax.axis_index("yx") * 2 + core
     slab = cache_ref.shape[1]
-    for which, out_ref in ((0, other_ref), (1, mine_ref)):
-        row = core if which == 1 else 1 - core
+    order = (1 - core, core)
+    ints = [
+        pltpu.make_async_copy(owner_hbm, owner_ref, sems.at[0]),
+        pltpu.make_async_copy(len_hbm, len_ref, sems.at[1]),
+    ]
+    loads = [
+        pltpu.make_async_copy(cache_hbm.at[row], cache_ref.at[k], sems.at[2 + k])
+        for k, row in enumerate(order)
+    ]
+    for copy in (*ints, *loads):
+        copy.start()
+    for copy in ints:
+        copy.wait()
+    for k, (row, out_ref) in enumerate(zip(order, (other_ref, mine_ref))):
         first = jnp.int32(0)
         for block in range(owner_ref.shape[1]):
             first = first + jnp.where(owner_ref[row, block] == me, block, 0)
         room = len_ref[0, row] - first * slab
-        live = lax.broadcasted_iota(jnp.int32, (QROWS, slab), 1) < room
-        for head in range(KVH):
-            keys = cache_ref[row, :, head * HD : (head + 1) * HD]
-            values = cache_ref[row, :, COLS + head * HD : COLS + (head + 1) * HD]
-            score = dot_nt(q_ref[row, head], keys) * SCALE
-            out, lse = attend(jnp.where(live, score, NEG), values)
-            out_ref[head, :QROWS] = out.astype(bf16)
-            out_ref[head, QROWS:] = packed_stat(lse)
+        live = lax.broadcasted_iota(jnp.int32, (KVH * QROWS, slab), 1) < room
+        loads[k].wait()
+        score = stacked(
+            [dot_nt(q_ref[row, head], cache_ref[k, :, head_cols(head)]) for head in range(KVH)]
+        )
+        score = jnp.where(live, score * SCALE, NEG)
+        top = jnp.max(score, axis=-1, keepdims=True)
+        weight = jnp.where(live, jnp.exp(score - top), 0.0)
+        total = jnp.sum(weight, axis=-1, keepdims=True)
+        safe = jnp.where(total > 0.0, total, 1.0)
+        weight = weight.astype(bf16)
+        out = stacked(
+            [
+                dot_nn(
+                    weight[head * QROWS : (head + 1) * QROWS],
+                    cache_ref[k, :, head_cols(head, COLS)],
+                )
+                for head in range(KVH)
+            ]
+        )
+        put_pair(out_ref, 0, out / safe, jnp.where(total > 0.0, top + jnp.log(safe), NEG))
 
 
 def project_kernel(
-    acts_ref, acts2_ref, w_ref, w2_ref, q_ref, mine_ref, theirs_ref, out_ref, qw_ref
+    acts_hbm,
+    acts2_hbm,
+    w_hbm,
+    w2_hbm,
+    q_ref,
+    mine_ref,
+    theirs_ref,
+    out_ref,
+    acts_ref,
+    w_ref,
+    qw_ref,
+    sems,
 ):
     core = lax.axis_index("core")
-    half = acts2_ref.shape[0]
-    acts = acts_ref[pl.ds(pl.multiple_of(core * half, half), half), :]
-    acts2 = acts2_ref[...]
-    for head in range(KVH):
-        cols = slice(head * HD, (head + 1) * HD)
-        rows = slice(head * QROWS, (head + 1) * QROWS)
-        qw_ref[0, rows] = dot_nt(q_ref[head], w_ref[:, cols]).astype(bf16)
-        qw_ref[1, rows] = dot_nt(q_ref[head], w2_ref[:, cols]).astype(bf16)
-    score = (dot_nt(qw_ref[0], acts) + dot_nt(qw_ref[1], acts2)) * SCALE
+    half = acts_ref.shape[1]
+    mine = pl.ds(pl.multiple_of(core * half, half), half)
+    keys, values = slice(0, COLS), slice(COLS, 2 * COLS)
+    loads = [
+        pltpu.make_async_copy(source.at[rows, cols], held.at[k, :, cols], sems.at[number])
+        for number, (source, rows, cols, held, k) in enumerate(
+            [
+                (w_hbm, slice(None), keys, w_ref, 0),
+                (w2_hbm, slice(None), keys, w_ref, 1),
+                (acts_hbm, mine, slice(None), acts_ref, 0),
+                (acts2_hbm, mine, slice(None), acts_ref, 1),
+                (w_hbm, slice(None), values, w_ref, 0),
+                (w2_hbm, slice(None), values, w_ref, 1),
+            ]
+        )
+    ]
+    for copy in loads:
+        copy.start()
+    for k in range(2):
+        loads[k].wait()
+        for head in range(KVH):
+            rows = slice(head * QROWS, (head + 1) * QROWS)
+            qw_ref[k, rows] = dot_nt(q_ref[head], w_ref[k, :, head_cols(head)]).astype(bf16)
+    for copy in loads[2:4]:
+        copy.wait()
+    score = (dot_nt(qw_ref[0], acts_ref[0]) + dot_nt(qw_ref[1], acts_ref[1])) * SCALE
     high = score.astype(bf16)
     low = (score - high.astype(f32)).astype(bf16)
     tiles = half // HD
+    for tile in range(tiles):
+        for part, words in enumerate((high, low)):
+            at = half + (part * tiles + tile) * QROWS
+            out_ref[:, at : at + QROWS] = words[:, head_cols(tile)].reshape(KVH, QROWS, HD)
+    for copy in loads[4:]:
+        copy.wait()
+    value = dot_nn(acts_ref[0], w_ref[0, :, values]) + dot_nn(acts_ref[1], w_ref[1, :, values])
+    value = value.astype(bf16)
     for head in range(KVH):
-        rows = slice(head * QROWS, (head + 1) * QROWS)
-        for tile in range(tiles):
-            cols = slice(tile * HD, (tile + 1) * HD)
-            at = half + tile * QROWS
-            out_ref[head, at : at + QROWS] = high[rows, cols]
-            at = half + (tiles + tile) * QROWS
-            out_ref[head, at : at + QROWS] = low[rows, cols]
-        cols = slice(COLS + head * HD, COLS + (head + 1) * HD)
-        value = dot_nn(acts, w_ref[:, cols]) + dot_nn(acts2, w2_ref[:, cols])
-        out_ref[head, :half] = value.astype(bf16)
-        out, lse = merge(
-            [
-                (ref[head, :QROWS].astype(f32), stat(ref[head, QROWS:]))
-                for ref in (mine_ref, theirs_ref)
-            ]
-        )
-        at = half + 2 * tiles * QROWS
-        out_ref[head, at : at + QROWS] = out.astype(bf16)
-        out_ref[head, at + QROWS : at + 2 * QROWS] = packed_stat(lse)
+        out_ref[head, :half] = value[:, head_cols(head)]
+    shape = (KVH * QROWS, HD)
+    out, lse = merge(
+        [
+            (
+                ref[:, :QROWS].reshape(shape).astype(f32),
+                stat(ref[:, QROWS:].reshape(shape)),
+            )
+            for ref in (mine_ref, theirs_ref)
+        ]
+    )
+    put_pair(out_ref, half + 2 * tiles * QROWS, out, lse)
 
 
 def span_kernel(got_ref, q_ref, draft_ref, out_ref):
@@ -197,27 +267,27 @@
             out_ref[row, head] = merge(parts)[0].astype(bf16)
 
 
-def call(kernel, out_shapes, spaces, scratch=(), flops=0, moved=0):
+def call(kernel, out_shapes, spaces, scratch=(), flops=0, moved=0, limit=24):
     return pl.pallas_call(
         kernel,
         out_shape=out_shapes,
         in_specs=[pl.BlockSpec(memory_space=space) for space in spaces],
         out_specs=jax.tree.map(lambda _: pl.BlockSpec(memory_space=pltpu.VMEM), out_shapes),
         scratch_shapes=list(scratch),
-        compiler_params=pltpu.CompilerParams(vmem_limit_bytes=24 << 20),
+        compiler_params=pltpu.CompilerParams(vmem_limit_bytes=limit << 20),
         cost_estimate=pl.CostEstimate(flops=flops, bytes_accessed=moved, transcendentals=0),
     )
 
 
 V = pltpu.VMEM
 S = pltpu.SMEM
+H = pltpu.HBM
 
 
 def shards(
     prompt_acts, kv_weight, cache_kv, cache_len, block_owner, span_row, draft_query, draft_kv
 ):
     swap = [(0, 1), (1, 0)]
-    core = lax.axis_index("core")
     acts = prompt_acts[0, 0]
     span, width = acts.shape
     half = span // 2
@@ -225,29 +295,45 @@
     n_yx = lax.axis_size("yx")
     struct = jax.ShapeDtypeStruct
 
-    weight2 = lax.ppermute(kv_weight, "core", swap)
     query = draft_query[0].reshape(rows, DRAFT, KVH, GROUP, HD).transpose(0, 2, 3, 1, 4)
     query = query.reshape(rows, KVH, QROWS, HD)
     chosen = lax.dynamic_index_in_dim(query, span_row[0, 0], 0, keepdims=False)
     asked = lax.ppermute(chosen, "role", swap)
-    acts2 = lax.ppermute(
-        lax.dynamic_slice_in_dim(acts, (1 - core) * half, half, 0), "core", swap
-    )
+    weight2 = lax.ppermute(kv_weight, "core", swap)
+    acts2 = lax.ppermute(acts, "core", swap)
 
     block = struct((KVH, 2 * QROWS, HD), bf16)
     mine, other = call(
-        cache_kernel, [block, block], [S, S, V, V], flops=400_000_000, moved=2_000_000
+        cache_kernel,
+        [block, block],
+        [H, H, V, H],
+        [
+            S(block_owner.shape[1:], jnp.int32),
+            S(cache_len.shape, jnp.int32),
+            V(cache_kv.shape[1:], bf16),
+            pltpu.SemaphoreType.DMA((4,)),
+        ],
+        flops=400_000_000,
+        moved=2_000_000,
+        limit=58,
     )(block_owner[0], cache_len, query, cache_kv[0])
+    asked, other = lax.optimization_barrier((asked, other))
     theirs = lax.ppermute(other, "core", swap)
 
     length = half + 2 * (half // HD) * QROWS + 2 * QROWS
     sent = call(
         project_kernel,
         struct((KVH, length, HD), bf16),
-        [V] * 7,
-        [V((2, KVH * QROWS, width), bf16)],
+        [H, H, H, H, V, V, V],
+        [
+            V((2, half, width), bf16),
+            V((2, *kv_weight.shape), bf16),
+            V((2, KVH * QROWS, width), bf16),
+            pltpu.SemaphoreType.DMA((6,)),
+        ],
         flops=1_700_000_000,
         moved=8_000_000,
+        limit=50,
     )(acts, acts2, kv_weight, weight2, asked, mine, theirs)
     got = lax.all_to_all(sent, "yx", 0, 0, tiled=True)
 

time: 80.4 us -> 71.7 us (0.89)
  local copies, waits for them, and re-layouts: 7.14 us -> 1.76 us
  waiting for transfers between devices: 3.69 us -> 1.18 us
  Pallas kernels: 11.2 us -> 9.27 us
  blocking collectives: 41.9 us -> 42.8 us
    unnamed x16 -> x8, local copies, waits for them, and re-layouts: 5.24 us -> 0.92 us
    ppermute x1, waiting for transfers between devices: 3.68 us -> 0.01 us  [shards(): asked = lax.ppermute(chosen, 'role', swap)]
    pallas_call x2, Pallas kernels: 9.75 us -> 7.85 us  [the longest x1 3.95 us: shards(): call(project_kernel, struct((KVH, length, HD), bf16), [H, H, H, H, V, V,...]
    dynamic_slice x1 -> x0, local copies, waits for them, and re-layouts: 1.88 us -> none  [shards(): lax.dynamic_slice_in_dim(acts, (1 - core) * half, half, 0)]
    ppermute x1, waiting for transfers between devices: 0.01 us -> 1.17 us  [shards(): theirs = lax.ppermute(other, 'core', swap)]
    squeeze x1, local copies, waits for them, and re-layouts: 0.01 us -> 0.85 us  [shards(): chosen = lax.dynamic_index_in_dim(query, span_row[0, 0], 0, keepdims=False)]
  transfers between devices with their start and end apart: 4 -> 4, of which waited for: 1 -> 1; matrix products, arithmetic and copies ran while one was open for 2% -> 1% of each run, Pallas kernels for 7% -> 5%
where the time goes in v2:
time: 71.7 us; the launch traced here: 71.3 us
  blocking collectives  42.8 us (60%)
  starting transfers between devices  15.5 us (22%)
  Pallas kernels  9.27 us (13%)
  local copies, waits for them, and re-layouts  1.76 us (2%)
  waiting for transfers between devices  1.18 us (2%)
  between operations  0.75 us (1%)
    all_to_all x1, blocking collectives, shards(): got = lax.all_to_all(sent, 'yx', 0, 0, tiled=True)  26.5 us
    all_to_all x1, blocking collectives, shards(): lax.all_to_all(parts.reshape(4 * n_yx, 2 * QROWS, HD), ('role', 'yx', 'co...  16.3 us
    ppermute x1, starting transfers between devices, shards(): weight2 = lax.ppermute(kv_weight, 'core', swap)  8.91 us
    pallas_call x1, Pallas kernels, shards(): call(project_kernel, struct((KVH, length, HD), bf16), [H, H, H, H, V, V,...  3.95 us
    pallas_call x1, Pallas kernels, shards(): call(cache_kernel, [block, block], [H, H, V, H], [S(block_owner.shape[1:]...  3.89 us
    ppermute x1, starting transfers between devices, shards(): theirs = lax.ppermute(other, 'core', swap)  2.71 us
    ppermute x1, starting transfers between devices, shards(): acts2 = lax.ppermute(acts, 'core', swap)  1.92 us
    ppermute x1, starting transfers between devices, shards(): asked = lax.ppermute(chosen, 'role', swap)  1.91 us
  transfers between devices with their start and end apart: 4, of which 1 were waited for; matrix products, arithmetic and copies ran while one was open for 1% of the time, Pallas kernels for 5%

profile of v2, /device:TPU:1, one launch (start us, length us, event | category | flops | bytes accessed | tf_op | source)
XLA Modules:
  0.0 71.3 jit_solution(2914457996812874167)
XLA Ops:
  0.0 0.0 copy-start
  0.0 8.9 %collective-permute-start.1 = (bf16[512,2048]{1,0:T(8,128)(2,1)}, bf16[512,2048]{1,0:T(8,128)(2,1)}, u32[]{:S(2)}, u32[]{:S(2)}) collective-permute-start(bf16[512,2048]{1,0:T(8,128)(2,1)} %w_hbm.1), channel_id=1, source_target_pairs={{0,1},{1,0},{2,3},{3,2},{4,5},{5,4},{6,7},{7,6},{8,9},{9,8},{10,11... | collective-permute-start | bytes 6291464 | tf_op jit(solution)/shard_map/ppermute | solution.py:302
  8.9 1.9 %collective-permute-start = (bf16[1024,512]{1,0:T(8,128)(2,1)}, bf16[1024,512]{1,0:T(8,128)(2,1)S(1)}, u32[]{:S(2)}, u32[]{:S(2)}) collective-permute-start(bf16[1024,512]{1,0:T(8,128)(2,1)} %bitcast.24), channel_id=1, source_target_pairs={{0,1},{1,0},{2,3},{3,2},{4,5},{5,4},{6,7},{7,6},{8,9},{9,8},{10,11... | collective-permute-start | bytes 3145736 | tf_op jit(solution)/shard_map/ppermute | solution.py:303
  11.5 0.8 %dynamic-slice_bitcast_fusion = bf16[8,32,128]{2,1,0:T(8,128)(2,1)S(1)} fusion(bf16[2,8,32,128]{3,2,1,0:T(8,128)(2,1)} %bitcast.26, s32[]{:T(128)S(6)} %select_n.4), kind=kLoop, calls=%fused_computation | loop fusion | bytes 131076 | tf_op jit(solution)/shard_map/jit(dynamic_index_in_dim)/squeeze | solution.py:300
  12.3 1.9 %collective-permute-start.2 = (bf16[8,32,128]{2,1,0:T(8,128)(2,1)S(1)}, bf16[8,32,128]{2,1,0:T(8,128)(2,1)S(1)}, u32[]{:S(2)}, u32[]{:S(2)}) collective-permute-start(bf16[8,32,128]{2,1,0:T(8,128)(2,1)S(1)} %dynamic-slice_bitcast_fusion), channel_id=1, source_target_pairs={{0,256},{256,0},{1,257},{257,1},{2,258},{258,2},{3,259},{259,3},{4... | collective-permute-start | bytes 196616 | tf_op jit(solution)/shard_map/ppermute | solution.py:301
  14.3 3.9 %shard_map.82 = (bf16[8,64,128]{2,1,0:T(8,128)(2,1)}, bf16[8,64,128]{2,1,0:T(8,128)(2,1)}) custom-call(s32[2,16]{1,0:T(2,128)} %bitcast.31, s32[1,2]{1,0:T(1,128)} %len_hbm.1, bf16[2,8,32,128]{3,2,1,0:T(8,128)(2,1)} %bitcast.27, bf16[2,192,2048]{2,1,0:T(8,128)(2,1)} %bitcast.30), custom_call_target="tpu_custom_call" | custom-call | flops 400000000 | bytes 2000000 | tf_op jit(solution)/shard_map/pallas_call | solution.py:306
  18.2 0.0 collective-permute-done.2.q_ref
  18.2 2.7 %collective-permute-start.3 = (bf16[8,64,128]{2,1,0:T(8,128)(2,1)}, bf16[8,64,128]{2,1,0:T(8,128)(2,1)S(1)}, u32[]{:S(2)}, u32[]{:S(2)}) collective-permute-start(bf16[8,64,128]{2,1,0:T(8,128)(2,1)} %get-tuple-element.12), channel_id=1, source_target_pairs={{0,1},{1,0},{2,3},{3,2},{4,5},{5,4},{6,7},{7,6},{8,9},{9,8},{10,11... | collective-permute-start | bytes 393224 | tf_op jit(solution)/shard_map/ppermute | solution.py:321
  20.9 1.2 %collective-permute-done.3.theirs_ref = bf16[8,64,128]{2,1,0:T(8,128)(2,1)S(1)} collective-permute-done((bf16[8,64,128]{2,1,0:T(8,128)(2,1)}, bf16[8,64,128]{2,1,0:T(8,128)(2,1)S(1)}, u32[]{:S(2)}, u32[]{:S(2)}) %collective-permute-start.3) | collective-permute-done | bytes 131104 | tf_op jit(solution)/shard_map/ppermute | solution.py:321
  22.1 0.0 collective-permute-done.acts2_hbm
  22.1 0.0 collective-permute-done.1.w2_hbm
  22.1 0.0 copy-done
  22.1 0.0 copy-start.2
  22.1 0.9 %copy-done.2 = bf16[8,64,128]{2,1,0:T(8,128)(2,1)S(1)} copy-done((bf16[8,64,128]{2,1,0:T(8,128)(2,1)S(1)}, bf16[8,64,128]{2,1,0:T(8,128)(2,1)}, u32[]{:S(2)}) %copy-start.2) | copy-done | bytes 131096
  23.0 4.0 %shard_map.83 = bf16[8,832,128]{2,1,0:T(8,128)(2,1)S(1)} custom-call(bf16[1024,512]{1,0:T(8,128)(2,1)S(1)} %bitcast.25, bf16[1024,512]{1,0:T(8,128)(2,1)S(1)} %collective-permute-done.acts2_hbm, bf16[512,2048]{1,0:T(8,128)(2,1)} %w_hbm.1, bf16[512,2048]{1,0:T(8,128)(2,1)} %collective-permute-done.1.w2_hbm, ...), custom_call_target="tpu_custom_call" | custom-call | flops 1700000000 | bytes 8000000 | tf_op jit(solution)/shard_map/pallas_call | solution.py:324
  27.0 0.0 copy-start.1
  27.0 0.0 copy-start.3
  27.0 26.5 %all_to_all.10.got_ref = bf16[8,832,128]{2,1,0:T(8,128)(2,1)S(1)} all-to-all(bf16[8,832,128]{2,1,0:T(8,128)(2,1)S(1)} %shard_map.83), channel_id=1, replica_groups=mesh['role'=2,'grp'=16,'yx'=8,'core'=2] {'yx'}, dimensions={0} | all-to-all | bytes 3407872 | tf_op jit(solution)/shard_map/all_to_all | solution.py:338
  53.5 0.0 copy-done.1
  53.5 0.0 copy-done.3
  53.5 0.4 shard_map.84
  53.9 16.3 %all_to_all.11 = bf16[32,64,128]{2,1,0:T(8,128)(2,1)S(1)} all-to-all(bf16[32,64,128]{2,1,0:T(8,128)(2,1)S(1)} %bitcast.23), channel_id=1, replica_groups=mesh['role'=2,'grp'=16,'yx'=8,'core'=2] {'role','yx','core'}, dimensions={0} | all-to-all | bytes 1048576 | tf_op jit(solution)/shard_map/all_to_all | solution.py:347
  70.2 1.1 %shard_map.85 = bf16[2,8,32,128]{3,2,1,0:T(8,128)(2,1)} custom-call(s32[1,1]{1,0:T(1,128)} %copy.11.span_ref, bf16[2,16,64,128]{3,2,1,0:T(8,128)(2,1)S(1)} %bitcast.22), custom_call_target="tpu_custom_call" | custom-call | flops 10000000 | bytes 700000 | tf_op jit(solution)/shard_map/pallas_call | solution.py:350
Async XLA Ops:
  0.0 22.1 %copy-start = (bf16[1,1,1024,512]{3,2,1,0:T(8,128)(2,1)S(1)}, bf16[1,1,1024,512]{3,2,1,0:T(8,128)(2,1)}, u32[]{:S(2)}) copy-start(bf16[1,1,1024,512]{3,2,1,0:T(8,128)(2,1)} %param.8) | copy-start | bytes 3145732
  0.0 22.1 %collective-permute-start.1 = (bf16[512,2048]{1,0:T(8,128)(2,1)}, bf16[512,2048]{1,0:T(8,128)(2,1)}, u32[]{:S(2)}, u32[]{:S(2)}) collective-permute-start(bf16[512,2048]{1,0:T(8,128)(2,1)} %w_hbm.1), channel_id=1, source_target_pairs={{0,1},{1,0},{2,3},{3,2},{4,5},{5,4},{6,7},{7,6},{8,9},{9,8},{10,11... | collective-permute-start | bytes 6291464 | tf_op jit(solution)/shard_map/ppermute | solution.py:302
  8.9 13.2 %collective-permute-start = (bf16[1024,512]{1,0:T(8,128)(2,1)}, bf16[1024,512]{1,0:T(8,128)(2,1)S(1)}, u32[]{:S(2)}, u32[]{:S(2)}) collective-permute-start(bf16[1024,512]{1,0:T(8,128)(2,1)} %bitcast.24), channel_id=1, source_target_pairs={{0,1},{1,0},{2,3},{3,2},{4,5},{5,4},{6,7},{7,6},{8,9},{9,8},{10,11... | collective-permute-start | bytes 3145736 | tf_op jit(solution)/shard_map/ppermute | solution.py:303
  12.3 5.8 %collective-permute-start.2 = (bf16[8,32,128]{2,1,0:T(8,128)(2,1)S(1)}, bf16[8,32,128]{2,1,0:T(8,128)(2,1)S(1)}, u32[]{:S(2)}, u32[]{:S(2)}) collective-permute-start(bf16[8,32,128]{2,1,0:T(8,128)(2,1)S(1)} %dynamic-slice_bitcast_fusion), channel_id=1, source_target_pairs={{0,256},{256,0},{1,257},{257,1},{2,258},{258,2},{3,259},{259,3},{4... | collective-permute-start | bytes 196616 | tf_op jit(solution)/shard_map/ppermute | solution.py:301
  18.2 3.9 %collective-permute-start.3 = (bf16[8,64,128]{2,1,0:T(8,128)(2,1)}, bf16[8,64,128]{2,1,0:T(8,128)(2,1)S(1)}, u32[]{:S(2)}, u32[]{:S(2)}) collective-permute-start(bf16[8,64,128]{2,1,0:T(8,128)(2,1)} %get-tuple-element.12), channel_id=1, source_target_pairs={{0,1},{1,0},{2,3},{3,2},{4,5},{5,4},{6,7},{7,6},{8,9},{9,8},{10,11... | collective-permute-start | bytes 393224 | tf_op jit(solution)/shard_map/ppermute | solution.py:321
  22.1 0.9 %copy-start.2 = (bf16[8,64,128]{2,1,0:T(8,128)(2,1)S(1)}, bf16[8,64,128]{2,1,0:T(8,128)(2,1)}, u32[]{:S(2)}) copy-start(bf16[8,64,128]{2,1,0:T(8,128)(2,1)} %get-tuple-element.11.mine_ref) | copy-start | bytes 393220
  27.0 26.6 %copy-start.1 = (bf16[1,2,4,8192]{3,2,1,0:T(4,128)(2,1)S(1)}, bf16[1,2,4,8192]{3,2,1,0:T(4,128)(2,1)}, u32[]{:S(2)}) copy-start(bf16[1,2,4,8192]{3,2,1,0:T(4,128)(2,1)} %param.14) | copy-start | bytes 393220
  27.0 26.6 %copy-start.3 = (bf16[1,2,4,2048]{3,2,1,0:T(4,128)(2,1)S(1)}, bf16[1,2,4,2048]{3,2,1,0:T(4,128)(2,1)}, u32[]{:S(2)}) copy-start(bf16[1,2,4,2048]{3,2,1,0:T(4,128)(2,1)} %param.15) | copy-start | bytes 98308

commit v3 on v2

--- a/solution.py
+++ b/solution.py
@@ -72,15 +72,16 @@
     return slice(start + head * HD, start + (head + 1) * HD)
 
 
-def put_pair(out_ref, start, out, lse):
-    shape = (KVH, QROWS, HD)
-    out_ref[:, start : start + QROWS] = out.astype(bf16).reshape(shape)
-    out_ref[:, start + QROWS : start + 2 * QROWS] = packed_stat(lse).reshape(shape)
+def get_pair(tile):
+    shape = (tile.shape[0] * QROWS, HD)
+    return tile[:, :QROWS].reshape(shape).astype(f32), stat(tile[:, QROWS:].reshape(shape))
 
 
 def cache_kernel(
-    owner_hbm, len_hbm, q_ref, cache_hbm, mine_ref, other_ref, owner_ref, len_ref, cache_ref, sems
+    owner_hbm, len_hbm, q_ref, cache_hbm, *refs
 ):
+    out_refs, (owner_ref, len_ref, cache_ref, sems) = refs[:4], refs[4:]
+    side = lax.rem(lax.axis_index("yx"), 2)
     core = lax.axis_index("core")
     me = lax.axis_index("yx") * 2 + core
     slab = cache_ref.shape[1]
@@ -97,7 +98,7 @@
         copy.start()
     for copy in ints:
         copy.wait()
-    for k, (row, out_ref) in enumerate(zip(order, (other_ref, mine_ref))):
+    for k, row in enumerate(order):
         first = jnp.int32(0)
         for block in range(owner_ref.shape[1]):
             first = first + jnp.where(owner_ref[row, block] == me, block, 0)
@@ -122,7 +123,34 @@
                 for head in range(KVH)
             ]
         )
-        put_pair(out_ref, 0, out / safe, jnp.where(total > 0.0, top + jnp.log(safe), NEG))
+        shape = (KVH, QROWS, HD)
+        out = (out / safe).astype(bf16).reshape(shape)
+        lse = packed_stat(jnp.where(total > 0.0, top + jnp.log(safe), NEG)).reshape(shape)
+        for head in range(KVH):
+            near, far = out_refs[1 - k], out_refs[3 - k]
+
+            def put(out_ref, head=head):
+                out_ref[head // 2, :QROWS] = out[head]
+                out_ref[head // 2, QROWS:] = lse[head]
+
+            pl.when(side == head % 2)(functools.partial(put, near))
+            pl.when(side != head % 2)(functools.partial(put, far))
+
+
+def chip_kernel(a_ref, b_ref, c_ref, d_ref, *out_refs):
+    out, lse = merge([get_pair(ref[...]) for ref in (a_ref, b_ref, c_ref, d_ref)])
+    shape = (KVH // 2, QROWS, HD)
+    out = out.astype(bf16).reshape(shape)
+    lse = packed_stat(lse).reshape(shape)
+    place = lax.axis_index("yx") // 2
+    for head in range(KVH // 2):
+        for step, out_ref in enumerate(out_refs):
+
+            def put(head=head, out_ref=out_ref):
+                out_ref[0, :QROWS] = out[head]
+                out_ref[0, QROWS:] = lse[head]
+
+            pl.when(lax.rem(place + step, KVH // 2) == head)(put)
 
 
 def project_kernel(
@@ -131,8 +159,6 @@
     w_hbm,
     w2_hbm,
     q_ref,
-    mine_ref,
-    theirs_ref,
     out_ref,
     acts_ref,
     w_ref,
@@ -166,35 +192,21 @@
     for copy in loads[2:4]:
         copy.wait()
     score = (dot_nt(qw_ref[0], acts_ref[0]) + dot_nt(qw_ref[1], acts_ref[1])) * SCALE
-    high = score.astype(bf16)
-    low = (score - high.astype(f32)).astype(bf16)
-    tiles = half // HD
-    for tile in range(tiles):
-        for part, words in enumerate((high, low)):
-            at = half + (part * tiles + tile) * QROWS
-            out_ref[:, at : at + QROWS] = words[:, head_cols(tile)].reshape(KVH, QROWS, HD)
+    score = score.astype(bf16)
+    for tile in range(half // HD):
+        at = half + tile * QROWS
+        out_ref[:, at : at + QROWS] = score[:, head_cols(tile)].reshape(KVH, QROWS, HD)
     for copy in loads[4:]:
         copy.wait()
     value = dot_nn(acts_ref[0], w_ref[0, :, values]) + dot_nn(acts_ref[1], w_ref[1, :, values])
     value = value.astype(bf16)
     for head in range(KVH):
         out_ref[head, :half] = value[:, head_cols(head)]
-    shape = (KVH * QROWS, HD)
-    out, lse = merge(
-        [
-            (
-                ref[:, :QROWS].reshape(shape).astype(f32),
-                stat(ref[:, QROWS:].reshape(shape)),
-            )
-            for ref in (mine_ref, theirs_ref)
-        ]
-    )
-    put_pair(out_ref, half + 2 * tiles * QROWS, out, lse)
-
-
-def span_kernel(got_ref, q_ref, draft_ref, out_ref):
+
+
+def span_kernel(got_ref, q_ref, draft_ref, a_ref, b_ref, c_ref, d_ref, out_ref):
     parts, length, _ = got_ref.shape
-    half = (length - 2 * QROWS) * HD // (HD + 2 * QROWS)
+    half = length * HD // (HD + QROWS)
     tiles = half // HD
     role = lax.axis_index("role")
     core = lax.axis_index("core")
@@ -208,23 +220,12 @@
 
     value = total(0, half).astype(bf16)
     score = jnp.concatenate(
-        [
-            total(half + tile * QROWS, QROWS) + total(half + (tiles + tile) * QROWS, QROWS)
-            for tile in range(tiles)
-        ],
-        axis=1,
+        [total(half + tile * QROWS, QROWS) for tile in range(tiles)], axis=1
     )
     out, lse = attend(score, value)
     fresh = jnp.concatenate([out.astype(bf16), packed_stat(lse)], axis=0)
 
-    at = half + 2 * tiles * QROWS
-    cached = [
-        (
-            got_ref[part, at : at + QROWS].astype(f32),
-            stat(got_ref[part, at + QROWS : at + 2 * QROWS]),
-        )
-        for part in range(parts)
-    ]
+    cached = [get_pair(ref[...]) for ref in (a_ref, b_ref, c_ref, d_ref)]
     query = q_ref[core, head]
     start = pl.multiple_of(head * HD, HD)
     draft_keys = draft_ref[core, :, pl.ds(start, HD)].astype(f32)
@@ -302,10 +303,17 @@
     weight2 = lax.ppermute(kv_weight, "core", swap)
     acts2 = lax.ppermute(acts, "core", swap)
 
-    block = struct((KVH, 2 * QROWS, HD), bf16)
-    mine, other = call(
+    tp = ("yx", "core")
+
+    def apart(x, flip):
+        return lax.ppermute(x, tp, [(i, i ^ flip) for i in range(2 * n_yx)])
+
+    def along(x, step):
+        return lax.ppermute(x, tp, [(i, (i + 4 * step) % (2 * n_yx)) for i in range(2 * n_yx)])
+
+    pieces = call(
         cache_kernel,
-        [block, block],
+        [struct((KVH // 2, 2 * QROWS, HD), bf16)] * 4,
         [H, H, V, H],
         [
             S(block_owner.shape[1:], jnp.int32),
@@ -317,14 +325,13 @@
         moved=2_000_000,
         limit=58,
     )(block_owner[0], cache_len, query, cache_kv[0])
-    asked, other = lax.optimization_barrier((asked, other))
-    theirs = lax.ppermute(other, "core", swap)
-
-    length = half + 2 * (half // HD) * QROWS + 2 * QROWS
+    asked, pieces = lax.optimization_barrier((asked, pieces))
+
+    length = half + (half // HD) * QROWS
     sent = call(
         project_kernel,
         struct((KVH, length, HD), bf16),
-        [H, H, H, H, V, V, V],
+        [H, H, H, H, V],
         [
             V((2, half, width), bf16),
             V((2, *kv_weight.shape), bf16),
@@ -334,16 +341,26 @@
         flops=1_700_000_000,
         moved=8_000_000,
         limit=50,
-    )(acts, acts2, kv_weight, weight2, asked, mine, theirs)
+    )(acts, acts2, kv_weight, weight2, asked)
+    sent, pieces = lax.optimization_barrier((sent, pieces))
     got = lax.all_to_all(sent, "yx", 0, 0, tiled=True)
+    pieces = [pieces[0]] + [apart(pieces[flip], flip) for flip in (1, 2, 3)]
+    pieces = call(
+        chip_kernel,
+        [struct((1, 2 * QROWS, HD), bf16)] * (n_yx // 2),
+        [V] * 4,
+        flops=10_000_000,
+        moved=400_000,
+    )(*pieces)
+    pieces = [pieces[0]] + [along(pieces[step], step) for step in range(1, n_yx // 2)]
 
     parts = call(
         span_kernel,
         struct((2, 2 * n_yx, 2 * QROWS, HD), bf16),
-        [V, V, V],
+        [V] * 7,
         flops=20_000_000,
         moved=3_000_000,
-    )(got, query, draft_kv[0])
+    )(got, query, draft_kv[0], *pieces)
     parts = lax.all_to_all(
         parts.reshape(4 * n_yx, 2 * QROWS, HD), ("role", "yx", "core"), 0, 0, tiled=True
     )

time: 71.7 us -> 80.8 us (1.13)
  blocking collectives: 42.8 us -> 18.5 us
  starting transfers between devices: 15.5 us -> 36.2 us
  waiting for transfers between devices: 1.18 us -> 13 us
  Pallas kernels: 9.27 us -> 10.8 us
  local copies, waits for them, and re-layouts: 1.76 us -> 0.88 us
    all_to_all x1 -> x0, blocking collectives: 26.5 us -> none  [shards(): got = lax.all_to_all(sent, 'yx', 0, 0, tiled=True)]
    ppermute x1 -> x6, starting transfers between devices: 2.71 us -> 19.8 us  [the longest x3 10.2 us: along(): lax.ppermute(x, tp, [(i, (i + 4 * step) % (2 * n_yx)) for i in range(2 *...]
    ppermute x1 -> x6, waiting for transfers between devices: 1.17 us -> 13 us  [the longest x3 11.6 us: apart(): return lax.ppermute(x, tp, [(i, i ^ flip) for i in range(2 * n_yx)])]
    all_to_all x0 -> x1, starting transfers between devices: none -> 3.71 us  [shards(): got = lax.all_to_all(sent, 'yx', 0, 0, tiled=True)]
    all_to_all x1, blocking collectives: 16.3 us -> 18.5 us  [shards(): lax.all_to_all(parts.reshape(4 * n_yx, 2 * QROWS, HD), ('role', 'yx', 'co...]
    pallas_call x3 -> x4, Pallas kernels: 8.22 us -> 9.71 us  [the longest x1 5.03 us: shards(): call(project_kernel, struct((KVH, length, HD), bf16), [H, H, H, H, V], [V...]
    unnamed x8 -> x14, local copies, waits for them, and re-layouts: 0.92 us -> 0.04 us
  transfers between devices with their start and end apart: 4 -> 10, of which waited for: 1 -> 3; matrix products, arithmetic and copies ran while one was open for 1% -> 1% of each run, Pallas kernels for 5% -> 5%
where the time goes in v3:
time: 80.8 us; the launch traced here: 80.3 us
  starting transfers between devices  36.2 us (45%)
  blocking collectives  18.5 us (23%)
  waiting for transfers between devices  13 us (16%)
  Pallas kernels  10.8 us (13%)
  between operations  0.9 us (1%)
  local copies, waits for them, and re-layouts  0.88 us (1%)
    all_to_all x1, blocking collectives, shards(): lax.all_to_all(parts.reshape(4 * n_yx, 2 * QROWS, HD), ('role', 'yx', 'co...  18.5 us
    ppermute x3, waiting for transfers between devices, apart(): return lax.ppermute(x, tp, [(i, i ^ flip) for i in range(2 * n_yx)])  11.6 us
    ppermute x3, starting transfers between devices, along(): lax.ppermute(x, tp, [(i, (i + 4 * step) % (2 * n_yx)) for i in range(2 *...  10.2 us
    ppermute x3, starting transfers between devices, apart(): return lax.ppermute(x, tp, [(i, i ^ flip) for i in range(2 * n_yx)])  9.55 us
    ppermute x1, starting transfers between devices, shards(): weight2 = lax.ppermute(kv_weight, 'core', swap)  8.91 us
    pallas_call x1, Pallas kernels, shards(): call(project_kernel, struct((KVH, length, HD), bf16), [H, H, H, H, V], [V...  5.03 us
    pallas_call x1, Pallas kernels, shards(): call(cache_kernel, [struct((KVH // 2, 2 * QROWS, HD), bf16)] * 4, [H, H,...  4.04 us
    all_to_all x1, starting transfers between devices, shards(): got = lax.all_to_all(sent, 'yx', 0, 0, tiled=True)  3.71 us
  transfers between devices with their start and end apart: 10, of which 3 were waited for; matrix products, arithmetic and copies ran while one was open for 1% of the time, Pallas kernels for 5%

profile of v3, /device:TPU:1, one launch (start us, length us, event | category | flops | bytes accessed | tf_op | source)
XLA Modules:
  0.0 80.3 jit_solution(10579063259507223156)
XLA Ops:
  0.0 8.9 %collective-permute-start.1 = (bf16[512,2048]{1,0:T(8,128)(2,1)}, bf16[512,2048]{1,0:T(8,128)(2,1)}, u32[]{:S(2)}, u32[]{:S(2)}) collective-permute-start(bf16[512,2048]{1,0:T(8,128)(2,1)} %w_hbm.1), channel_id=1, source_target_pairs={{0,1},{1,0},{2,3},{3,2},{4,5},{5,4},{6,7},{7,6},{8,9},{9,8},{10,11... | collective-permute-start | bytes 6291464 | tf_op jit(solution)/shard_map/ppermute | solution.py:303
  8.9 1.9 %collective-permute-start = (bf16[1024,512]{1,0:T(8,128)(2,1)}, bf16[1024,512]{1,0:T(8,128)(2,1)S(1)}, u32[]{:S(2)}, u32[]{:S(2)}) collective-permute-start(bf16[1024,512]{1,0:T(8,128)(2,1)} %bitcast.24), channel_id=1, source_target_pairs={{0,1},{1,0},{2,3},{3,2},{4,5},{5,4},{6,7},{7,6},{8,9},{9,8},{10,11... | collective-permute-start | bytes 3145736 | tf_op jit(solution)/shard_map/ppermute | solution.py:304
  11.5 0.8 %dynamic-slice_bitcast_fusion = bf16[8,32,128]{2,1,0:T(8,128)(2,1)S(1)} fusion(bf16[2,8,32,128]{3,2,1,0:T(8,128)(2,1)} %bitcast.26, s32[]{:T(128)S(6)} %select_n.4), kind=kLoop, calls=%fused_computation | loop fusion | bytes 131076 | tf_op jit(solution)/shard_map/jit(dynamic_index_in_dim)/squeeze | solution.py:301
  12.3 1.9 %collective-permute-start.2 = (bf16[8,32,128]{2,1,0:T(8,128)(2,1)S(1)}, bf16[8,32,128]{2,1,0:T(8,128)(2,1)S(1)}, u32[]{:S(2)}, u32[]{:S(2)}) collective-permute-start(bf16[8,32,128]{2,1,0:T(8,128)(2,1)S(1)} %dynamic-slice_bitcast_fusion), channel_id=1, source_target_pairs={{0,256},{256,0},{1,257},{257,1},{2,258},{258,2},{3,259},{259,3},{4... | collective-permute-start | bytes 196616 | tf_op jit(solution)/shard_map/ppermute | solution.py:302
  14.3 4.0 %shard_map.82 = (bf16[4,64,128]{2,1,0:T(8,128)(2,1)}, bf16[4,64,128]{2,1,0:T(8,128)(2,1)}, bf16[4,64,128]{2,1,0:T(8,128)(2,1)}, bf16[4,64,128]{2,1,0:T(8,128)(2,1)}) custom-call(s32[2,16]{1,0:T(2,128)} %bitcast.31, s32[1,2]{1,0:T(1,128)} %len_hbm.1, bf16[2,8,32,128]{3,2,1,0:T(8,128)(2,1)} %bitcast.27, bf16[2,192,2048]{2,1,0:T(8,128)(2,1)} %bitcast.30), custom_call_target="tpu_custom_call" | custom-call | flops 400000000 | bytes 2000000 | tf_op jit(solution)/shard_map/pallas_call | solution.py:314
  18.3 0.0 collective-permute-done.2.q_ref
  18.3 5.0 %shard_map.83 = bf16[8,640,128]{2,1,0:T(8,128)(2,1)} custom-call(bf16[1024,512]{1,0:T(8,128)(2,1)S(1)} %bitcast.25, bf16[1024,512]{1,0:T(8,128)(2,1)S(1)} %collective-permute-done.acts2_hbm, bf16[512,2048]{1,0:T(8,128)(2,1)} %w_hbm.1, bf16[512,2048]{1,0:T(8,128)(2,1)} %collective-permute-done.1.w2_hbm, bf16[8,32,128]{2,1,0:T(8,128)(2,1)S(1)} %collective-permute-done.2.q_ref), custom_call_target="tpu_custom_call" | custom-call | flops 1700000000 | bytes 8000000 | tf_op jit(solution)/shard_map/pallas_call | solution.py:331
  23.4 0.0 copy-start.2
  23.4 0.0 copy-start.1
  23.4 0.0 copy-start.3
  23.4 3.7 %all-to-all-start = ((bf16[8,640,128]{2,1,0:T(8,128)(2,1)}), bf16[8,640,128]{2,1,0:T(8,128)(2,1)S(1)}, u32[]{:S(2)}, u32[]{:S(2)}) async-start(bf16[8,640,128]{2,1,0:T(8,128)(2,1)} %shard_map.83), calls=%async_computation | async-start | bytes 2621440 | tf_op jit(solution)/shard_map/all_to_all | solution.py:346
  27.2 2.6 %collective-permute-start.3 = (bf16[4,64,128]{2,1,0:T(8,128)(2,1)S(1)}, bf16[4,64,128]{2,1,0:T(8,128)(2,1)S(1)}, u32[]{:S(2)}, u32[]{:S(2)}) collective-permute-start(bf16[4,64,128]{2,1,0:T(8,128)(2,1)S(1)} %copy-done.6), channel_id=1, source_target_pairs={{0,1},{1,0},{2,3},{3,2},{4,5},{5,4},{6,7},{7,6},{8,9},{9,8},{10,11... | collective-permute-start | bytes 196616 | tf_op jit(solution)/shard_map/ppermute | solution.py:309
  29.8 5.0 %collective-permute-start.4 = (bf16[4,64,128]{2,1,0:T(8,128)(2,1)S(1)}, bf16[4,64,128]{2,1,0:T(8,128)(2,1)S(1)}, u32[]{:S(2)}, u32[]{:S(2)}) collective-permute-start(bf16[4,64,128]{2,1,0:T(8,128)(2,1)S(1)} %copy-done.5), channel_id=1, source_target_pairs={{0,2},{1,3},{2,0},{3,1},{4,6},{5,7},{6,4},{7,5},{8,10},{9,11},{10,... | collective-permute-start | bytes 196616 | tf_op jit(solution)/shard_map/ppermute | solution.py:309
  34.8 2.0 %collective-permute-start.5 = (bf16[4,64,128]{2,1,0:T(8,128)(2,1)S(1)}, bf16[4,64,128]{2,1,0:T(8,128)(2,1)S(1)}, u32[]{:S(2)}, u32[]{:S(2)}) collective-permute-start(bf16[4,64,128]{2,1,0:T(8,128)(2,1)S(1)} %copy-done.4), channel_id=1, source_target_pairs={{0,3},{1,2},{2,1},{3,0},{4,7},{5,6},{6,5},{7,4},{8,11},{9,10},{10,... | collective-permute-start | bytes 196616 | tf_op jit(solution)/shard_map/ppermute | solution.py:309
  36.8 9.0 %collective-permute-done.4.c_ref = bf16[4,64,128]{2,1,0:T(8,128)(2,1)S(1)} collective-permute-done((bf16[4,64,128]{2,1,0:T(8,128)(2,1)S(1)}, bf16[4,64,128]{2,1,0:T(8,128)(2,1)S(1)}, u32[]{:S(2)}, u32[]{:S(2)}) %collective-permute-start.4) | collective-permute-done | bytes 65568 | tf_op jit(solution)/shard_map/ppermute | solution.py:309
  45.8 2.5 %collective-permute-done.5.d_ref = bf16[4,64,128]{2,1,0:T(8,128)(2,1)S(1)} collective-permute-done((bf16[4,64,128]{2,1,0:T(8,128)(2,1)S(1)}, bf16[4,64,128]{2,1,0:T(8,128)(2,1)S(1)}, u32[]{:S(2)}, u32[]{:S(2)}) %collective-permute-start.5) | collective-permute-done | bytes 65568 | tf_op jit(solution)/shard_map/ppermute | solution.py:309
  48.3 0.3 shard_map.84
  48.7 2.9 %collective-permute-start.6 = (bf16[1,64,128]{2,1,0:T(8,128)(2,1)S(1)}, bf16[1,64,128]{2,1,0:T(8,128)(2,1)S(1)}, u32[]{:S(2)}, u32[]{:S(2)}) collective-permute-start(bf16[1,64,128]{2,1,0:T(8,128)(2,1)S(1)} %get-tuple-element.38), channel_id=1, source_target_pairs={{0,4},{1,5},{2,6},{3,7},{4,8},{5,9},{6,10},{7,11},{8,12},{9,13},{1... | collective-permute-start | bytes 49160 | tf_op jit(solution)/shard_map/ppermute | solution.py:312
  51.5 4.3 %collective-permute-start.7 = (bf16[1,64,128]{2,1,0:T(8,128)(2,1)S(1)}, bf16[1,64,128]{2,1,0:T(8,128)(2,1)S(1)}, u32[]{:S(2)}, u32[]{:S(2)}) collective-permute-start(bf16[1,64,128]{2,1,0:T(8,128)(2,1)S(1)} %get-tuple-element.39), channel_id=1, source_target_pairs={{0,8},{1,9},{2,10},{3,11},{4,12},{5,13},{6,14},{7,15},{8,0},{9,1},... | collective-permute-start | bytes 49160 | tf_op jit(solution)/shard_map/ppermute | solution.py:312
  55.9 3.0 %collective-permute-start.8 = (bf16[1,64,128]{2,1,0:T(8,128)(2,1)S(1)}, bf16[1,64,128]{2,1,0:T(8,128)(2,1)S(1)}, u32[]{:S(2)}, u32[]{:S(2)}) collective-permute-start(bf16[1,64,128]{2,1,0:T(8,128)(2,1)S(1)} %get-tuple-element.40), channel_id=1, source_target_pairs={{0,12},{1,13},{2,14},{3,15},{4,0},{5,1},{6,2},{7,3},{8,4},{9,5},{1... | collective-permute-start | bytes 49160 | tf_op jit(solution)/shard_map/ppermute | solution.py:312
  58.9 1.4 %collective-permute-done.8.d_ref = bf16[1,64,128]{2,1,0:T(8,128)(2,1)S(1)} collective-permute-done((bf16[1,64,128]{2,1,0:T(8,128)(2,1)S(1)}, bf16[1,64,128]{2,1,0:T(8,128)(2,1)S(1)}, u32[]{:S(2)}, u32[]{:S(2)}) %collective-permute-start.8) | collective-permute-done | bytes 16416 | tf_op jit(solution)/shard_map/ppermute | solution.py:312
  60.4 0.3 shard_map.85
  60.7 18.5 %all_to_all.10 = bf16[32,64,128]{2,1,0:T(8,128)(2,1)S(1)} all-to-all(bf16[32,64,128]{2,1,0:T(8,128)(2,1)S(1)} %bitcast.23), channel_id=1, replica_groups=mesh['role'=2,'grp'=16,'yx'=8,'core'=2] {'role','yx','core'}, dimensions={0} | all-to-all | bytes 1048576 | tf_op jit(solution)/shard_map/all_to_all | solution.py:364
  79.2 1.1 %shard_map.86 = bf16[2,8,32,128]{3,2,1,0:T(8,128)(2,1)} custom-call(s32[1,1]{1,0:T(1,128)} %copy.11.span_ref, bf16[2,16,64,128]{3,2,1,0:T(8,128)(2,1)S(1)} %bitcast.22), custom_call_target="tpu_custom_call" | custom-call | flops 10000000 | bytes 700000 | tf_op jit(solution)/shard_map/pallas_call | solution.py:367
  (17 shorter events, 0.0 us)
Async XLA Ops:
  0.0 18.3 %copy-start = (bf16[1,1,1024,512]{3,2,1,0:T(8,128)(2,1)S(1)}, bf16[1,1,1024,512]{3,2,1,0:T(8,128)(2,1)}, u32[]{:S(2)}) copy-start(bf16[1,1,1024,512]{3,2,1,0:T(8,128)(2,1)} %param.8) | copy-start | bytes 3145732
  0.0 18.3 %collective-permute-start.1 = (bf16[512,2048]{1,0:T(8,128)(2,1)}, bf16[512,2048]{1,0:T(8,128)(2,1)}, u32[]{:S(2)}, u32[]{:S(2)}) collective-permute-start(bf16[512,2048]{1,0:T(8,128)(2,1)} %w_hbm.1), channel_id=1, source_target_pairs={{0,1},{1,0},{2,3},{3,2},{4,5},{5,4},{6,7},{7,6},{8,9},{9,8},{10,11... | collective-permute-start | bytes 6291464 | tf_op jit(solution)/shard_map/ppermute | solution.py:303
  8.9 9.4 %collective-permute-start = (bf16[1024,512]{1,0:T(8,128)(2,1)}, bf16[1024,512]{1,0:T(8,128)(2,1)S(1)}, u32[]{:S(2)}, u32[]{:S(2)}) collective-permute-start(bf16[1024,512]{1,0:T(8,128)(2,1)} %bitcast.24), channel_id=1, source_target_pairs={{0,1},{1,0},{2,3},{3,2},{4,5},{5,4},{6,7},{7,6},{8,9},{9,8},{10,11... | collective-permute-start | bytes 3145736 | tf_op jit(solution)/shard_map/ppermute | solution.py:304
  12.3 6.0 %collective-permute-start.2 = (bf16[8,32,128]{2,1,0:T(8,128)(2,1)S(1)}, bf16[8,32,128]{2,1,0:T(8,128)(2,1)S(1)}, u32[]{:S(2)}, u32[]{:S(2)}) collective-permute-start(bf16[8,32,128]{2,1,0:T(8,128)(2,1)S(1)} %dynamic-slice_bitcast_fusion), channel_id=1, source_target_pairs={{0,256},{256,0},{1,257},{257,1},{2,258},{258,2},{3,259},{259,3},{4... | collective-permute-start | bytes 196616 | tf_op jit(solution)/shard_map/ppermute | solution.py:302
  23.4 3.8 %copy-start.6 = (bf16[4,64,128]{2,1,0:T(8,128)(2,1)S(1)}, bf16[4,64,128]{2,1,0:T(8,128)(2,1)}, u32[]{:S(2)}) copy-start(bf16[4,64,128]{2,1,0:T(8,128)(2,1)} %get-tuple-element.34) | copy-start | bytes 196612
  23.4 6.4 %copy-start.5 = (bf16[4,64,128]{2,1,0:T(8,128)(2,1)S(1)}, bf16[4,64,128]{2,1,0:T(8,128)(2,1)}, u32[]{:S(2)}) copy-start(bf16[4,64,128]{2,1,0:T(8,128)(2,1)} %get-tuple-element.35) | copy-start | bytes 196612
  23.4 11.4 %copy-start.4 = (bf16[4,64,128]{2,1,0:T(8,128)(2,1)S(1)}, bf16[4,64,128]{2,1,0:T(8,128)(2,1)}, u32[]{:S(2)}) copy-start(bf16[4,64,128]{2,1,0:T(8,128)(2,1)} %get-tuple-element.36) | copy-start | bytes 196612
  23.4 24.9 %copy-start.2 = (bf16[4,64,128]{2,1,0:T(8,128)(2,1)S(1)}, bf16[4,64,128]{2,1,0:T(8,128)(2,1)}, u32[]{:S(2)}) copy-start(bf16[4,64,128]{2,1,0:T(8,128)(2,1)} %get-tuple-element.33.a_ref) | copy-start | bytes 196612
  23.4 36.9 %copy-start.1 = (bf16[1,2,4,8192]{3,2,1,0:T(4,128)(2,1)S(1)}, bf16[1,2,4,8192]{3,2,1,0:T(4,128)(2,1)}, u32[]{:S(2)}) copy-start(bf16[1,2,4,8192]{3,2,1,0:T(4,128)(2,1)} %param.14) | copy-start | bytes 393220
  23.4 36.9 %copy-start.3 = (bf16[1,2,4,2048]{3,2,1,0:T(4,128)(2,1)S(1)}, bf16[1,2,4,2048]{3,2,1,0:T(4,128)(2,1)}, u32[]{:S(2)}) copy-start(bf16[1,2,4,2048]{3,2,1,0:T(4,128)(2,1)} %param.15) | copy-start | bytes 98308
  23.4 36.9 %all-to-all-start = ((bf16[8,640,128]{2,1,0:T(8,128)(2,1)}), bf16[8,640,128]{2,1,0:T(8,128)(2,1)S(1)}, u32[]{:S(2)}, u32[]{:S(2)}) async-start(bf16[8,640,128]{2,1,0:T(8,128)(2,1)} %shard_map.83), calls=%async_computation | async-start | bytes 2621440 | tf_op jit(solution)/shard_map/all_to_all | solution.py:346
  27.2 9.6 %collective-permute-start.3 = (bf16[4,64,128]{2,1,0:T(8,128)(2,1)S(1)}, bf16[4,64,128]{2,1,0:T(8,128)(2,1)S(1)}, u32[]{:S(2)}, u32[]{:S(2)}) collective-permute-start(bf16[4,64,128]{2,1,0:T(8,128)(2,1)S(1)} %copy-done.6), channel_id=1, source_target_pairs={{0,1},{1,0},{2,3},{3,2},{4,5},{5,4},{6,7},{7,6},{8,9},{9,8},{10,11... | collective-permute-start | bytes 196616 | tf_op jit(solution)/shard_map/ppermute | solution.py:309
  29.8 16.0 %collective-permute-start.4 = (bf16[4,64,128]{2,1,0:T(8,128)(2,1)S(1)}, bf16[4,64,128]{2,1,0:T(8,128)(2,1)S(1)}, u32[]{:S(2)}, u32[]{:S(2)}) collective-permute-start(bf16[4,64,128]{2,1,0:T(8,128)(2,1)S(1)} %copy-done.5), channel_id=1, source_target_pairs={{0,2},{1,3},{2,0},{3,1},{4,6},{5,7},{6,4},{7,5},{8,10},{9,11},{10,... | collective-permute-start | bytes 196616 | tf_op jit(solution)/shard_map/ppermute | solution.py:309
  34.8 13.5 %collective-permute-start.5 = (bf16[4,64,128]{2,1,0:T(8,128)(2,1)S(1)}, bf16[4,64,128]{2,1,0:T(8,128)(2,1)S(1)}, u32[]{:S(2)}, u32[]{:S(2)}) collective-permute-start(bf16[4,64,128]{2,1,0:T(8,128)(2,1)S(1)} %copy-done.4), channel_id=1, source_target_pairs={{0,3},{1,2},{2,1},{3,0},{4,7},{5,6},{6,5},{7,4},{8,11},{9,10},{10,... | collective-permute-start | bytes 196616 | tf_op jit(solution)/shard_map/ppermute | solution.py:309
  48.7 10.2 %collective-permute-start.6 = (bf16[1,64,128]{2,1,0:T(8,128)(2,1)S(1)}, bf16[1,64,128]{2,1,0:T(8,128)(2,1)S(1)}, u32[]{:S(2)}, u32[]{:S(2)}) collective-permute-start(bf16[1,64,128]{2,1,0:T(8,128)(2,1)S(1)} %get-tuple-element.38), channel_id=1, source_target_pairs={{0,4},{1,5},{2,6},{3,7},{4,8},{5,9},{6,10},{7,11},{8,12},{9,13},{1... | collective-permute-start | bytes 49160 | tf_op jit(solution)/shard_map/ppermute | solution.py:312
  51.5 7.4 %collective-permute-start.7 = (bf16[1,64,128]{2,1,0:T(8,128)(2,1)S(1)}, bf16[1,64,128]{2,1,0:T(8,128)(2,1)S(1)}, u32[]{:S(2)}, u32[]{:S(2)}) collective-permute-start(bf16[1,64,128]{2,1,0:T(8,128)(2,1)S(1)} %get-tuple-element.39), channel_id=1, source_target_pairs={{0,8},{1,9},{2,10},{3,11},{4,12},{5,13},{6,14},{7,15},{8,0},{9,1},... | collective-permute-start | bytes 49160 | tf_op jit(solution)/shard_map/ppermute | solution.py:312
  55.9 4.5 %collective-permute-start.8 = (bf16[1,64,128]{2,1,0:T(8,128)(2,1)S(1)}, bf16[1,64,128]{2,1,0:T(8,128)(2,1)S(1)}, u32[]{:S(2)}, u32[]{:S(2)}) collective-permute-start(bf16[1,64,128]{2,1,0:T(8,128)(2,1)S(1)} %get-tuple-element.40), channel_id=1, source_target_pairs={{0,12},{1,13},{2,14},{3,15},{4,0},{5,1},{6,2},{7,3},{8,4},{9,5},{1... | collective-permute-start | bytes 49160 | tf_op jit(solution)/shard_map/ppermute | solution.py:312

commit v4 on v2

--- a/solution.py
+++ b/solution.py
@@ -78,26 +78,57 @@
     out_ref[:, start + QROWS : start + 2 * QROWS] = packed_stat(lse).reshape(shape)
 
 
-def cache_kernel(
-    owner_hbm, len_hbm, q_ref, cache_hbm, mine_ref, other_ref, owner_ref, len_ref, cache_ref, sems
+def get_pair(ref, start):
+    shape = (KVH * QROWS, HD)
+    middle = start + QROWS
+    return (
+        ref[:, start:middle].reshape(shape).astype(f32),
+        stat(ref[:, middle : middle + QROWS].reshape(shape)),
+    )
+
+
+def front_kernel(
+    owner_hbm,
+    len_hbm,
+    q_hbm,
+    cache_hbm,
+    acts_hbm,
+    w_hbm,
+    away_ref,
+    value_ref,
+    mine_ref,
+    owner_ref,
+    len_ref,
+    q_ref,
+    cache_ref,
+    acts_ref,
+    w_ref,
+    sems,
 ):
     core = lax.axis_index("core")
     me = lax.axis_index("yx") * 2 + core
     slab = cache_ref.shape[1]
+    span = acts_ref.shape[0]
+    half = span // 2
     order = (1 - core, core)
     ints = [
         pltpu.make_async_copy(owner_hbm, owner_ref, sems.at[0]),
         pltpu.make_async_copy(len_hbm, len_ref, sems.at[1]),
+        pltpu.make_async_copy(q_hbm, q_ref, sems.at[2]),
     ]
     loads = [
-        pltpu.make_async_copy(cache_hbm.at[row], cache_ref.at[k], sems.at[2 + k])
+        pltpu.make_async_copy(cache_hbm.at[row], cache_ref.at[k], sems.at[3 + k])
         for k, row in enumerate(order)
     ]
-    for copy in (*ints, *loads):
+    late = [
+        pltpu.make_async_copy(acts_hbm, acts_ref, sems.at[5]),
+        pltpu.make_async_copy(w_hbm.at[:, COLS : 2 * COLS], w_ref, sems.at[6]),
+    ]
+    for copy in (*ints, *loads, *late):
         copy.start()
     for copy in ints:
         copy.wait()
-    for k, (row, out_ref) in enumerate(zip(order, (other_ref, mine_ref))):
+    for k, row in enumerate(order):
         first = jnp.int32(0)
         for block in range(owner_ref.shape[1]):
             first = first + jnp.where(owner_ref[row, block] == me, block, 0)
@@ -122,79 +153,77 @@
                 for head in range(KVH)
             ]
         )
-        put_pair(out_ref, 0, out / safe, jnp.where(total > 0.0, top + jnp.log(safe), NEG))
-
-
-def project_kernel(
-    acts_hbm,
-    acts2_hbm,
-    w_hbm,
-    w2_hbm,
-    q_ref,
-    mine_ref,
-    theirs_ref,
-    out_ref,
-    acts_ref,
-    w_ref,
-    qw_ref,
-    sems,
+        lse = jnp.where(total > 0.0, top + jnp.log(safe), NEG)
+        if k == 0:
+            put_pair(away_ref, half, out / safe, lse)
+        else:
+            put_pair(mine_ref, 0, out / safe, lse)
+    for copy in late:
+        copy.wait()
+    for row, out_ref in zip(order, (away_ref, value_ref)):
+        tokens = acts_ref[pl.ds(pl.multiple_of(row * half, half), half), :]
+        value = dot_nn(tokens, w_ref[...]).astype(bf16)
+        for head in range(KVH):
+            out_ref[head, :half] = value[:, head_cols(head)]
+
+
+def score_kernel(
+    q_ref, acts_hbm, w_hbm, _, away_hbm, own_ref, acts_ref, w_ref, qw_ref, words_ref, sems
 ):
     core = lax.axis_index("core")
-    half = acts_ref.shape[1]
-    mine = pl.ds(pl.multiple_of(core * half, half), half)
-    keys, values = slice(0, COLS), slice(COLS, 2 * COLS)
+    half = acts_ref.shape[0] // 2
     loads = [
-        pltpu.make_async_copy(source.at[rows, cols], held.at[k, :, cols], sems.at[number])
-        for number, (source, rows, cols, held, k) in enumerate(
-            [
-                (w_hbm, slice(None), keys, w_ref, 0),
-                (w2_hbm, slice(None), keys, w_ref, 1),
-                (acts_hbm, mine, slice(None), acts_ref, 0),
-                (acts2_hbm, mine, slice(None), acts_ref, 1),
-                (w_hbm, slice(None), values, w_ref, 0),
-                (w2_hbm, slice(None), values, w_ref, 1),
-            ]
-        )
+        pltpu.make_async_copy(w_hbm.at[:, 0:COLS], w_ref, sems.at[0]),
+        pltpu.make_async_copy(acts_hbm, acts_ref, sems.at[1]),
     ]
     for copy in loads:
         copy.start()
-    for k in range(2):
-        loads[k].wait()
-        for head in range(KVH):
-            rows = slice(head * QROWS, (head + 1) * QROWS)
-            qw_ref[k, rows] = dot_nt(q_ref[head], w_ref[k, :, head_cols(head)]).astype(bf16)
-    for copy in loads[2:4]:
-        copy.wait()
-    score = (dot_nt(qw_ref[0], acts_ref[0]) + dot_nt(qw_ref[1], acts_ref[1])) * SCALE
+    loads[0].wait()
+    for head in range(KVH):
+        rows = slice(head * QROWS, (head + 1) * QROWS)
+        qw_ref[rows] = dot_nt(q_ref[head], w_ref[:, head_cols(head)]).astype(bf16)
+    loads[1].wait()
+    tiles = half // HD
+
+    def tokens(row):
+        return acts_ref[pl.ds(pl.multiple_of(row * half, half), half), :]
+
+    score = dot_nt(qw_ref[...], tokens(1 - core)) * SCALE
     high = score.astype(bf16)
     low = (score - high.astype(f32)).astype(bf16)
+    for part, words in enumerate((high, low)):
+        for tile in range(tiles):
+            at = (part * tiles + tile) * QROWS
+            words_ref[:, at : at + QROWS] = words[:, head_cols(tile)].reshape(KVH, QROWS, HD)
+    start = half + 2 * QROWS
+    store = pltpu.make_async_copy(
+        words_ref, away_hbm.at[:, start : start + 2 * tiles * QROWS], sems.at[2]
+    )
+    store.start()
+    own_ref[...] = dot_nt(qw_ref[...], tokens(core)) * SCALE
+    store.wait()
+
+
+def pack_kernel(got_ref, value_ref, own_ref, mine_ref, out_ref):
+    half = value_ref.shape[1]
     tiles = half // HD
+    out_ref[:, :half] = (value_ref[...].astype(f32) + got_ref[:, :half].astype(f32)).astype(bf16)
+    shape = (KVH, QROWS, HD)
+    start = half + 2 * QROWS
     for tile in range(tiles):
-        for part, words in enumerate((high, low)):
-            at = half + (part * tiles + tile) * QROWS
-            out_ref[:, at : at + QROWS] = words[:, head_cols(tile)].reshape(KVH, QROWS, HD)
-    for copy in loads[4:]:
-        copy.wait()
-    value = dot_nn(acts_ref[0], w_ref[0, :, values]) + dot_nn(acts_ref[1], w_ref[1, :, values])
-    value = value.astype(bf16)
-    for head in range(KVH):
-        out_ref[head, :half] = value[:, head_cols(head)]
-    shape = (KVH * QROWS, HD)
-    out, lse = merge(
-        [
-            (
-                ref[:, :QROWS].reshape(shape).astype(f32),
-                stat(ref[:, QROWS:].reshape(shape)),
-            )
-            for ref in (mine_ref, theirs_ref)
-        ]
-    )
-    put_pair(out_ref, half + 2 * tiles * QROWS, out, lse)
+        score = own_ref[:, head_cols(tile)].reshape(shape)
+        for part in range(2):
+            at = start + (part * tiles + tile) * QROWS
+            score = score + got_ref[:, at : at + QROWS].astype(f32)
+        at = half + tile * QROWS
+        out_ref[:, at : at + QROWS] = score.astype(bf16)
+    out, lse = merge([get_pair(mine_ref, 0), get_pair(got_ref, half)])
+    put_pair(out_ref, half + tiles * QROWS, out, lse)
 
 
 def span_kernel(got_ref, q_ref, draft_ref, out_ref):
     parts, length, _ = got_ref.shape
-    half = (length - 2 * QROWS) * HD // (HD + 2 * QROWS)
+    half = (length - 2 * QROWS) * HD // (HD + QROWS)
     tiles = half // HD
     role = lax.axis_index("role")
     core = lax.axis_index("core")
@@ -208,16 +237,12 @@
 
     value = total(0, half).astype(bf16)
     score = jnp.concatenate(
-        [
-            total(half + tile * QROWS, QROWS) + total(half + (tiles + tile) * QROWS, QROWS)
-            for tile in range(tiles)
-        ],
-        axis=1,
+        [total(half + tile * QROWS, QROWS) for tile in range(tiles)], axis=1
     )
     out, lse = attend(score, value)
     fresh = jnp.concatenate([out.astype(bf16), packed_stat(lse)], axis=0)
 
-    at = half + 2 * tiles * QROWS
+    at = half + tiles * QROWS
     cached = [
         (
             got_ref[part, at : at + QROWS].astype(f32),
@@ -267,12 +292,16 @@
             out_ref[row, head] = merge(parts)[0].astype(bf16)
 
 
-def call(kernel, out_shapes, spaces, scratch=(), flops=0, moved=0, limit=24):
+def call(kernel, out_shapes, spaces, scratch=(), flops=0, moved=0, limit=24, aliases=None):
+    out_specs = jax.tree.map(lambda _: pl.BlockSpec(memory_space=pltpu.VMEM), out_shapes)
+    for target in (aliases or {}).values():
+        out_specs[target] = pl.BlockSpec(memory_space=H)
     return pl.pallas_call(
         kernel,
         out_shape=out_shapes,
         in_specs=[pl.BlockSpec(memory_space=space) for space in spaces],
-        out_specs=jax.tree.map(lambda _: pl.BlockSpec(memory_space=pltpu.VMEM), out_shapes),
+        out_specs=out_specs,
+        input_output_aliases=aliases or {},
         scratch_shapes=list(scratch),
         compiler_params=pltpu.CompilerParams(vmem_limit_bytes=limit << 20),
         cost_estimate=pl.CostEstimate(flops=flops, bytes_accessed=moved, transcendentals=0),
@@ -282,6 +311,8 @@
 V = pltpu.VMEM
 S = pltpu.SMEM
 H = pltpu.HBM
+FRONT = 58
+SCORE = 52
 
 
 def shards(
@@ -299,42 +330,52 @@
     query = query.reshape(rows, KVH, QROWS, HD)
     chosen = lax.dynamic_index_in_dim(query, span_row[0, 0], 0, keepdims=False)
     asked = lax.ppermute(chosen, "role", swap)
-    weight2 = lax.ppermute(kv_weight, "core", swap)
-    acts2 = lax.ppermute(acts, "core", swap)
-
-    block = struct((KVH, 2 * QROWS, HD), bf16)
-    mine, other = call(
-        cache_kernel,
-        [block, block],
-        [H, H, V, H],
+
+    dma = pltpu.SemaphoreType.DMA
+    words = 2 * (half // HD) * QROWS
+    away = struct((KVH, half + 2 * QROWS + words, HD), bf16)
+    away, value, mine = call(
+        front_kernel,
+        [away, struct((KVH, half, HD), bf16), struct((KVH, 2 * QROWS, HD), bf16)],
+        [H] * 6,
         [
             S(block_owner.shape[1:], jnp.int32),
             S(cache_len.shape, jnp.int32),
+            V(query.shape, bf16),
             V(cache_kv.shape[1:], bf16),
-            pltpu.SemaphoreType.DMA((4,)),
+            V(acts.shape, bf16),
+            V((width, COLS), bf16),
+            dma((7,)),
         ],
-        flops=400_000_000,
-        moved=2_000_000,
-        limit=58,
-    )(block_owner[0], cache_len, query, cache_kv[0])
-    asked, other = lax.optimization_barrier((asked, other))
-    theirs = lax.ppermute(other, "core", swap)
-
-    length = half + 2 * (half // HD) * QROWS + 2 * QROWS
+        flops=1_500_000_000,
+        moved=6_000_000,
+        limit=FRONT,
+    )(block_owner[0], cache_len, query, cache_kv[0], acts, kv_weight)
+    asked, away = lax.optimization_barrier((asked, away))
+    away, own = call(
+        score_kernel,
+        [struct(away.shape, bf16), struct((KVH * QROWS, half), f32)],
+        [V, H, H, H],
+        [
+            V(acts.shape, bf16),
+            V((width, COLS), bf16),
+            V((KVH * QROWS, width), bf16),
+            V((KVH, words, HD), bf16),
+            dma((3,)),
+        ],
+        flops=600_000_000,
+        moved=3_000_000,
+        limit=SCORE,
+        aliases={3: 0},
+    )(asked, acts, kv_weight, away)
+    theirs = lax.ppermute(away, "core", swap)
     sent = call(
-        project_kernel,
-        struct((KVH, length, HD), bf16),
-        [H, H, H, H, V, V, V],
-        [
-            V((2, half, width), bf16),
-            V((2, *kv_weight.shape), bf16),
-            V((2, KVH * QROWS, width), bf16),
-            pltpu.SemaphoreType.DMA((6,)),
-        ],
-        flops=1_700_000_000,
-        moved=8_000_000,
-        limit=50,
-    )(acts, acts2, kv_weight, weight2, asked, mine, theirs)
+        pack_kernel,
+        struct((KVH, half + (half // HD) * QROWS + 2 * QROWS, HD), bf16),
+        [V] * 4,
+        flops=10_000_000,
+        moved=5_000_000,
+    )(theirs, value, own, mine)
     got = lax.all_to_all(sent, "yx", 0, 0, tiled=True)
 
     parts = call(

time: 71.7 us -> 66.5 us (0.927)
  starting transfers between devices: 15.5 us -> 10.7 us
  blocking collectives: 42.8 us -> 40.3 us
  waiting for transfers between devices: 1.18 us -> 3.42 us
  local copies, waits for them, and re-layouts: 1.76 us -> 0.88 us
  Pallas kernels: 9.27 us -> 10.1 us
    ppermute x3 -> x1, starting transfers between devices: 13.5 us -> 6.75 us  [shards(): theirs = lax.ppermute(away, 'core', swap)]
    all_to_all x1, blocking collectives: 26.5 us -> 23.6 us  [shards(): got = lax.all_to_all(sent, 'yx', 0, 0, tiled=True)]
    ppermute x3 -> x1, waiting for transfers between devices: 1.18 us -> 3.41 us  [shards(): theirs = lax.ppermute(away, 'core', swap)]
    ppermute x1, starting transfers between devices: 1.91 us -> 3.94 us  [shards(): asked = lax.ppermute(chosen, 'role', swap)]
    unnamed x8 -> x10, local copies, waits for them, and re-layouts: 0.92 us -> 0.03 us
    pallas_call x2 -> x3, Pallas kernels: 7.85 us -> 8.69 us  [the longest x1 4.79 us: shards(): call(front_kernel, [away, struct((KVH, half, HD), bf16), struct((KVH, 2 *...]
  transfers between devices with their start and end apart: 4 -> 2, of which waited for: 1 -> 1; matrix products, arithmetic and copies ran while one was open for 1% -> 0% of each run, Pallas kernels for 5% -> 7%
where the time goes in v4:
time: 66.5 us; the launch traced here: 66.2 us
  blocking collectives  40.3 us (61%)
  starting transfers between devices  10.7 us (16%)
  Pallas kernels  10.1 us (15%)
  waiting for transfers between devices  3.42 us (5%)
  local copies, waits for them, and re-layouts  0.88 us (1%)
  between operations  0.76 us (1%)
    all_to_all x1, blocking collectives, shards(): got = lax.all_to_all(sent, 'yx', 0, 0, tiled=True)  23.6 us
    all_to_all x1, blocking collectives, shards(): lax.all_to_all(parts.reshape(4 * n_yx, 2 * QROWS, HD), ('role', 'yx', 'co...  16.8 us
    ppermute x1, starting transfers between devices, shards(): theirs = lax.ppermute(away, 'core', swap)  6.75 us
    pallas_call x1, Pallas kernels, shards(): call(front_kernel, [away, struct((KVH, half, HD), bf16), struct((KVH, 2 *...  4.79 us
    ppermute x1, starting transfers between devices, shards(): asked = lax.ppermute(chosen, 'role', swap)  3.94 us
    ppermute x1, waiting for transfers between devices, shards(): theirs = lax.ppermute(away, 'core', swap)  3.41 us
    pallas_call x1, Pallas kernels, shards(): call(score_kernel, [struct(away.shape, bf16), struct((KVH * QROWS, half),...  3.01 us
  transfers between devices with their start and end apart: 2, of which 1 were waited for; matrix products, arithmetic and copies ran while one was open for 0% of the time, Pallas kernels for 7%

profile of v4, /device:TPU:1, one launch (start us, length us, event | category | flops | bytes accessed | tf_op | source)
XLA Modules:
  0.0 66.2 jit_solution(17917611967983955212)
XLA Ops:
  0.7 0.8 %dynamic-slice_bitcast_fusion = bf16[8,32,128]{2,1,0:T(8,128)(2,1)S(1)} fusion(bf16[2,8,32,128]{3,2,1,0:T(8,128)(2,1)} %bitcast.26, s32[]{:T(128)S(6)} %select_n.4), kind=kLoop, calls=%fused_computation | loop fusion | bytes 131076 | tf_op jit(solution)/shard_map/jit(dynamic_index_in_dim)/squeeze | solution.py:331
  1.5 3.9 %collective-permute-start = (bf16[8,32,128]{2,1,0:T(8,128)(2,1)S(1)}, bf16[8,32,128]{2,1,0:T(8,128)(2,1)S(1)}, u32[]{:S(2)}, u32[]{:S(2)}) collective-permute-start(bf16[8,32,128]{2,1,0:T(8,128)(2,1)S(1)} %dynamic-slice_bitcast_fusion), channel_id=1, source_target_pairs={{0,256},{256,0},{1,257},{257,1},{2,258},{258,2},{3,259},{259,3},{4... | collective-permute-start | bytes 196616 | tf_op jit(solution)/shard_map/ppermute | solution.py:332
  5.5 0.0 copy-start
  5.5 4.8 %shard_map.82 = (bf16[8,832,128]{2,1,0:T(8,128)(2,1)}, bf16[8,512,128]{2,1,0:T(8,128)(2,1)}, bf16[8,64,128]{2,1,0:T(8,128)(2,1)}) custom-call(s32[2,16]{1,0:T(2,128)} %bitcast.31, s32[1,2]{1,0:T(1,128)} %len_hbm.1, bf16[2,8,32,128]{3,2,1,0:T(8,128)(2,1)} %bitcast.27, bf16[2,192,2048]{2,1,0:T(8,128)(2,1)} %bitcast.30, bf16[1024,512]{1,0:T(8,128)(2,1)} %bitcast.24, ...), custom_call_target="tpu_custom_call" | custom-call | flops 1500000000 | bytes 6000000 | tf_op jit(solution)/shard_map/pallas_call | solution.py:337
  10.3 0.0 collective-permute-done.q_ref
  10.3 0.0 copy-done
  10.3 0.0 copy-start.1
  10.3 0.0 copy-start.3
  10.3 3.0 %shard_map.83 = (bf16[8,832,128]{2,1,0:T(8,128)(2,1)}, f32[256,512]{1,0:T(8,128)S(1)}) custom-call(bf16[8,32,128]{2,1,0:T(8,128)(2,1)S(1)} %collective-permute-done.q_ref, bf16[1024,512]{1,0:T(8,128)(2,1)S(1)} %bitcast.25, bf16[512,2048]{1,0:T(8,128)(2,1)} %w_hbm.3, bf16[8,832,128]{2,1,0:T(8,128)(2,1)} %get-tuple-element.14._), custom_call_target="tpu_custom_call", output_to_operand_aliasing={{0}: (3, {})} | custom-call | flops 600000000 | bytes 3000000 | tf_op jit(solution)/shard_map/pallas_call | solution.py:355
  13.3 6.8 %collective-permute-start.1 = (bf16[8,832,128]{2,1,0:T(8,128)(2,1)}, bf16[8,832,128]{2,1,0:T(8,128)(2,1)S(1)}, u32[]{:S(2)}, u32[]{:S(2)}) collective-permute-start(bf16[8,832,128]{2,1,0:T(8,128)(2,1)} %get-tuple-element.15), channel_id=1, source_target_pairs={{0,1},{1,0},{2,3},{3,2},{4,5},{5,4},{6,7},{7,6},{8,9},{9,8},{10,11... | collective-permute-start | bytes 5111816 | tf_op jit(solution)/shard_map/ppermute | solution.py:371
  20.1 3.4 %collective-permute-done.1.got_ref = bf16[8,832,128]{2,1,0:T(8,128)(2,1)S(1)} collective-permute-done((bf16[8,832,128]{2,1,0:T(8,128)(2,1)}, bf16[8,832,128]{2,1,0:T(8,128)(2,1)S(1)}, u32[]{:S(2)}, u32[]{:S(2)}) %collective-permute-start.1) | collective-permute-done | bytes 1703968 | tf_op jit(solution)/shard_map/ppermute | solution.py:371
  23.5 0.0 copy-done.1
  23.5 0.0 copy-done.3
  23.5 0.9 %shard_map.84 = bf16[8,704,128]{2,1,0:T(8,128)(2,1)S(1)} custom-call(bf16[8,832,128]{2,1,0:T(8,128)(2,1)S(1)} %collective-permute-done.1.got_ref, bf16[8,512,128]{2,1,0:T(8,128)(2,1)S(1)} %copy-done.1, f32[256,512]{1,0:T(8,128)S(1)} %get-tuple-element.17.own_ref, bf16[8,64,128]{2,1,0:T(8,128)(2,1)S(1)} %copy-done.3), custom_call_target="tpu_custom_call" | custom-call | flops 10000000 | bytes 5000000 | tf_op jit(solution)/shard_map/pallas_call | solution.py:372
  24.4 0.0 copy-start.2
  24.4 0.0 copy-start.4
  24.4 23.6 %all_to_all.10.got_ref = bf16[8,704,128]{2,1,0:T(8,128)(2,1)S(1)} all-to-all(bf16[8,704,128]{2,1,0:T(8,128)(2,1)S(1)} %shard_map.84), channel_id=1, replica_groups=mesh['role'=2,'grp'=16,'yx'=8,'core'=2] {'yx'}, dimensions={0} | all-to-all | bytes 2883584 | tf_op jit(solution)/shard_map/all_to_all | solution.py:379
  48.0 0.0 copy-done.2
  48.0 0.0 copy-done.4
  48.0 0.3 shard_map.85
  48.3 16.8 %all_to_all.11 = bf16[32,64,128]{2,1,0:T(8,128)(2,1)S(1)} all-to-all(bf16[32,64,128]{2,1,0:T(8,128)(2,1)S(1)} %bitcast.23), channel_id=1, replica_groups=mesh['role'=2,'grp'=16,'yx'=8,'core'=2] {'role','yx','core'}, dimensions={0} | all-to-all | bytes 1048576 | tf_op jit(solution)/shard_map/all_to_all | solution.py:388
  65.1 1.1 %shard_map.86 = bf16[2,8,32,128]{3,2,1,0:T(8,128)(2,1)} custom-call(s32[1,1]{1,0:T(1,128)} %copy.13.span_ref, bf16[2,16,64,128]{3,2,1,0:T(8,128)(2,1)S(1)} %bitcast.22), custom_call_target="tpu_custom_call" | custom-call | flops 10000000 | bytes 700000 | tf_op jit(solution)/shard_map/pallas_call | solution.py:391
Async XLA Ops:
  1.5 8.8 %collective-permute-start = (bf16[8,32,128]{2,1,0:T(8,128)(2,1)S(1)}, bf16[8,32,128]{2,1,0:T(8,128)(2,1)S(1)}, u32[]{:S(2)}, u32[]{:S(2)}) collective-permute-start(bf16[8,32,128]{2,1,0:T(8,128)(2,1)S(1)} %dynamic-slice_bitcast_fusion), channel_id=1, source_target_pairs={{0,256},{256,0},{1,257},{257,1},{2,258},{258,2},{3,259},{259,3},{4... | collective-permute-start | bytes 196616 | tf_op jit(solution)/shard_map/ppermute | solution.py:332
  5.5 4.8 %copy-start = (bf16[1,1,1024,512]{3,2,1,0:T(8,128)(2,1)S(1)}, bf16[1,1,1024,512]{3,2,1,0:T(8,128)(2,1)}, u32[]{:S(2)}) copy-start(bf16[1,1,1024,512]{3,2,1,0:T(8,128)(2,1)} %param.8) | copy-start | bytes 3145732
  10.3 13.2 %copy-start.1 = (bf16[8,512,128]{2,1,0:T(8,128)(2,1)S(1)}, bf16[8,512,128]{2,1,0:T(8,128)(2,1)}, u32[]{:S(2)}) copy-start(bf16[8,512,128]{2,1,0:T(8,128)(2,1)} %get-tuple-element.16.value_ref) | copy-start | bytes 3145732
  10.3 13.2 %copy-start.3 = (bf16[8,64,128]{2,1,0:T(8,128)(2,1)S(1)}, bf16[8,64,128]{2,1,0:T(8,128)(2,1)}, u32[]{:S(2)}) copy-start(bf16[8,64,128]{2,1,0:T(8,128)(2,1)} %get-tuple-element.18.mine_ref) | copy-start | bytes 393220
  13.3 10.2 %collective-permute-start.1 = (bf16[8,832,128]{2,1,0:T(8,128)(2,1)}, bf16[8,832,128]{2,1,0:T(8,128)(2,1)S(1)}, u32[]{:S(2)}, u32[]{:S(2)}) collective-permute-start(bf16[8,832,128]{2,1,0:T(8,128)(2,1)} %get-tuple-element.15), channel_id=1, source_target_pairs={{0,1},{1,0},{2,3},{3,2},{4,5},{5,4},{6,7},{7,6},{8,9},{9,8},{10,11... | collective-permute-start | bytes 5111816 | tf_op jit(solution)/shard_map/ppermute | solution.py:371
  24.4 23.6 %copy-start.2 = (bf16[1,2,4,8192]{3,2,1,0:T(4,128)(2,1)S(1)}, bf16[1,2,4,8192]{3,2,1,0:T(4,128)(2,1)}, u32[]{:S(2)}) copy-start(bf16[1,2,4,8192]{3,2,1,0:T(4,128)(2,1)} %param.14) | copy-start | bytes 393220
  24.4 23.6 %copy-start.4 = (bf16[1,2,4,2048]{3,2,1,0:T(4,128)(2,1)S(1)}, bf16[1,2,4,2048]{3,2,1,0:T(4,128)(2,1)}, u32[]{:S(2)}) copy-start(bf16[1,2,4,2048]{3,2,1,0:T(4,128)(2,1)} %param.15) | copy-start | bytes 98308

commit v5 on v4

--- a/solution.py
+++ b/solution.py
@@ -15,6 +15,8 @@
 DRAFT = 4
 GROUP = QH // KVH
 QROWS = GROUP * DRAFT
+STAT = 16
+PAIR = QROWS + STAT
 COLS = KVH * HD
 NEG = -1e30
 SCALE = 1.0 / math.sqrt(HD)
@@ -31,18 +33,30 @@
     return jnp.dot(a, b, preferred_element_type=f32)
 
 
-def packed_stat(lse):
+def terms(lse):
     hi = lse.astype(bf16).astype(f32)
     mid = (lse - hi).astype(bf16).astype(f32)
-    lo = lse - hi - mid
-    lane = lax.broadcasted_iota(jnp.int32, (lse.shape[0], HD), 1)
-    return jnp.where(
-        lane == 0, hi, jnp.where(lane == 1, mid, jnp.where(lane == 2, lo, 0.0))
-    ).astype(bf16)
-
-
-def stat(tile):
-    return jnp.sum(tile.astype(f32), axis=-1, keepdims=True)
+    return hi, mid, lse - hi - mid
+
+
+def packed_stat(lse):
+    lane = lax.broadcasted_iota(jnp.int32, (QROWS, HD), 1)
+    tile = jnp.zeros((QROWS, HD), f32)
+    for at, term in enumerate(terms(lse)):
+        tile = jnp.where(lane == at, term, tile)
+    rows = tile.T[:STAT]
+    return jnp.concatenate([rows, jnp.zeros((STAT, HD - QROWS), f32)], axis=1).astype(bf16)
+
+
+def stat_row(tile):
+    rows = tile.astype(f32)
+    return rows[0:1] + rows[1:2] + rows[2:3]
+
+
+def columns(rows):
+    count = rows.shape[0]
+    square = jnp.concatenate([rows, jnp.zeros((HD - count, HD), f32)], axis=0).T
+    return [square[:QROWS, k : k + 1] for k in range(count)]
 
 
 def attend(score, value):
@@ -55,13 +69,12 @@
     return out, jnp.where(any_key, top + jnp.log(safe), NEG)
 
 
-def merge(parts):
-    top = functools.reduce(jnp.maximum, [lse for _, lse in parts])
-    weights = [jnp.where(lse > 0.5 * NEG, jnp.exp(lse - top), 0.0) for _, lse in parts]
+def shares(rows):
+    top = functools.reduce(jnp.maximum, rows)
+    weights = [jnp.where(row > 0.5 * NEG, jnp.exp(row - top), 0.0) for row in rows]
     total = functools.reduce(jnp.add, weights)
     safe = jnp.where(total > 0.0, total, 1.0)
-    out = functools.reduce(jnp.add, [w * o for w, (o, _) in zip(weights, parts)])
-    return out / safe, jnp.where(total > 0.0, top + jnp.log(safe), NEG)
+    return [w / safe for w in weights], jnp.where(total > 0.0, top + jnp.log(safe), NEG)
 
 
 def stacked(parts):
@@ -73,18 +86,12 @@
 
 
 def put_pair(out_ref, start, out, lse):
-    shape = (KVH, QROWS, HD)
-    out_ref[:, start : start + QROWS] = out.astype(bf16).reshape(shape)
-    out_ref[:, start + QROWS : start + 2 * QROWS] = packed_stat(lse).reshape(shape)
-
-
-def get_pair(ref, start):
-    shape = (KVH * QROWS, HD)
     middle = start + QROWS
-    return (
-        ref[:, start:middle].reshape(shape).astype(f32),
-        stat(ref[:, middle : middle + QROWS].reshape(shape)),
-    )
+    out_ref[:, start:middle] = out.astype(bf16).reshape(KVH, QROWS, HD)
+    for head in range(KVH):
+        out_ref[head, middle : middle + STAT] = packed_stat(
+            lse[head * QROWS : (head + 1) * QROWS]
+        )
 
 
 def front_kernel(
@@ -195,7 +202,7 @@
         for tile in range(tiles):
             at = (part * tiles + tile) * QROWS
             words_ref[:, at : at + QROWS] = words[:, head_cols(tile)].reshape(KVH, QROWS, HD)
-    start = half + 2 * QROWS
+    start = half + PAIR
     store = pltpu.make_async_copy(
         words_ref, away_hbm.at[:, start : start + 2 * tiles * QROWS], sems.at[2]
     )
@@ -209,7 +216,7 @@
     tiles = half // HD
     out_ref[:, :half] = (value_ref[...].astype(f32) + got_ref[:, :half].astype(f32)).astype(bf16)
     shape = (KVH, QROWS, HD)
-    start = half + 2 * QROWS
+    start = half + PAIR
     for tile in range(tiles):
         score = own_ref[:, head_cols(tile)].reshape(shape)
         for part in range(2):
@@ -217,13 +224,28 @@
             score = score + got_ref[:, at : at + QROWS].astype(f32)
         at = half + tile * QROWS
         out_ref[:, at : at + QROWS] = score.astype(bf16)
-    out, lse = merge([get_pair(mine_ref, 0), get_pair(got_ref, half)])
-    put_pair(out_ref, half + tiles * QROWS, out, lse)
+    at = half + tiles * QROWS
+    middle = at + QROWS
+    pair = [
+        [stat_row(ref[head, first : first + STAT]) for head in range(KVH)]
+        for ref, first in ((mine_ref, QROWS), (got_ref, half + QROWS))
+    ]
+    weights, lse = shares([stacked(rows) for rows in pair])
+    weights = columns(stacked(weights))
+    packed = [jnp.concatenate(terms(lse[head : head + 1]), axis=0) for head in range(KVH)]
+    for head in range(KVH):
+        out_ref[head, at:middle] = (
+            weights[head] * mine_ref[head, :QROWS].astype(f32)
+            + weights[KVH + head] * got_ref[head, half : half + QROWS].astype(f32)
+        ).astype(bf16)
+        out_ref[head, middle : middle + STAT] = jnp.concatenate(
+            [packed[head], jnp.zeros((STAT - 3, HD), f32)], axis=0
+        ).astype(bf16)
 
 
 def span_kernel(got_ref, q_ref, draft_ref, out_ref):
     parts, length, _ = got_ref.shape
-    half = (length - 2 * QROWS) * HD // (HD + QROWS)
+    half = (length - PAIR) * HD // (HD + QROWS)
     tiles = half // HD
     role = lax.axis_index("role")
     core = lax.axis_index("core")
@@ -240,16 +262,8 @@
         [total(half + tile * QROWS, QROWS) for tile in range(tiles)], axis=1
     )
     out, lse = attend(score, value)
-    fresh = jnp.concatenate([out.astype(bf16), packed_stat(lse)], axis=0)
-
-    at = half + tiles * QROWS
-    cached = [
-        (
-            got_ref[part, at : at + QROWS].astype(f32),
-            stat(got_ref[part, at + QROWS : at + 2 * QROWS]),
-        )
-        for part in range(parts)
-    ]
+    fresh = stacked([out.astype(bf16), packed_stat(lse)])
+
     query = q_ref[core, head]
     start = pl.multiple_of(head * HD, HD)
     draft_keys = draft_ref[core, :, pl.ds(start, HD)].astype(f32)
@@ -266,8 +280,17 @@
         jnp.add,
         [w.astype(bf16).astype(f32) * draft_vals[u : u + 1] for u, w in enumerate(weights)],
     )
-    out, lse = merge([*cached, (drafted / sums, top + jnp.log(sums))])
-    kept = jnp.concatenate([out.astype(bf16), packed_stat(lse)], axis=0)
+    at = half + tiles * QROWS
+    middle = at + QROWS
+    rows = [stat_row(got_ref[part, middle : middle + STAT]) for part in range(parts)]
+    rows.append(stat_row(packed_stat(top + jnp.log(sums))))
+    weights, lse = shares(rows)
+    weights = columns(stacked(weights))
+    out = weights[parts] * (drafted / sums)
+    for part in range(parts):
+        out = out + weights[part] * got_ref[part, at:middle].astype(f32)
+    spare = jnp.zeros((STAT - 3, HD), f32)
+    kept = stacked([out.astype(bf16), stacked([*terms(lse), spare]).astype(bf16)])
 
     chunks = out_ref.shape[1]
     for chunk in range(chunks):
@@ -277,19 +300,26 @@
 
 def join_kernel(span_ref, got_ref, out_ref):
     role = lax.axis_index("role")
-    for row in range(out_ref.shape[0]):
+    rows = out_ref.shape[0]
+
+    def stats(pool, core):
+        return stacked([stat_row(got_ref[pool, 2 * head + core, QROWS:]) for head in range(KVH)])
+
+    fresh = [stats(1 - role, core) for core in range(2)]
+    weights = []
+    for row in range(rows):
         taken = span_ref[0, 0] == row
+        kept = [jnp.where(taken, lse, NEG) for lse in fresh]
+        weights += shares([stats(role, row), *kept])[0]
+    weights = columns(stacked(weights))
+    for row in range(rows):
         for head in range(KVH):
-
-            def pair(pool, core):
-                tile = got_ref.at[pool, head * 2 + core]
-                return tile[:QROWS].astype(f32), stat(tile[QROWS:])
-
-            parts = [pair(role, row)]
-            for core in range(2):
-                out, lse = pair(1 - role, core)
-                parts.append((out, jnp.where(taken, lse, NEG)))
-            out_ref[row, head] = merge(parts)[0].astype(bf16)
+            sources = [(role, row), (1 - role, 0), (1 - role, 1)]
+            out = jnp.zeros((QROWS, HD), f32)
+            for k, (pool, core) in enumerate(sources):
+                weight = weights[(row * 3 + k) * KVH + head]
+                out = out + weight * got_ref[pool, 2 * head + core, :QROWS].astype(f32)
+            out_ref[row, head] = out.astype(bf16)
 
 
 def call(kernel, out_shapes, spaces, scratch=(), flops=0, moved=0, limit=24, aliases=None):
@@ -328,15 +358,17 @@
 
     query = draft_query[0].reshape(rows, DRAFT, KVH, GROUP, HD).transpose(0, 2, 3, 1, 4)
     query = query.reshape(rows, KVH, QROWS, HD)
-    chosen = lax.dynamic_index_in_dim(query, span_row[0, 0], 0, keepdims=False)
+    chosen = query[0]
+    for row in range(1, rows):
+        chosen = jnp.where(span_row[0] == row, query[row], chosen)
     asked = lax.ppermute(chosen, "role", swap)
 
     dma = pltpu.SemaphoreType.DMA
     words = 2 * (half // HD) * QROWS
-    away = struct((KVH, half + 2 * QROWS + words, HD), bf16)
+    away = struct((KVH, half + PAIR + words, HD), bf16)
     away, value, mine = call(
         front_kernel,
-        [away, struct((KVH, half, HD), bf16), struct((KVH, 2 * QROWS, HD), bf16)],
+        [away, struct((KVH, half, HD), bf16), struct((KVH, PAIR, HD), bf16)],
         [H] * 6,
         [
             S(block_owner.shape[1:], jnp.int32),
@@ -371,7 +403,7 @@
     theirs = lax.ppermute(away, "core", swap)
     sent = call(
         pack_kernel,
-        struct((KVH, half + (half // HD) * QROWS + 2 * QROWS, HD), bf16),
+        struct((KVH, half + (half // HD) * QROWS + PAIR, HD), bf16),
         [V] * 4,
         flops=10_000_000,
         moved=5_000_000,
@@ -380,17 +412,17 @@
 
     parts = call(
         span_kernel,
-        struct((2, 2 * n_yx, 2 * QROWS, HD), bf16),
+        struct((2, 2 * n_yx, PAIR, HD), bf16),
         [V, V, V],
         flops=20_000_000,
         moved=3_000_000,
     )(got, query, draft_kv[0])
     parts = lax.all_to_all(
-        parts.reshape(4 * n_yx, 2 * QROWS, HD), ("role", "yx", "core"), 0, 0, tiled=True
+        parts.reshape(4 * n_yx, PAIR, HD), ("role", "yx", "core"), 0, 0, tiled=True
     )
     joined = call(
         join_kernel, struct((rows, KVH, QROWS, HD), bf16), [S, V], flops=10_000_000, moved=700_000
-    )(span_row, parts.reshape(2, 2 * n_yx, 2 * QROWS, HD))
+    )(span_row, parts.reshape(2, 2 * n_yx, PAIR, HD))
     output = joined.reshape(rows, KVH, GROUP, DRAFT, HD).transpose(0, 3, 1, 2, 4)
     return output.reshape(1, rows, DRAFT, QH * HD)
 

time: 66.5 us -> 65.3 us (0.982)
  blocking collectives: 40.3 us -> 38.7 us
  other arithmetic: 0 us -> 0.91 us
  local copies, waits for them, and re-layouts: 0.88 us -> 0.03 us
    all_to_all x1, blocking collectives: 16.8 us -> 15.7 us  [shards(): lax.all_to_all(parts.reshape(4 * n_yx, PAIR, HD), ('role', 'yx', 'core'),...]
    select_n x0 -> x1, other arithmetic: none -> 0.91 us  [shards(): chosen = jnp.where(span_row[0] == row, query[row], chosen)]
    squeeze x1 -> x0, local copies, waits for them, and re-layouts: 0.85 us -> none  [shards(): chosen = lax.dynamic_index_in_dim(query, span_row[0, 0], 0, keepdims=False)]
where the time goes in v5:
time: 65.3 us; the launch traced here: 65 us
  blocking collectives  38.7 us (59%)
  starting transfers between devices  10.7 us (16%)
  Pallas kernels  10.5 us (16%)
  waiting for transfers between devices  3.37 us (5%)
  other arithmetic  0.91 us (1%)
  between operations  0.76 us (1%)
    all_to_all x1, blocking collectives, shards(): got = lax.all_to_all(sent, 'yx', 0, 0, tiled=True)  23 us
    all_to_all x1, blocking collectives, shards(): lax.all_to_all(parts.reshape(4 * n_yx, PAIR, HD), ('role', 'yx', 'core'),...  15.7 us
    ppermute x1, starting transfers between devices, shards(): theirs = lax.ppermute(away, 'core', swap)  6.76 us
    pallas_call x1, Pallas kernels, shards(): call(front_kernel, [away, struct((KVH, half, HD), bf16), struct((KVH, PAI...  4.87 us
    ppermute x1, starting transfers between devices, shards(): asked = lax.ppermute(chosen, 'role', swap)  3.95 us
    ppermute x1, waiting for transfers between devices, shards(): theirs = lax.ppermute(away, 'core', swap)  3.37 us
    pallas_call x1, Pallas kernels, shards(): call(score_kernel, [struct(away.shape, bf16), struct((KVH * QROWS, half),...  2.98 us
  transfers between devices with their start and end apart: 2, of which 1 were waited for; matrix products, arithmetic and copies ran while one was open for 0% of the time, Pallas kernels for 7%

profile of v5, /device:TPU:1, one launch (start us, length us, event | category | flops | bytes accessed | tf_op | source)
XLA Modules:
  0.0 65.0 jit_solution(6451096470691107448)
XLA Ops:
  0.7 0.9 %slice_select_fusion = bf16[1,8,8,4,128]{4,3,2,1,0:T(4,128)(2,1)S(1)} fusion(bf16[2,8,8,4,128]{4,3,2,1,0:T(4,128)(2,1)} %bitcast.22, pred[]{:T(512)} %bitcast), kind=kLoop, calls=%fused_computation | loop fusion | flops 32768 | bytes 196609 | tf_op jit(solution)/shard_map/jit(_where)/select_n | solution.py:363
  1.6 3.9 %collective-permute-start = (bf16[8,32,128]{2,1,0:T(8,128)(2,1)S(1)}, bf16[8,32,128]{2,1,0:T(8,128)(2,1)S(1)}, u32[]{:S(2)}, u32[]{:S(2)}) collective-permute-start(bf16[8,32,128]{2,1,0:T(8,128)(2,1)S(1)} %bitcast.26), channel_id=1, source_target_pairs={{0,256},{256,0},{1,257},{257,1},{2,258},{258,2},{3,259},{259,3},{4... | collective-permute-start | bytes 196616 | tf_op jit(solution)/shard_map/ppermute | solution.py:364
  5.5 0.0 copy-start
  5.5 4.9 %shard_map.82 = (bf16[8,816,128]{2,1,0:T(8,128)(2,1)}, bf16[8,512,128]{2,1,0:T(8,128)(2,1)}, bf16[8,48,128]{2,1,0:T(8,128)(2,1)}) custom-call(s32[2,16]{1,0:T(2,128)} %bitcast.28, s32[1,2]{1,0:T(1,128)} %len_hbm.1, bf16[2,8,32,128]{3,2,1,0:T(8,128)(2,1)} %bitcast.23, bf16[2,192,2048]{2,1,0:T(8,128)(2,1)} %bitcast.27, bf16[1024,512]{1,0:T(8,128)(2,1)} %bitcast.20, ...), custom_call_target="tpu_custom_call" | custom-call | flops 1500000000 | bytes 6000000 | tf_op jit(solution)/shard_map/pallas_call | solution.py:369
  10.4 0.0 collective-permute-done.q_ref
  10.4 0.0 copy-done
  10.4 0.0 copy-start.1
  10.4 0.0 copy-start.3
  10.5 3.0 %shard_map.83 = (bf16[8,816,128]{2,1,0:T(8,128)(2,1)}, f32[256,512]{1,0:T(8,128)S(1)}) custom-call(bf16[8,32,128]{2,1,0:T(8,128)(2,1)S(1)} %collective-permute-done.q_ref, bf16[1024,512]{1,0:T(8,128)(2,1)S(1)} %bitcast.21, bf16[512,2048]{1,0:T(8,128)(2,1)} %w_hbm.3, bf16[8,816,128]{2,1,0:T(8,128)(2,1)} %get-tuple-element.14._), custom_call_target="tpu_custom_call", output_to_operand_aliasing={{0}: (3, {})} | custom-call | flops 600000000 | bytes 3000000 | tf_op jit(solution)/shard_map/pallas_call | solution.py:387
  13.4 6.8 %collective-permute-start.1 = (bf16[8,816,128]{2,1,0:T(8,128)(2,1)}, bf16[8,816,128]{2,1,0:T(8,128)(2,1)S(1)}, u32[]{:S(2)}, u32[]{:S(2)}) collective-permute-start(bf16[8,816,128]{2,1,0:T(8,128)(2,1)} %get-tuple-element.15), channel_id=1, source_target_pairs={{0,1},{1,0},{2,3},{3,2},{4,5},{5,4},{6,7},{7,6},{8,9},{9,8},{10,11... | collective-permute-start | bytes 5013512 | tf_op jit(solution)/shard_map/ppermute | solution.py:403
  20.2 3.4 %collective-permute-done.1.got_ref = bf16[8,816,128]{2,1,0:T(8,128)(2,1)S(1)} collective-permute-done((bf16[8,816,128]{2,1,0:T(8,128)(2,1)}, bf16[8,816,128]{2,1,0:T(8,128)(2,1)S(1)}, u32[]{:S(2)}, u32[]{:S(2)}) %collective-permute-start.1) | collective-permute-done | bytes 1671200 | tf_op jit(solution)/shard_map/ppermute | solution.py:403
  23.6 0.0 copy-done.1
  23.6 0.0 copy-done.3
  23.6 0.9 %shard_map.84 = bf16[8,688,128]{2,1,0:T(8,128)(2,1)S(1)} custom-call(bf16[8,816,128]{2,1,0:T(8,128)(2,1)S(1)} %collective-permute-done.1.got_ref, bf16[8,512,128]{2,1,0:T(8,128)(2,1)S(1)} %copy-done.1, f32[256,512]{1,0:T(8,128)S(1)} %get-tuple-element.17.own_ref, bf16[8,48,128]{2,1,0:T(8,128)(2,1)S(1)} %copy-done.3), custom_call_target="tpu_custom_call" | custom-call | flops 10000000 | bytes 5000000 | tf_op jit(solution)/shard_map/pallas_call | solution.py:404
  24.5 0.0 copy-start.2
  24.5 0.0 copy-start.4
  24.5 23.0 %all_to_all.10.got_ref = bf16[8,688,128]{2,1,0:T(8,128)(2,1)S(1)} all-to-all(bf16[8,688,128]{2,1,0:T(8,128)(2,1)S(1)} %shard_map.84), channel_id=1, replica_groups=mesh['role'=2,'grp'=16,'yx'=8,'core'=2] {'yx'}, dimensions={0} | all-to-all | bytes 2818048 | tf_op jit(solution)/shard_map/all_to_all | solution.py:411
  47.5 0.0 copy-done.2
  47.5 0.0 copy-done.4
  47.5 0.6 shard_map.85
  48.1 15.7 %all_to_all.11 = bf16[32,48,128]{2,1,0:T(8,128)(2,1)S(1)} all-to-all(bf16[32,48,128]{2,1,0:T(8,128)(2,1)S(1)} %bitcast.19), channel_id=1, replica_groups=mesh['role'=2,'grp'=16,'yx'=8,'core'=2] {'role','yx','core'}, dimensions={0} | all-to-all | bytes 786432 | tf_op jit(solution)/shard_map/all_to_all | solution.py:420
  63.8 1.1 %shard_map.86 = bf16[2,8,32,128]{3,2,1,0:T(8,128)(2,1)} custom-call(s32[1,1]{1,0:T(1,128)S(6)} %copy.13.span_ref, bf16[2,16,48,128]{3,2,1,0:T(8,128)(2,1)S(1)} %bitcast.18), custom_call_target="tpu_custom_call" | custom-call | flops 10000000 | bytes 700000 | tf_op jit(solution)/shard_map/pallas_call | solution.py:423
Async XLA Ops:
  1.6 8.8 %collective-permute-start = (bf16[8,32,128]{2,1,0:T(8,128)(2,1)S(1)}, bf16[8,32,128]{2,1,0:T(8,128)(2,1)S(1)}, u32[]{:S(2)}, u32[]{:S(2)}) collective-permute-start(bf16[8,32,128]{2,1,0:T(8,128)(2,1)S(1)} %bitcast.26), channel_id=1, source_target_pairs={{0,256},{256,0},{1,257},{257,1},{2,258},{258,2},{3,259},{259,3},{4... | collective-permute-start | bytes 196616 | tf_op jit(solution)/shard_map/ppermute | solution.py:364
  5.5 4.9 %copy-start = (bf16[1,1,1024,512]{3,2,1,0:T(8,128)(2,1)S(1)}, bf16[1,1,1024,512]{3,2,1,0:T(8,128)(2,1)}, u32[]{:S(2)}) copy-start(bf16[1,1,1024,512]{3,2,1,0:T(8,128)(2,1)} %param.8) | copy-start | bytes 3145732
  10.4 13.1 %copy-start.1 = (bf16[8,512,128]{2,1,0:T(8,128)(2,1)S(1)}, bf16[8,512,128]{2,1,0:T(8,128)(2,1)}, u32[]{:S(2)}) copy-start(bf16[8,512,128]{2,1,0:T(8,128)(2,1)} %get-tuple-element.16.value_ref) | copy-start | bytes 3145732
  10.4 13.1 %copy-start.3 = (bf16[8,48,128]{2,1,0:T(8,128)(2,1)S(1)}, bf16[8,48,128]{2,1,0:T(8,128)(2,1)}, u32[]{:S(2)}) copy-start(bf16[8,48,128]{2,1,0:T(8,128)(2,1)} %get-tuple-element.18.mine_ref) | copy-start | bytes 294916
  13.4 10.1 %collective-permute-start.1 = (bf16[8,816,128]{2,1,0:T(8,128)(2,1)}, bf16[8,816,128]{2,1,0:T(8,128)(2,1)S(1)}, u32[]{:S(2)}, u32[]{:S(2)}) collective-permute-start(bf16[8,816,128]{2,1,0:T(8,128)(2,1)} %get-tuple-element.15), channel_id=1, source_target_pairs={{0,1},{1,0},{2,3},{3,2},{4,5},{5,4},{6,7},{7,6},{8,9},{9,8},{10,11... | collective-permute-start | bytes 5013512 | tf_op jit(solution)/shard_map/ppermute | solution.py:403
  24.5 23.0 %copy-start.2 = (bf16[1,2,4,8192]{3,2,1,0:T(4,128)(2,1)S(1)}, bf16[1,2,4,8192]{3,2,1,0:T(4,128)(2,1)}, u32[]{:S(2)}) copy-start(bf16[1,2,4,8192]{3,2,1,0:T(4,128)(2,1)} %param.14) | copy-start | bytes 393220
  24.5 23.0 %copy-start.4 = (bf16[1,2,4,2048]{3,2,1,0:T(4,128)(2,1)S(1)}, bf16[1,2,4,2048]{3,2,1,0:T(4,128)(2,1)}, u32[]{:S(2)}) copy-start(bf16[1,2,4,2048]{3,2,1,0:T(4,128)(2,1)} %param.15) | copy-start | bytes 98308

commit v6 on v5

--- a/solution.py
+++ b/solution.py
@@ -174,41 +174,38 @@
             out_ref[head, :half] = value[:, head_cols(head)]
 
 
-def score_kernel(
-    q_ref, acts_hbm, w_hbm, _, away_hbm, own_ref, acts_ref, w_ref, qw_ref, words_ref, sems
-):
+def score_kernel(q_ref, acts_ref, w_hbm, _, away_hbm, qw_ref, w_ref, words_ref, sems):
     core = lax.axis_index("core")
     half = acts_ref.shape[0] // 2
+    middle = COLS // 2
     loads = [
-        pltpu.make_async_copy(w_hbm.at[:, 0:COLS], w_ref, sems.at[0]),
-        pltpu.make_async_copy(acts_hbm, acts_ref, sems.at[1]),
+        pltpu.make_async_copy(w_hbm.at[:, cols], w_ref.at[:, cols], sems.at[k])
+        for k, cols in enumerate((slice(0, middle), slice(middle, COLS)))
     ]
     for copy in loads:
         copy.start()
-    loads[0].wait()
     for head in range(KVH):
+        if head * HD % middle == 0:
+            loads[head * HD // middle].wait()
         rows = slice(head * QROWS, (head + 1) * QROWS)
         qw_ref[rows] = dot_nt(q_ref[head], w_ref[:, head_cols(head)]).astype(bf16)
-    loads[1].wait()
+    start = pl.multiple_of((1 - core) * half, half)
+    score = (dot_nt(qw_ref[...], acts_ref[pl.ds(start, half), :]) * SCALE).astype(bf16)
     tiles = half // HD
-
-    def tokens(row):
-        return acts_ref[pl.ds(pl.multiple_of(row * half, half), half), :]
-
-    score = dot_nt(qw_ref[...], tokens(1 - core)) * SCALE
-    high = score.astype(bf16)
-    low = (score - high.astype(f32)).astype(bf16)
-    for part, words in enumerate((high, low)):
-        for tile in range(tiles):
-            at = (part * tiles + tile) * QROWS
-            words_ref[:, at : at + QROWS] = words[:, head_cols(tile)].reshape(KVH, QROWS, HD)
-    start = half + PAIR
+    for tile in range(tiles):
+        at = tile * QROWS
+        words_ref[:, at : at + QROWS] = score[:, head_cols(tile)].reshape(KVH, QROWS, HD)
     store = pltpu.make_async_copy(
-        words_ref, away_hbm.at[:, start : start + 2 * tiles * QROWS], sems.at[2]
+        words_ref, away_hbm.at[:, half + PAIR : half + PAIR + tiles * QROWS], sems.at[2]
     )
     store.start()
-    own_ref[...] = dot_nt(qw_ref[...], tokens(core)) * SCALE
     store.wait()
+
+
+def own_kernel(qw_ref, acts_ref, own_ref):
+    half = acts_ref.shape[0] // 2
+    start = pl.multiple_of(lax.axis_index("core") * half, half)
+    own_ref[...] = dot_nt(qw_ref[...], acts_ref[pl.ds(start, half), :]) * SCALE
 
 
 def pack_kernel(got_ref, value_ref, own_ref, mine_ref, out_ref):
@@ -219,9 +216,8 @@
     start = half + PAIR
     for tile in range(tiles):
         score = own_ref[:, head_cols(tile)].reshape(shape)
-        for part in range(2):
-            at = start + (part * tiles + tile) * QROWS
-            score = score + got_ref[:, at : at + QROWS].astype(f32)
+        at = start + tile * QROWS
+        score = score + got_ref[:, at : at + QROWS].astype(f32)
         at = half + tile * QROWS
         out_ref[:, at : at + QROWS] = score.astype(bf16)
     at = half + tiles * QROWS
@@ -364,7 +360,7 @@
     asked = lax.ppermute(chosen, "role", swap)
 
     dma = pltpu.SemaphoreType.DMA
-    words = 2 * (half // HD) * QROWS
+    words = (half // HD) * QROWS
     away = struct((KVH, half + PAIR + words, HD), bf16)
     away, value, mine = call(
         front_kernel,
@@ -384,23 +380,24 @@
         limit=FRONT,
     )(block_owner[0], cache_len, query, cache_kv[0], acts, kv_weight)
     asked, away = lax.optimization_barrier((asked, away))
-    away, own = call(
+    away, absorbed = call(
         score_kernel,
-        [struct(away.shape, bf16), struct((KVH * QROWS, half), f32)],
-        [V, H, H, H],
-        [
-            V(acts.shape, bf16),
-            V((width, COLS), bf16),
-            V((KVH * QROWS, width), bf16),
-            V((KVH, words, HD), bf16),
-            dma((3,)),
-        ],
-        flops=600_000_000,
+        [struct(away.shape, bf16), struct((KVH * QROWS, width), bf16)],
+        [V, V, H, H],
+        [V((width, COLS), bf16), V((KVH, words, HD), bf16), dma((3,))],
+        flops=300_000_000,
         moved=3_000_000,
         limit=SCORE,
         aliases={3: 0},
     )(asked, acts, kv_weight, away)
     theirs = lax.ppermute(away, "core", swap)
+    own = call(
+        own_kernel,
+        struct((KVH * QROWS, half), f32),
+        [V, V],
+        flops=140_000_000,
+        moved=2_000_000,
+    )(absorbed, acts)
     sent = call(
         pack_kernel,
         struct((KVH, half + (half // HD) * QROWS + PAIR, HD), bf16),

time: 65.3 us -> 64.6 us (0.989)
  waiting for transfers between devices: 3.37 us -> 2.64 us
    ppermute x1, waiting for transfers between devices: 3.37 us -> 2.64 us  [shards(): theirs = lax.ppermute(away, 'core', swap)]
    pallas_call x1 -> x2, Pallas kernels: 2.98 us -> 2.95 us  [the longest x1 2.61 us: shards(): call(score_kernel, [struct(away.shape, bf16), struct((KVH * QROWS, width)...]
  transfers between devices with their start and end apart: 2 -> 2, of which waited for: 1 -> 1; matrix products, arithmetic and copies ran while one was open for 0% -> 0% of each run, Pallas kernels for 7% -> 8%
where the time goes in v6:
time: 64.6 us; the launch traced here: 64.3 us
  blocking collectives  38.7 us (60%)
  starting transfers between devices  10.8 us (17%)
  Pallas kernels  10.4 us (16%)
  waiting for transfers between devices  2.64 us (4%)
  other arithmetic  0.91 us (1%)
  between operations  0.77 us (1%)
    all_to_all x1, blocking collectives, shards(): got = lax.all_to_all(sent, 'yx', 0, 0, tiled=True)  23 us
    all_to_all x1, blocking collectives, shards(): lax.all_to_all(parts.reshape(4 * n_yx, PAIR, HD), ('role', 'yx', 'core'),...  15.7 us
    ppermute x1, starting transfers between devices, shards(): theirs = lax.ppermute(away, 'core', swap)  6.89 us
    pallas_call x1, Pallas kernels, shards(): call(front_kernel, [away, struct((KVH, half, HD), bf16), struct((KVH, PAI...  4.86 us
    ppermute x1, starting transfers between devices, shards(): asked = lax.ppermute(chosen, 'role', swap)  3.95 us
    ppermute x1, waiting for transfers between devices, shards(): theirs = lax.ppermute(away, 'core', swap)  2.64 us
    pallas_call x1, Pallas kernels, shards(): call(score_kernel, [struct(away.shape, bf16), struct((KVH * QROWS, width)...  2.61 us
  transfers between devices with their start and end apart: 2, of which 1 were waited for; matrix products, arithmetic and copies ran while one was open for 0% of the time, Pallas kernels for 8%

profile of v6, /device:TPU:1, one launch (start us, length us, event | category | flops | bytes accessed | tf_op | source)
XLA Modules:
  0.0 64.3 jit_solution(15752380342575253432)
XLA Ops:
  0.7 0.9 %slice_select_fusion = bf16[1,8,8,4,128]{4,3,2,1,0:T(4,128)(2,1)S(1)} fusion(bf16[2,8,8,4,128]{4,3,2,1,0:T(4,128)(2,1)} %bitcast.23, pred[]{:T(512)} %bitcast), kind=kLoop, calls=%fused_computation | loop fusion | flops 32768 | bytes 196609 | tf_op jit(solution)/shard_map/jit(_where)/select_n | solution.py:359
  1.6 3.9 %collective-permute-start = (bf16[8,32,128]{2,1,0:T(8,128)(2,1)S(1)}, bf16[8,32,128]{2,1,0:T(8,128)(2,1)S(1)}, u32[]{:S(2)}, u32[]{:S(2)}) collective-permute-start(bf16[8,32,128]{2,1,0:T(8,128)(2,1)S(1)} %bitcast.27), channel_id=1, source_target_pairs={{0,256},{256,0},{1,257},{257,1},{2,258},{258,2},{3,259},{259,3},{4... | collective-permute-start | bytes 196616 | tf_op jit(solution)/shard_map/ppermute | solution.py:360
  5.5 0.0 copy-start
  5.5 4.9 %shard_map.82 = (bf16[8,688,128]{2,1,0:T(8,128)(2,1)}, bf16[8,512,128]{2,1,0:T(8,128)(2,1)}, bf16[8,48,128]{2,1,0:T(8,128)(2,1)}) custom-call(s32[2,16]{1,0:T(2,128)} %bitcast.29, s32[1,2]{1,0:T(1,128)} %len_hbm.1, bf16[2,8,32,128]{3,2,1,0:T(8,128)(2,1)} %bitcast.24, bf16[2,192,2048]{2,1,0:T(8,128)(2,1)} %bitcast.28, bf16[1024,512]{1,0:T(8,128)(2,1)} %bitcast.18, ...), custom_call_target="tpu_custom_call" | custom-call | flops 1500000000 | bytes 6000000 | tf_op jit(solution)/shard_map/pallas_call | solution.py:365
  10.4 0.0 collective-permute-done.q_ref
  10.4 0.0 copy-done
  10.4 2.6 %shard_map.83 = (bf16[8,688,128]{2,1,0:T(8,128)(2,1)}, bf16[256,512]{1,0:T(8,128)(2,1)S(1)}) custom-call(bf16[8,32,128]{2,1,0:T(8,128)(2,1)S(1)} %collective-permute-done.q_ref, bf16[1024,512]{1,0:T(8,128)(2,1)S(1)} %bitcast.19, bf16[512,2048]{1,0:T(8,128)(2,1)} %w_hbm.3, bf16[8,688,128]{2,1,0:T(8,128)(2,1)} %get-tuple-element.14._), custom_call_target="tpu_custom_call", output_to_operand_aliasing={{0}: (3, {})} | custom-call | flops 300000000 | bytes 3000000 | tf_op jit(solution)/shard_map/pallas_call | solution.py:383
  13.1 0.0 copy-start.1
  13.1 0.0 copy-start.3
  13.1 6.9 %collective-permute-start.1 = (bf16[8,688,128]{2,1,0:T(8,128)(2,1)}, bf16[8,688,128]{2,1,0:T(8,128)(2,1)S(1)}, u32[]{:S(2)}, u32[]{:S(2)}) collective-permute-start(bf16[8,688,128]{2,1,0:T(8,128)(2,1)} %get-tuple-element.15), channel_id=1, source_target_pairs={{0,1},{1,0},{2,3},{3,2},{4,5},{5,4},{6,7},{7,6},{8,9},{9,8},{10,11... | collective-permute-start | bytes 4227080 | tf_op jit(solution)/shard_map/ppermute | solution.py:393
  20.0 0.3 shard_map.84.own_ref
  20.3 2.6 %collective-permute-done.1.got_ref = bf16[8,688,128]{2,1,0:T(8,128)(2,1)S(1)} collective-permute-done((bf16[8,688,128]{2,1,0:T(8,128)(2,1)}, bf16[8,688,128]{2,1,0:T(8,128)(2,1)S(1)}, u32[]{:S(2)}, u32[]{:S(2)}) %collective-permute-start.1) | collective-permute-done | bytes 1409056 | tf_op jit(solution)/shard_map/ppermute | solution.py:393
  23.0 0.0 copy-done.1
  23.0 0.0 copy-done.3
  23.0 0.9 %shard_map.85 = bf16[8,688,128]{2,1,0:T(8,128)(2,1)S(1)} custom-call(bf16[8,688,128]{2,1,0:T(8,128)(2,1)S(1)} %collective-permute-done.1.got_ref, bf16[8,512,128]{2,1,0:T(8,128)(2,1)S(1)} %copy-done.1, f32[256,512]{1,0:T(8,128)S(1)} %shard_map.84.own_ref, bf16[8,48,128]{2,1,0:T(8,128)(2,1)S(1)} %copy-done.3), custom_call_target="tpu_custom_call" | custom-call | flops 10000000 | bytes 5000000 | tf_op jit(solution)/shard_map/pallas_call | solution.py:401
  23.8 0.0 copy-start.2
  23.8 0.0 copy-start.4
  23.9 23.0 %all_to_all.10.got_ref = bf16[8,688,128]{2,1,0:T(8,128)(2,1)S(1)} all-to-all(bf16[8,688,128]{2,1,0:T(8,128)(2,1)S(1)} %shard_map.85), channel_id=1, replica_groups=mesh['role'=2,'grp'=16,'yx'=8,'core'=2] {'yx'}, dimensions={0} | all-to-all | bytes 2818048 | tf_op jit(solution)/shard_map/all_to_all | solution.py:408
  46.8 0.0 copy-done.2
  46.8 0.0 copy-done.4
  46.8 0.6 shard_map.86
  47.4 15.7 %all_to_all.11 = bf16[32,48,128]{2,1,0:T(8,128)(2,1)S(1)} all-to-all(bf16[32,48,128]{2,1,0:T(8,128)(2,1)S(1)} %bitcast.22), channel_id=1, replica_groups=mesh['role'=2,'grp'=16,'yx'=8,'core'=2] {'role','yx','core'}, dimensions={0} | all-to-all | bytes 786432 | tf_op jit(solution)/shard_map/all_to_all | solution.py:417
  63.2 1.1 %shard_map.87 = bf16[2,8,32,128]{3,2,1,0:T(8,128)(2,1)} custom-call(s32[1,1]{1,0:T(1,128)S(6)} %copy.13.span_ref, bf16[2,16,48,128]{3,2,1,0:T(8,128)(2,1)S(1)} %bitcast.21), custom_call_target="tpu_custom_call" | custom-call | flops 10000000 | bytes 700000 | tf_op jit(solution)/shard_map/pallas_call | solution.py:420
Async XLA Ops:
  1.6 8.8 %collective-permute-start = (bf16[8,32,128]{2,1,0:T(8,128)(2,1)S(1)}, bf16[8,32,128]{2,1,0:T(8,128)(2,1)S(1)}, u32[]{:S(2)}, u32[]{:S(2)}) collective-permute-start(bf16[8,32,128]{2,1,0:T(8,128)(2,1)S(1)} %bitcast.27), channel_id=1, source_target_pairs={{0,256},{256,0},{1,257},{257,1},{2,258},{258,2},{3,259},{259,3},{4... | collective-permute-start | bytes 196616 | tf_op jit(solution)/shard_map/ppermute | solution.py:360
  5.5 4.9 %copy-start = (bf16[1,1,1024,512]{3,2,1,0:T(8,128)(2,1)S(1)}, bf16[1,1,1024,512]{3,2,1,0:T(8,128)(2,1)}, u32[]{:S(2)}) copy-start(bf16[1,1,1024,512]{3,2,1,0:T(8,128)(2,1)} %param.8) | copy-start | bytes 3145732
  13.1 9.9 %copy-start.1 = (bf16[8,512,128]{2,1,0:T(8,128)(2,1)S(1)}, bf16[8,512,128]{2,1,0:T(8,128)(2,1)}, u32[]{:S(2)}) copy-start(bf16[8,512,128]{2,1,0:T(8,128)(2,1)} %get-tuple-element.16.value_ref) | copy-start | bytes 3145732
  13.1 9.9 %copy-start.3 = (bf16[8,48,128]{2,1,0:T(8,128)(2,1)S(1)}, bf16[8,48,128]{2,1,0:T(8,128)(2,1)}, u32[]{:S(2)}) copy-start(bf16[8,48,128]{2,1,0:T(8,128)(2,1)} %get-tuple-element.18.mine_ref) | copy-start | bytes 294916
  13.1 9.9 %collective-permute-start.1 = (bf16[8,688,128]{2,1,0:T(8,128)(2,1)}, bf16[8,688,128]{2,1,0:T(8,128)(2,1)S(1)}, u32[]{:S(2)}, u32[]{:S(2)}) collective-permute-start(bf16[8,688,128]{2,1,0:T(8,128)(2,1)} %get-tuple-element.15), channel_id=1, source_target_pairs={{0,1},{1,0},{2,3},{3,2},{4,5},{5,4},{6,7},{7,6},{8,9},{9,8},{10,11... | collective-permute-start | bytes 4227080 | tf_op jit(solution)/shard_map/ppermute | solution.py:393
  23.8 23.0 %copy-start.2 = (bf16[1,2,4,8192]{3,2,1,0:T(4,128)(2,1)S(1)}, bf16[1,2,4,8192]{3,2,1,0:T(4,128)(2,1)}, u32[]{:S(2)}) copy-start(bf16[1,2,4,8192]{3,2,1,0:T(4,128)(2,1)} %param.14) | copy-start | bytes 393220
  23.8 23.0 %copy-start.4 = (bf16[1,2,4,2048]{3,2,1,0:T(4,128)(2,1)S(1)}, bf16[1,2,4,2048]{3,2,1,0:T(4,128)(2,1)}, u32[]{:S(2)}) copy-start(bf16[1,2,4,2048]{3,2,1,0:T(4,128)(2,1)} %param.15) | copy-start | bytes 98308

commit v7 on v6

--- a/solution.py
+++ b/solution.py
@@ -174,32 +174,31 @@
             out_ref[head, :half] = value[:, head_cols(head)]
 
 
-def score_kernel(q_ref, acts_ref, w_hbm, _, away_hbm, qw_ref, w_ref, words_ref, sems):
-    core = lax.axis_index("core")
-    half = acts_ref.shape[0] // 2
+def absorb_kernel(span_ref, q_hbm, w_hbm, out_ref, q_ref, w_ref, sems):
     middle = COLS // 2
+    row = span_ref[0, 0]
+    first = pltpu.make_async_copy(q_hbm.at[row], q_ref, sems.at[2])
     loads = [
         pltpu.make_async_copy(w_hbm.at[:, cols], w_ref.at[:, cols], sems.at[k])
         for k, cols in enumerate((slice(0, middle), slice(middle, COLS)))
     ]
-    for copy in loads:
+    for copy in (first, *loads):
         copy.start()
+    first.wait()
     for head in range(KVH):
         if head * HD % middle == 0:
             loads[head * HD // middle].wait()
         rows = slice(head * QROWS, (head + 1) * QROWS)
-        qw_ref[rows] = dot_nt(q_ref[head], w_ref[:, head_cols(head)]).astype(bf16)
-    start = pl.multiple_of((1 - core) * half, half)
+        out_ref[rows] = dot_nt(q_ref[head], w_ref[:, head_cols(head)]).astype(bf16)
+
+
+def other_kernel(qw_ref, acts_ref, out_ref):
+    half = acts_ref.shape[0] // 2
+    start = pl.multiple_of((1 - lax.axis_index("core")) * half, half)
     score = (dot_nt(qw_ref[...], acts_ref[pl.ds(start, half), :]) * SCALE).astype(bf16)
-    tiles = half // HD
-    for tile in range(tiles):
+    for tile in range(half // HD):
         at = tile * QROWS
-        words_ref[:, at : at + QROWS] = score[:, head_cols(tile)].reshape(KVH, QROWS, HD)
-    store = pltpu.make_async_copy(
-        words_ref, away_hbm.at[:, half + PAIR : half + PAIR + tiles * QROWS], sems.at[2]
-    )
-    store.start()
-    store.wait()
+        out_ref[:, at : at + QROWS] = score[:, head_cols(tile)].reshape(KVH, QROWS, HD)
 
 
 def own_kernel(qw_ref, acts_ref, own_ref):
@@ -208,17 +207,16 @@
     own_ref[...] = dot_nt(qw_ref[...], acts_ref[pl.ds(start, half), :]) * SCALE
 
 
-def pack_kernel(got_ref, value_ref, own_ref, mine_ref, out_ref):
+def pack_kernel(got_ref, score_ref, value_ref, own_ref, mine_ref, out_ref):
     half = value_ref.shape[1]
     tiles = half // HD
     out_ref[:, :half] = (value_ref[...].astype(f32) + got_ref[:, :half].astype(f32)).astype(bf16)
     shape = (KVH, QROWS, HD)
-    start = half + PAIR
     for tile in range(tiles):
+        at = tile * QROWS
         score = own_ref[:, head_cols(tile)].reshape(shape)
-        at = start + tile * QROWS
-        score = score + got_ref[:, at : at + QROWS].astype(f32)
-        at = half + tile * QROWS
+        score = score + score_ref[:, at : at + QROWS].astype(f32)
+        at = half + at
         out_ref[:, at : at + QROWS] = score.astype(bf16)
     at = half + tiles * QROWS
     middle = at + QROWS
@@ -338,7 +336,6 @@
 S = pltpu.SMEM
 H = pltpu.HBM
 FRONT = 58
-SCORE = 52
 
 
 def shards(
@@ -354,14 +351,21 @@
 
     query = draft_query[0].reshape(rows, DRAFT, KVH, GROUP, HD).transpose(0, 2, 3, 1, 4)
     query = query.reshape(rows, KVH, QROWS, HD)
-    chosen = query[0]
-    for row in range(1, rows):
-        chosen = jnp.where(span_row[0] == row, query[row], chosen)
-    asked = lax.ppermute(chosen, "role", swap)
-
     dma = pltpu.SemaphoreType.DMA
+    absorbed = call(
+        absorb_kernel,
+        struct((KVH * QROWS, width), bf16),
+        [S, H, H],
+        [V(query.shape[1:], bf16), V((width, COLS), bf16), dma((3,))],
+        flops=70_000_000,
+        moved=1_500_000,
+        limit=FRONT,
+    )(span_row, query, kv_weight)
+    asked = lax.ppermute(absorbed, "role", swap)
+    absorbed, own_query = lax.optimization_barrier((absorbed, query))
+
     words = (half // HD) * QROWS
-    away = struct((KVH, half + PAIR + words, HD), bf16)
+    away = struct((KVH, half + PAIR, HD), bf16)
     away, value, mine = call(
         front_kernel,
         [away, struct((KVH, half, HD), bf16), struct((KVH, PAIR, HD), bf16)],
@@ -378,33 +382,31 @@
         flops=1_500_000_000,
         moved=6_000_000,
         limit=FRONT,
-    )(block_owner[0], cache_len, query, cache_kv[0], acts, kv_weight)
-    asked, away = lax.optimization_barrier((asked, away))
-    away, absorbed = call(
-        score_kernel,
-        [struct(away.shape, bf16), struct((KVH * QROWS, width), bf16)],
-        [V, V, H, H],
-        [V((width, COLS), bf16), V((KVH, words, HD), bf16), dma((3,))],
-        flops=300_000_000,
-        moved=3_000_000,
-        limit=SCORE,
-        aliases={3: 0},
-    )(asked, acts, kv_weight, away)
+    )(block_owner[0], cache_len, own_query, cache_kv[0], acts, kv_weight)
     theirs = lax.ppermute(away, "core", swap)
+    asked, value = lax.optimization_barrier((asked, value))
+    score = call(
+        other_kernel,
+        struct((KVH, words, HD), bf16),
+        [V, V],
+        flops=140_000_000,
+        moved=1_000_000,
+    )(asked, acts)
+    score = lax.ppermute(score, "core", swap)
     own = call(
         own_kernel,
         struct((KVH * QROWS, half), f32),
         [V, V],
-        flops=140_000_000,
+        flops=10_000_000_000,
         moved=2_000_000,
-    )(absorbed, acts)
+    )(asked, acts)
     sent = call(
         pack_kernel,
         struct((KVH, half + (half // HD) * QROWS + PAIR, HD), bf16),
-        [V] * 4,
+        [V] * 5,
         flops=10_000_000,
         moved=5_000_000,
-    )(theirs, value, own, mine)
+    )(theirs, score, value, own, mine)
     got = lax.all_to_all(sent, "yx", 0, 0, tiled=True)
 
     parts = call(

time: 64.6 us -> 64.3 us (level)
  starting transfers between devices: 10.8 us -> 12.8 us
  waiting for transfers between devices: 2.64 us -> 1.16 us
  other arithmetic: 0.91 us -> 0 us
    ppermute x1, waiting for transfers between devices: 2.64 us -> 0.01 us  [shards(): theirs = lax.ppermute(away, 'core', swap)]
    ppermute x1 -> x2, starting transfers between devices: 3.95 us -> 6 us  [the longest x1 3.95 us: shards(): asked = lax.ppermute(absorbed, 'role', swap)]
    ppermute x1 -> x2, waiting for transfers between devices: 0.01 us -> 1.15 us  [the longest x1 1.15 us: shards(): score = lax.ppermute(score, 'core', swap)]
    select_n x1 -> x0, other arithmetic: 0.91 us -> none  [shards(): chosen = jnp.where(span_row[0] == row, query[row], chosen)]
    pallas_call x2 -> x3, Pallas kernels: 2.95 us -> 3.08 us  [the longest x1 2.4 us: shards(): call(absorb_kernel, struct((KVH * QROWS, width), bf16), [S, H, H], [V(que...]
  transfers between devices with their start and end apart: 2 -> 3, of which waited for: 1 -> 1; matrix products, arithmetic and copies ran while one was open for 0% -> 0% of each run, Pallas kernels for 8% -> 9%
where the time goes in v7:
time: 64.3 us; the launch traced here: 64 us
  blocking collectives  38.7 us (60%)
  starting transfers between devices  12.8 us (20%)
  Pallas kernels  10.6 us (16%)
  waiting for transfers between devices  1.16 us (2%)
  between operations  0.78 us (1%)
    all_to_all x1, blocking collectives, shards(): got = lax.all_to_all(sent, 'yx', 0, 0, tiled=True)  23.4 us
    all_to_all x1, blocking collectives, shards(): lax.all_to_all(parts.reshape(4 * n_yx, PAIR, HD), ('role', 'yx', 'core'),...  15.3 us
    ppermute x1, starting transfers between devices, shards(): theirs = lax.ppermute(away, 'core', swap)  6.76 us
    pallas_call x1, Pallas kernels, shards(): call(front_kernel, [away, struct((KVH, half, HD), bf16), struct((KVH, PAI...  4.88 us
    ppermute x1, starting transfers between devices, shards(): asked = lax.ppermute(absorbed, 'role', swap)  3.95 us
    pallas_call x1, Pallas kernels, shards(): call(absorb_kernel, struct((KVH * QROWS, width), bf16), [S, H, H], [V(que...  2.4 us
    ppermute x1, starting transfers between devices, shards(): score = lax.ppermute(score, 'core', swap)  2.05 us
  transfers between devices with their start and end apart: 3, of which 1 were waited for; matrix products, arithmetic and copies ran while one was open for 0% of the time, Pallas kernels for 9%

profile of v7, /device:TPU:1, one launch (start us, length us, event | category | flops | bytes accessed | tf_op | source)
XLA Modules:
  0.0 64.0 jit_solution(275711420824405002)
XLA Ops:
  0.7 2.4 %shard_map.82 = bf16[256,512]{1,0:T(8,128)(2,1)} custom-call(s32[1,1]{1,0:T(1,128)S(6)} %copy.11.span_ref, bf16[2,8,32,128]{3,2,1,0:T(8,128)(2,1)} %bitcast.21, bf16[512,2048]{1,0:T(8,128)(2,1)} %w_hbm.3), custom_call_target="tpu_custom_call" | custom-call | flops 70000000 | bytes 1500000 | tf_op jit(solution)/shard_map/pallas_call | solution.py:355
  3.1 3.9 %collective-permute-start.1 = (bf16[256,512]{1,0:T(8,128)(2,1)}, bf16[256,512]{1,0:T(8,128)(2,1)S(1)}, u32[]{:S(2)}, u32[]{:S(2)}) collective-permute-start(bf16[256,512]{1,0:T(8,128)(2,1)} %shard_map.82), channel_id=1, source_target_pairs={{0,256},{256,0},{1,257},{257,1},{2,258},{258,2},{3,259},{259,3},{4... | collective-permute-start | bytes 786440 | tf_op jit(solution)/shard_map/ppermute | solution.py:364
  7.0 0.0 copy-start.1
  7.0 4.9 %shard_map.83 = (bf16[8,560,128]{2,1,0:T(8,128)(2,1)}, bf16[8,512,128]{2,1,0:T(8,128)(2,1)}, bf16[8,48,128]{2,1,0:T(8,128)(2,1)}) custom-call(s32[2,16]{1,0:T(2,128)} %bitcast.26, s32[1,2]{1,0:T(1,128)} %len_hbm.1, bf16[2,8,32,128]{3,2,1,0:T(8,128)(2,1)} %bitcast.22, bf16[2,192,2048]{2,1,0:T(8,128)(2,1)} %bitcast.25, bf16[1024,512]{1,0:T(8,128)(2,1)} %bitcast.18, ...), custom_call_target="tpu_custom_call" | custom-call | flops 1500000000 | bytes 6000000 | tf_op jit(solution)/shard_map/pallas_call | solution.py:369
  11.9 6.8 %collective-permute-start = (bf16[8,560,128]{2,1,0:T(8,128)(2,1)}, bf16[8,560,128]{2,1,0:T(8,128)(2,1)S(1)}, u32[]{:S(2)}, u32[]{:S(2)}) collective-permute-start(bf16[8,560,128]{2,1,0:T(8,128)(2,1)} %get-tuple-element.12), channel_id=1, source_target_pairs={{0,1},{1,0},{2,3},{3,2},{4,5},{5,4},{6,7},{7,6},{8,9},{9,8},{10,11... | collective-permute-start | bytes 3440648 | tf_op jit(solution)/shard_map/ppermute | solution.py:386
  18.7 0.0 collective-permute-done.1.qw_ref
  18.7 0.0 copy-done.1
  18.7 0.3 shard_map.84
  19.1 0.0 copy-start
  19.1 0.0 copy-start.3
  19.1 2.1 %collective-permute-start.2 = (bf16[8,128,128]{2,1,0:T(8,128)(2,1)S(1)}, bf16[8,128,128]{2,1,0:T(8,128)(2,1)S(1)}, u32[]{:S(2)}, u32[]{:S(2)}) collective-permute-start(bf16[8,128,128]{2,1,0:T(8,128)(2,1)S(1)} %shard_map.84), channel_id=1, source_target_pairs={{0,1},{1,0},{2,3},{3,2},{4,5},{5,4},{6,7},{7,6},{8,9},{9,8},{10,11... | collective-permute-start | bytes 786440 | tf_op jit(solution)/shard_map/ppermute | solution.py:395
  21.1 0.3 shard_map.85.own_ref
  21.5 1.2 %collective-permute-done.2.score_ref = bf16[8,128,128]{2,1,0:T(8,128)(2,1)S(1)} collective-permute-done((bf16[8,128,128]{2,1,0:T(8,128)(2,1)S(1)}, bf16[8,128,128]{2,1,0:T(8,128)(2,1)S(1)}, u32[]{:S(2)}, u32[]{:S(2)}) %collective-permute-start.2) | collective-permute-done | bytes 262176 | tf_op jit(solution)/shard_map/ppermute | solution.py:395
  22.6 0.0 collective-permute-done.got_ref
  22.6 0.0 copy-done
  22.6 0.0 copy-done.3
  22.6 0.9 %shard_map.86 = bf16[8,688,128]{2,1,0:T(8,128)(2,1)S(1)} custom-call(bf16[8,560,128]{2,1,0:T(8,128)(2,1)S(1)} %collective-permute-done.got_ref, bf16[8,128,128]{2,1,0:T(8,128)(2,1)S(1)} %collective-permute-done.2.score_ref, bf16[8,512,128]{2,1,0:T(8,128)(2,1)S(1)} %copy-done, f32[256,512]{1,0:T(8,128)S(1)} %shard_map.85.own_ref, ...), custom_call_target="tpu_custom_call" | custom-call | flops 10000000 | bytes 5000000 | tf_op jit(solution)/shard_map/pallas_call | solution.py:403
  23.5 0.0 copy-start.2
  23.5 0.0 copy-start.4
  23.5 23.4 %all_to_all.10.got_ref = bf16[8,688,128]{2,1,0:T(8,128)(2,1)S(1)} all-to-all(bf16[8,688,128]{2,1,0:T(8,128)(2,1)S(1)} %shard_map.86), channel_id=1, replica_groups=mesh['role'=2,'grp'=16,'yx'=8,'core'=2] {'yx'}, dimensions={0} | all-to-all | bytes 2818048 | tf_op jit(solution)/shard_map/all_to_all | solution.py:410
  46.9 0.0 copy-done.2
  46.9 0.6 shard_map.87
  47.6 15.3 %all_to_all.11 = bf16[32,48,128]{2,1,0:T(8,128)(2,1)S(1)} all-to-all(bf16[32,48,128]{2,1,0:T(8,128)(2,1)S(1)} %bitcast.17), channel_id=1, replica_groups=mesh['role'=2,'grp'=16,'yx'=8,'core'=2] {'role','yx','core'}, dimensions={0} | all-to-all | bytes 786432 | tf_op jit(solution)/shard_map/all_to_all | solution.py:419
  62.8 1.1 %shard_map.88 = bf16[2,8,32,128]{3,2,1,0:T(8,128)(2,1)} custom-call(s32[1,1]{1,0:T(1,128)S(6)} %copy.11.span_ref, bf16[2,16,48,128]{3,2,1,0:T(8,128)(2,1)S(1)} %bitcast.16), custom_call_target="tpu_custom_call" | custom-call | flops 10000000 | bytes 700000 | tf_op jit(solution)/shard_map/pallas_call | solution.py:422
  (1 shorter events, 0.0 us)
Async XLA Ops:
  3.1 15.6 %collective-permute-start.1 = (bf16[256,512]{1,0:T(8,128)(2,1)}, bf16[256,512]{1,0:T(8,128)(2,1)S(1)}, u32[]{:S(2)}, u32[]{:S(2)}) collective-permute-start(bf16[256,512]{1,0:T(8,128)(2,1)} %shard_map.82), channel_id=1, source_target_pairs={{0,256},{256,0},{1,257},{257,1},{2,258},{258,2},{3,259},{259,3},{4... | collective-permute-start | bytes 786440 | tf_op jit(solution)/shard_map/ppermute | solution.py:364
  7.0 11.7 %copy-start.1 = (bf16[1,1,1024,512]{3,2,1,0:T(8,128)(2,1)S(1)}, bf16[1,1,1024,512]{3,2,1,0:T(8,128)(2,1)}, u32[]{:S(2)}) copy-start(bf16[1,1,1024,512]{3,2,1,0:T(8,128)(2,1)} %param.8) | copy-start | bytes 3145732
  11.9 10.7 %collective-permute-start = (bf16[8,560,128]{2,1,0:T(8,128)(2,1)}, bf16[8,560,128]{2,1,0:T(8,128)(2,1)S(1)}, u32[]{:S(2)}, u32[]{:S(2)}) collective-permute-start(bf16[8,560,128]{2,1,0:T(8,128)(2,1)} %get-tuple-element.12), channel_id=1, source_target_pairs={{0,1},{1,0},{2,3},{3,2},{4,5},{5,4},{6,7},{7,6},{8,9},{9,8},{10,11... | collective-permute-start | bytes 3440648 | tf_op jit(solution)/shard_map/ppermute | solution.py:386
  19.1 3.6 %copy-start = (bf16[8,512,128]{2,1,0:T(8,128)(2,1)S(1)}, bf16[8,512,128]{2,1,0:T(8,128)(2,1)}, u32[]{:S(2)}) copy-start(bf16[8,512,128]{2,1,0:T(8,128)(2,1)} %get-tuple-element.15.value_ref) | copy-start | bytes 3145732
  19.1 3.6 %copy-start.3 = (bf16[8,48,128]{2,1,0:T(8,128)(2,1)S(1)}, bf16[8,48,128]{2,1,0:T(8,128)(2,1)}, u32[]{:S(2)}) copy-start(bf16[8,48,128]{2,1,0:T(8,128)(2,1)} %get-tuple-element.16.mine_ref) | copy-start | bytes 294916
  19.1 3.6 %collective-permute-start.2 = (bf16[8,128,128]{2,1,0:T(8,128)(2,1)S(1)}, bf16[8,128,128]{2,1,0:T(8,128)(2,1)S(1)}, u32[]{:S(2)}, u32[]{:S(2)}) collective-permute-start(bf16[8,128,128]{2,1,0:T(8,128)(2,1)S(1)} %shard_map.84), channel_id=1, source_target_pairs={{0,1},{1,0},{2,3},{3,2},{4,5},{5,4},{6,7},{7,6},{8,9},{9,8},{10,11... | collective-permute-start | bytes 786440 | tf_op jit(solution)/shard_map/ppermute | solution.py:395
  23.5 23.4 %copy-start.2 = (bf16[1,2,4,8192]{3,2,1,0:T(4,128)(2,1)S(1)}, bf16[1,2,4,8192]{3,2,1,0:T(4,128)(2,1)}, u32[]{:S(2)}) copy-start(bf16[1,2,4,8192]{3,2,1,0:T(4,128)(2,1)} %param.14) | copy-start | bytes 393220
  23.5 23.4 %copy-start.4 = (bf16[1,2,4,2048]{3,2,1,0:T(4,128)(2,1)S(1)}, bf16[1,2,4,2048]{3,2,1,0:T(4,128)(2,1)}, u32[]{:S(2)}) copy-start(bf16[1,2,4,2048]{3,2,1,0:T(4,128)(2,1)} %param.15) | copy-start | bytes 98308

commit v8 on v7

--- a/solution.py
+++ b/solution.py
@@ -101,15 +101,17 @@
     cache_hbm,
     acts_hbm,
     w_hbm,
-    away_ref,
-    value_ref,
-    mine_ref,
+    away_hbm,
+    value_hbm,
+    mine_hbm,
     owner_ref,
     len_ref,
     q_ref,
     cache_ref,
     acts_ref,
     w_ref,
+    value_ref,
+    pair_ref,
     sems,
 ):
     core = lax.axis_index("core")
@@ -118,60 +120,72 @@
     span = acts_ref.shape[0]
     half = span // 2
     order = (1 - core, core)
-    ints = [
+    early = [
+        pltpu.make_async_copy(acts_hbm, acts_ref, sems.at[5]),
+        pltpu.make_async_copy(w_hbm.at[:, COLS : 2 * COLS], w_ref, sems.at[6]),
+    ]
+    loads = [
         pltpu.make_async_copy(owner_hbm, owner_ref, sems.at[0]),
         pltpu.make_async_copy(len_hbm, len_ref, sems.at[1]),
         pltpu.make_async_copy(q_hbm, q_ref, sems.at[2]),
     ]
-    loads = [
+    loads += [
         pltpu.make_async_copy(cache_hbm.at[row], cache_ref.at[k], sems.at[3 + k])
         for k, row in enumerate(order)
     ]
-    late = [
-        pltpu.make_async_copy(acts_hbm, acts_ref, sems.at[5]),
-        pltpu.make_async_copy(w_hbm.at[:, COLS : 2 * COLS], w_ref, sems.at[6]),
-    ]
-    for copy in (*ints, *loads, *late):
+    stores = [
+        pltpu.make_async_copy(value_ref.at[0], away_hbm.at[:, :half], sems.at[7]),
+        pltpu.make_async_copy(value_ref.at[1], value_hbm, sems.at[8]),
+        pltpu.make_async_copy(pair_ref.at[0], away_hbm.at[:, half : half + PAIR], sems.at[9]),
+        pltpu.make_async_copy(pair_ref.at[1], mine_hbm, sems.at[10]),
+    ]
+    for copy in (*early, *loads):
         copy.start()
-    for copy in ints:
+    for copy in early:
         copy.wait()
     for k, row in enumerate(order):
+        tokens = acts_ref[pl.ds(pl.multiple_of(row * half, half), half), :]
+        value = dot_nn(tokens, w_ref[...]).astype(bf16)
+        for head in range(KVH):
+            value_ref[k, head] = value[:, head_cols(head)]
+        stores[k].start()
+    for copy in loads:
+        copy.wait()
+    lives = []
+    for row in order:
         first = jnp.int32(0)
         for block in range(owner_ref.shape[1]):
             first = first + jnp.where(owner_ref[row, block] == me, block, 0)
         room = len_ref[0, row] - first * slab
-        live = lax.broadcasted_iota(jnp.int32, (KVH * QROWS, slab), 1) < room
-        loads[k].wait()
-        score = stacked(
-            [dot_nt(q_ref[row, head], cache_ref[k, :, head_cols(head)]) for head in range(KVH)]
-        )
-        score = jnp.where(live, score * SCALE, NEG)
-        top = jnp.max(score, axis=-1, keepdims=True)
-        weight = jnp.where(live, jnp.exp(score - top), 0.0)
-        total = jnp.sum(weight, axis=-1, keepdims=True)
-        safe = jnp.where(total > 0.0, total, 1.0)
-        weight = weight.astype(bf16)
-        out = stacked(
-            [
-                dot_nn(
-                    weight[head * QROWS : (head + 1) * QROWS],
-                    cache_ref[k, :, head_cols(head, COLS)],
-                )
-                for head in range(KVH)
-            ]
-        )
-        lse = jnp.where(total > 0.0, top + jnp.log(safe), NEG)
-        if k == 0:
-            put_pair(away_ref, half, out / safe, lse)
-        else:
-            put_pair(mine_ref, 0, out / safe, lse)
-    for copy in late:
-        copy.wait()
-    for row, out_ref in zip(order, (away_ref, value_ref)):
-        tokens = acts_ref[pl.ds(pl.multiple_of(row * half, half), half), :]
-        value = dot_nn(tokens, w_ref[...]).astype(bf16)
-        for head in range(KVH):
-            out_ref[head, :half] = value[:, head_cols(head)]
+        lives.append(lax.broadcasted_iota(jnp.int32, (KVH * QROWS, slab), 1) < room)
+    live = stacked(lives)
+    places = [(k, row, head) for k, row in enumerate(order) for head in range(KVH)]
+    score = stacked(
+        [dot_nt(q_ref[row, head], cache_ref[k, :, head_cols(head)]) for k, row, head in places]
+    )
+    score = jnp.where(live, score * SCALE, NEG)
+    top = jnp.max(score, axis=-1, keepdims=True)
+    weight = jnp.where(live, jnp.exp(score - top), 0.0)
+    total = jnp.sum(weight, axis=-1, keepdims=True)
+    safe = jnp.where(total > 0.0, total, 1.0)
+    weight = weight.astype(bf16)
+    out = stacked(
+        [
+            dot_nn(
+                weight[at * QROWS : (at + 1) * QROWS], cache_ref[k, :, head_cols(head, COLS)]
+            )
+            for at, (k, _, head) in enumerate(places)
+        ]
+    )
+    out = out / safe
+    lse = jnp.where(total > 0.0, top + jnp.log(safe), NEG)
+    middle = KVH * QROWS
+    put_pair(pair_ref.at[0], 0, out[:middle], lse[:middle])
+    put_pair(pair_ref.at[1], 0, out[middle:], lse[middle:])
+    for store in stores[2:]:
+        store.start()
+    for store in stores:
+        store.wait()
 
 
 def absorb_kernel(span_ref, q_hbm, w_hbm, out_ref, q_ref, w_ref, sems):
@@ -292,9 +306,13 @@
         out_ref[1 - role, chunk] = fresh
 
 
-def join_kernel(span_ref, got_ref, out_ref):
+def join_kernel(span_ref, got_ref, out_hbm, out_ref, sems):
     role = lax.axis_index("role")
     rows = out_ref.shape[0]
+    stores = [
+        pltpu.make_async_copy(out_ref.at[row], out_hbm.at[row], sems.at[row])
+        for row in range(rows)
+    ]
 
     def stats(pool, core):
         return stacked([stat_row(got_ref[pool, 2 * head + core, QROWS:]) for head in range(KVH)])
@@ -314,18 +332,18 @@
                 weight = weights[(row * 3 + k) * KVH + head]
                 out = out + weight * got_ref[pool, 2 * head + core, :QROWS].astype(f32)
             out_ref[row, head] = out.astype(bf16)
-
-
-def call(kernel, out_shapes, spaces, scratch=(), flops=0, moved=0, limit=24, aliases=None):
-    out_specs = jax.tree.map(lambda _: pl.BlockSpec(memory_space=pltpu.VMEM), out_shapes)
-    for target in (aliases or {}).values():
-        out_specs[target] = pl.BlockSpec(memory_space=H)
+        stores[row].start()
+    for store in stores:
+        store.wait()
+
+
+def call(kernel, out_shapes, spaces, scratch=(), flops=0, moved=0, limit=24, out_space=pltpu.VMEM):
+    out_specs = jax.tree.map(lambda _: pl.BlockSpec(memory_space=out_space), out_shapes)
     return pl.pallas_call(
         kernel,
         out_shape=out_shapes,
         in_specs=[pl.BlockSpec(memory_space=space) for space in spaces],
         out_specs=out_specs,
-        input_output_aliases=aliases or {},
         scratch_shapes=list(scratch),
         compiler_params=pltpu.CompilerParams(vmem_limit_bytes=limit << 20),
         cost_estimate=pl.CostEstimate(flops=flops, bytes_accessed=moved, transcendentals=0),
@@ -377,11 +395,14 @@
             V(cache_kv.shape[1:], bf16),
             V(acts.shape, bf16),
             V((width, COLS), bf16),
-            dma((7,)),
+            V((2, KVH, half, HD), bf16),
+            V((2, KVH, PAIR, HD), bf16),
+            dma((11,)),
         ],
         flops=1_500_000_000,
         moved=6_000_000,
         limit=FRONT,
+        out_space=H,
     )(block_owner[0], cache_len, own_query, cache_kv[0], acts, kv_weight)
     theirs = lax.ppermute(away, "core", swap)
     asked, value = lax.optimization_barrier((asked, value))
@@ -419,8 +440,15 @@
     parts = lax.all_to_all(
         parts.reshape(4 * n_yx, PAIR, HD), ("role", "yx", "core"), 0, 0, tiled=True
     )
+    joined = struct((rows, KVH, QROWS, HD), bf16)
     joined = call(
-        join_kernel, struct((rows, KVH, QROWS, HD), bf16), [S, V], flops=10_000_000, moved=700_000
+        join_kernel,
+        joined,
+        [S, V],
+        [V(joined.shape, bf16), dma((rows,))],
+        flops=10_000_000,
+        moved=700_000,
+        out_space=H,
     )(span_row, parts.reshape(2, 2 * n_yx, PAIR, HD))
     output = joined.reshape(rows, KVH, GROUP, DRAFT, HD).transpose(0, 3, 1, 2, 4)
     return output.reshape(1, rows, DRAFT, QH * HD)

time: 64.3 us -> 64.1 us (level)
  transfers between devices with their start and end apart: 3 -> 3, of which waited for: 1 -> 1; matrix products, arithmetic and copies ran while one was open for 0% -> 0% of each run, Pallas kernels for 9% -> 8%
where the time goes in v8:
time: 64.1 us; the launch traced here: 63.8 us
  blocking collectives  38.7 us (60%)
  starting transfers between devices  12.8 us (20%)
  Pallas kernels  10.4 us (16%)
  waiting for transfers between devices  1.16 us (2%)
  between operations  0.78 us (1%)
    all_to_all x1, blocking collectives, shards(): got = lax.all_to_all(sent, 'yx', 0, 0, tiled=True)  23 us
    all_to_all x1, blocking collectives, shards(): lax.all_to_all(parts.reshape(4 * n_yx, PAIR, HD), ('role', 'yx', 'core'),...  15.7 us
    ppermute x1, starting transfers between devices, shards(): theirs = lax.ppermute(away, 'core', swap)  6.75 us
    pallas_call x1, Pallas kernels, shards(): call(front_kernel, [away, struct((KVH, half, HD), bf16), struct((KVH, PAI...  4.69 us
    ppermute x1, starting transfers between devices, shards(): asked = lax.ppermute(absorbed, 'role', swap)  3.95 us
    pallas_call x1, Pallas kernels, shards(): call(absorb_kernel, struct((KVH * QROWS, width), bf16), [S, H, H], [V(que...  2.4 us
    ppermute x1, starting transfers between devices, shards(): score = lax.ppermute(score, 'core', swap)  2.05 us
  transfers between devices with their start and end apart: 3, of which 1 were waited for; matrix products, arithmetic and copies ran while one was open for 0% of the time, Pallas kernels for 8%

profile of v8, /device:TPU:1, one launch (start us, length us, event | category | flops | bytes accessed | tf_op | source)
XLA Modules:
  0.0 63.8 jit_solution(17322503987192020644)
XLA Ops:
  0.7 2.4 %shard_map.82 = bf16[256,512]{1,0:T(8,128)(2,1)} custom-call(s32[1,1]{1,0:T(1,128)S(6)} %copy.11.span_ref, bf16[2,8,32,128]{3,2,1,0:T(8,128)(2,1)} %bitcast.21, bf16[512,2048]{1,0:T(8,128)(2,1)} %w_hbm.3), custom_call_target="tpu_custom_call" | custom-call | flops 70000000 | bytes 1500000 | tf_op jit(solution)/shard_map/pallas_call | solution.py:373
  3.1 3.9 %collective-permute-start.1 = (bf16[256,512]{1,0:T(8,128)(2,1)}, bf16[256,512]{1,0:T(8,128)(2,1)S(1)}, u32[]{:S(2)}, u32[]{:S(2)}) collective-permute-start(bf16[256,512]{1,0:T(8,128)(2,1)} %shard_map.82), channel_id=1, source_target_pairs={{0,256},{256,0},{1,257},{257,1},{2,258},{258,2},{3,259},{259,3},{4... | collective-permute-start | bytes 786440 | tf_op jit(solution)/shard_map/ppermute | solution.py:382
  7.0 0.0 copy-start.1
  7.0 4.7 %shard_map.83 = (bf16[8,560,128]{2,1,0:T(8,128)(2,1)}, bf16[8,512,128]{2,1,0:T(8,128)(2,1)}, bf16[8,48,128]{2,1,0:T(8,128)(2,1)}) custom-call(s32[2,16]{1,0:T(2,128)} %bitcast.26, s32[1,2]{1,0:T(1,128)} %len_hbm.1, bf16[2,8,32,128]{3,2,1,0:T(8,128)(2,1)} %bitcast.22, bf16[2,192,2048]{2,1,0:T(8,128)(2,1)} %bitcast.25, bf16[1024,512]{1,0:T(8,128)(2,1)} %bitcast.18, ...), custom_call_target="tpu_custom_call" | custom-call | flops 1500000000 | bytes 6000000 | tf_op jit(solution)/shard_map/pallas_call | solution.py:387
  11.7 6.8 %collective-permute-start = (bf16[8,560,128]{2,1,0:T(8,128)(2,1)}, bf16[8,560,128]{2,1,0:T(8,128)(2,1)S(1)}, u32[]{:S(2)}, u32[]{:S(2)}) collective-permute-start(bf16[8,560,128]{2,1,0:T(8,128)(2,1)} %get-tuple-element.12), channel_id=1, source_target_pairs={{0,1},{1,0},{2,3},{3,2},{4,5},{5,4},{6,7},{7,6},{8,9},{9,8},{10,11... | collective-permute-start | bytes 3440648 | tf_op jit(solution)/shard_map/ppermute | solution.py:407
  18.5 0.0 collective-permute-done.1.qw_ref
  18.5 0.0 copy-done.1
  18.5 0.3 shard_map.84
  18.9 0.0 copy-start
  18.9 0.0 copy-start.3
  18.9 2.1 %collective-permute-start.2 = (bf16[8,128,128]{2,1,0:T(8,128)(2,1)S(1)}, bf16[8,128,128]{2,1,0:T(8,128)(2,1)S(1)}, u32[]{:S(2)}, u32[]{:S(2)}) collective-permute-start(bf16[8,128,128]{2,1,0:T(8,128)(2,1)S(1)} %shard_map.84), channel_id=1, source_target_pairs={{0,1},{1,0},{2,3},{3,2},{4,5},{5,4},{6,7},{7,6},{8,9},{9,8},{10,11... | collective-permute-start | bytes 786440 | tf_op jit(solution)/shard_map/ppermute | solution.py:416
  20.9 0.3 shard_map.85.own_ref
  21.3 1.2 %collective-permute-done.2.score_ref = bf16[8,128,128]{2,1,0:T(8,128)(2,1)S(1)} collective-permute-done((bf16[8,128,128]{2,1,0:T(8,128)(2,1)S(1)}, bf16[8,128,128]{2,1,0:T(8,128)(2,1)S(1)}, u32[]{:S(2)}, u32[]{:S(2)}) %collective-permute-start.2) | collective-permute-done | bytes 262176 | tf_op jit(solution)/shard_map/ppermute | solution.py:416
  22.4 0.0 collective-permute-done.got_ref
  22.4 0.0 copy-done
  22.4 0.0 copy-done.3
  22.5 0.9 %shard_map.86 = bf16[8,688,128]{2,1,0:T(8,128)(2,1)S(1)} custom-call(bf16[8,560,128]{2,1,0:T(8,128)(2,1)S(1)} %collective-permute-done.got_ref, bf16[8,128,128]{2,1,0:T(8,128)(2,1)S(1)} %collective-permute-done.2.score_ref, bf16[8,512,128]{2,1,0:T(8,128)(2,1)S(1)} %copy-done, f32[256,512]{1,0:T(8,128)S(1)} %shard_map.85.own_ref, ...), custom_call_target="tpu_custom_call" | custom-call | flops 10000000 | bytes 5000000 | tf_op jit(solution)/shard_map/pallas_call | solution.py:424
  23.3 0.0 copy-start.2
  23.3 0.0 copy-start.4
  23.3 23.0 %all_to_all.10.got_ref = bf16[8,688,128]{2,1,0:T(8,128)(2,1)S(1)} all-to-all(bf16[8,688,128]{2,1,0:T(8,128)(2,1)S(1)} %shard_map.86), channel_id=1, replica_groups=mesh['role'=2,'grp'=16,'yx'=8,'core'=2] {'yx'}, dimensions={0} | all-to-all | bytes 2818048 | tf_op jit(solution)/shard_map/all_to_all | solution.py:431
  46.3 0.0 copy-done.4
  46.3 0.6 shard_map.87
  46.9 15.7 %all_to_all.11 = bf16[32,48,128]{2,1,0:T(8,128)(2,1)S(1)} all-to-all(bf16[32,48,128]{2,1,0:T(8,128)(2,1)S(1)} %bitcast.17), channel_id=1, replica_groups=mesh['role'=2,'grp'=16,'yx'=8,'core'=2] {'role','yx','core'}, dimensions={0} | all-to-all | bytes 786432 | tf_op jit(solution)/shard_map/all_to_all | solution.py:440
  62.6 1.1 %shard_map.88 = bf16[2,8,32,128]{3,2,1,0:T(8,128)(2,1)} custom-call(s32[1,1]{1,0:T(1,128)S(6)} %copy.11.span_ref, bf16[2,16,48,128]{3,2,1,0:T(8,128)(2,1)S(1)} %bitcast.16), custom_call_target="tpu_custom_call" | custom-call | flops 10000000 | bytes 700000 | tf_op jit(solution)/shard_map/pallas_call | solution.py:444
  (1 shorter events, 0.0 us)
Async XLA Ops:
  3.1 15.4 %collective-permute-start.1 = (bf16[256,512]{1,0:T(8,128)(2,1)}, bf16[256,512]{1,0:T(8,128)(2,1)S(1)}, u32[]{:S(2)}, u32[]{:S(2)}) collective-permute-start(bf16[256,512]{1,0:T(8,128)(2,1)} %shard_map.82), channel_id=1, source_target_pairs={{0,256},{256,0},{1,257},{257,1},{2,258},{258,2},{3,259},{259,3},{4... | collective-permute-start | bytes 786440 | tf_op jit(solution)/shard_map/ppermute | solution.py:382
  7.0 11.5 %copy-start.1 = (bf16[1,1,1024,512]{3,2,1,0:T(8,128)(2,1)S(1)}, bf16[1,1,1024,512]{3,2,1,0:T(8,128)(2,1)}, u32[]{:S(2)}) copy-start(bf16[1,1,1024,512]{3,2,1,0:T(8,128)(2,1)} %param.8) | copy-start | bytes 3145732
  11.7 10.7 %collective-permute-start = (bf16[8,560,128]{2,1,0:T(8,128)(2,1)}, bf16[8,560,128]{2,1,0:T(8,128)(2,1)S(1)}, u32[]{:S(2)}, u32[]{:S(2)}) collective-permute-start(bf16[8,560,128]{2,1,0:T(8,128)(2,1)} %get-tuple-element.12), channel_id=1, source_target_pairs={{0,1},{1,0},{2,3},{3,2},{4,5},{5,4},{6,7},{7,6},{8,9},{9,8},{10,11... | collective-permute-start | bytes 3440648 | tf_op jit(solution)/shard_map/ppermute | solution.py:407
  18.9 3.6 %copy-start = (bf16[8,512,128]{2,1,0:T(8,128)(2,1)S(1)}, bf16[8,512,128]{2,1,0:T(8,128)(2,1)}, u32[]{:S(2)}) copy-start(bf16[8,512,128]{2,1,0:T(8,128)(2,1)} %get-tuple-element.15.value_ref) | copy-start | bytes 3145732
  18.9 3.6 %copy-start.3 = (bf16[8,48,128]{2,1,0:T(8,128)(2,1)S(1)}, bf16[8,48,128]{2,1,0:T(8,128)(2,1)}, u32[]{:S(2)}) copy-start(bf16[8,48,128]{2,1,0:T(8,128)(2,1)} %get-tuple-element.16.mine_ref) | copy-start | bytes 294916
  18.9 3.6 %collective-permute-start.2 = (bf16[8,128,128]{2,1,0:T(8,128)(2,1)S(1)}, bf16[8,128,128]{2,1,0:T(8,128)(2,1)S(1)}, u32[]{:S(2)}, u32[]{:S(2)}) collective-permute-start(bf16[8,128,128]{2,1,0:T(8,128)(2,1)S(1)} %shard_map.84), channel_id=1, source_target_pairs={{0,1},{1,0},{2,3},{3,2},{4,5},{5,4},{6,7},{7,6},{8,9},{9,8},{10,11... | collective-permute-start | bytes 786440 | tf_op jit(solution)/shard_map/ppermute | solution.py:416
  23.3 23.0 %copy-start.2 = (bf16[1,2,4,8192]{3,2,1,0:T(4,128)(2,1)S(1)}, bf16[1,2,4,8192]{3,2,1,0:T(4,128)(2,1)}, u32[]{:S(2)}) copy-start(bf16[1,2,4,8192]{3,2,1,0:T(4,128)(2,1)} %param.14) | copy-start | bytes 393220
  23.3 23.0 %copy-start.4 = (bf16[1,2,4,2048]{3,2,1,0:T(4,128)(2,1)S(1)}, bf16[1,2,4,2048]{3,2,1,0:T(4,128)(2,1)}, u32[]{:S(2)}) copy-start(bf16[1,2,4,2048]{3,2,1,0:T(4,128)(2,1)} %param.15) | copy-start | bytes 98308

commit v9 on v8

--- a/solution.py
+++ b/solution.py
@@ -16,6 +16,7 @@
 GROUP = QH // KVH
 QROWS = GROUP * DRAFT
 STAT = 16
+PARTS = 4
 PAIR = QROWS + STAT
 COLS = KVH * HD
 NEG = -1e30
@@ -143,12 +144,15 @@
         copy.start()
     for copy in early:
         copy.wait()
-    for k, row in enumerate(order):
-        tokens = acts_ref[pl.ds(pl.multiple_of(row * half, half), half), :]
-        value = dot_nn(tokens, w_ref[...]).astype(bf16)
+
+    def values(k):
+        start = pl.multiple_of(order[k] * half, half)
+        value = dot_nn(acts_ref[pl.ds(start, half), :], w_ref[...]).astype(bf16)
         for head in range(KVH):
             value_ref[k, head] = value[:, head_cols(head)]
         stores[k].start()
+
+    values(0)
     for copy in loads:
         copy.wait()
     lives = []
@@ -163,6 +167,7 @@
     score = stacked(
         [dot_nt(q_ref[row, head], cache_ref[k, :, head_cols(head)]) for k, row, head in places]
     )
+    values(1)
     score = jnp.where(live, score * SCALE, NEG)
     top = jnp.max(score, axis=-1, keepdims=True)
     weight = jnp.where(live, jnp.exp(score - top), 0.0)
@@ -189,19 +194,19 @@
 
 
 def absorb_kernel(span_ref, q_hbm, w_hbm, out_ref, q_ref, w_ref, sems):
-    middle = COLS // 2
+    part = COLS // PARTS
     row = span_ref[0, 0]
-    first = pltpu.make_async_copy(q_hbm.at[row], q_ref, sems.at[2])
+    first = pltpu.make_async_copy(q_hbm.at[row], q_ref, sems.at[PARTS])
     loads = [
         pltpu.make_async_copy(w_hbm.at[:, cols], w_ref.at[:, cols], sems.at[k])
-        for k, cols in enumerate((slice(0, middle), slice(middle, COLS)))
+        for k, cols in enumerate(slice(k * part, (k + 1) * part) for k in range(PARTS))
     ]
     for copy in (first, *loads):
         copy.start()
     first.wait()
     for head in range(KVH):
-        if head * HD % middle == 0:
-            loads[head * HD // middle].wait()
+        if head * HD % part == 0:
+            loads[head * HD // part].wait()
         rows = slice(head * QROWS, (head + 1) * QROWS)
         out_ref[rows] = dot_nt(q_ref[head], w_ref[:, head_cols(head)]).astype(bf16)
 
@@ -224,7 +229,7 @@
 def pack_kernel(got_ref, score_ref, value_ref, own_ref, mine_ref, out_ref):
     half = value_ref.shape[1]
     tiles = half // HD
-    out_ref[:, :half] = (value_ref[...].astype(f32) + got_ref[:, :half].astype(f32)).astype(bf16)
+    out_ref[:, :half] = value_ref[...] + got_ref[:, :half]
     shape = (KVH, QROWS, HD)
     for tile in range(tiles):
         at = tile * QROWS
@@ -374,7 +379,7 @@
         absorb_kernel,
         struct((KVH * QROWS, width), bf16),
         [S, H, H],
-        [V(query.shape[1:], bf16), V((width, COLS), bf16), dma((3,))],
+        [V(query.shape[1:], bf16), V((width, COLS), bf16), dma((PARTS + 1,))],
         flops=70_000_000,
         moved=1_500_000,
         limit=FRONT,

time: 64.1 us -> 64.3 us (level)
  transfers between devices with their start and end apart: 3 -> 3, of which waited for: 1 -> 1; matrix products, arithmetic and copies ran while one was open for 0% -> 0% of each run, Pallas kernels for 8% -> 9%
where the time goes in v9:
time: 64.3 us; the launch traced here: 64 us
  blocking collectives  38.7 us (60%)
  starting transfers between devices  12.8 us (20%)
  Pallas kernels  10.6 us (16%)
  waiting for transfers between devices  1.16 us (2%)
  between operations  0.78 us (1%)
    all_to_all x1, blocking collectives, shards(): got = lax.all_to_all(sent, 'yx', 0, 0, tiled=True)  23.4 us
    all_to_all x1, blocking collectives, shards(): lax.all_to_all(parts.reshape(4 * n_yx, PAIR, HD), ('role', 'yx', 'core'),...  15.3 us
    ppermute x1, starting transfers between devices, shards(): theirs = lax.ppermute(away, 'core', swap)  6.76 us
    pallas_call x1, Pallas kernels, shards(): call(front_kernel, [away, struct((KVH, half, HD), bf16), struct((KVH, PAI...  4.82 us
    ppermute x1, starting transfers between devices, shards(): asked = lax.ppermute(absorbed, 'role', swap)  3.95 us
    pallas_call x1, Pallas kernels, shards(): call(absorb_kernel, struct((KVH * QROWS, width), bf16), [S, H, H], [V(que...  2.56 us
    ppermute x1, starting transfers between devices, shards(): score = lax.ppermute(score, 'core', swap)  2.05 us
  transfers between devices with their start and end apart: 3, of which 1 were waited for; matrix products, arithmetic and copies ran while one was open for 0% of the time, Pallas kernels for 9%

profile of v9, /device:TPU:1, one launch (start us, length us, event | category | flops | bytes accessed | tf_op | source)
XLA Modules:
  0.0 64.0 jit_solution(3959373626759673400)
XLA Ops:
  0.7 2.6 %shard_map.82 = bf16[256,512]{1,0:T(8,128)(2,1)} custom-call(s32[1,1]{1,0:T(1,128)S(6)} %copy.11.span_ref, bf16[2,8,32,128]{3,2,1,0:T(8,128)(2,1)} %bitcast.21, bf16[512,2048]{1,0:T(8,128)(2,1)} %w_hbm.3), custom_call_target="tpu_custom_call" | custom-call | flops 70000000 | bytes 1500000 | tf_op jit(solution)/shard_map/pallas_call | solution.py:378
  3.2 3.9 %collective-permute-start.1 = (bf16[256,512]{1,0:T(8,128)(2,1)}, bf16[256,512]{1,0:T(8,128)(2,1)S(1)}, u32[]{:S(2)}, u32[]{:S(2)}) collective-permute-start(bf16[256,512]{1,0:T(8,128)(2,1)} %shard_map.82), channel_id=1, source_target_pairs={{0,256},{256,0},{1,257},{257,1},{2,258},{258,2},{3,259},{259,3},{4... | collective-permute-start | bytes 786440 | tf_op jit(solution)/shard_map/ppermute | solution.py:387
  7.2 0.0 copy-start.1
  7.2 4.8 %shard_map.83 = (bf16[8,560,128]{2,1,0:T(8,128)(2,1)}, bf16[8,512,128]{2,1,0:T(8,128)(2,1)}, bf16[8,48,128]{2,1,0:T(8,128)(2,1)}) custom-call(s32[2,16]{1,0:T(2,128)} %bitcast.26, s32[1,2]{1,0:T(1,128)} %len_hbm.1, bf16[2,8,32,128]{3,2,1,0:T(8,128)(2,1)} %bitcast.22, bf16[2,192,2048]{2,1,0:T(8,128)(2,1)} %bitcast.25, bf16[1024,512]{1,0:T(8,128)(2,1)} %bitcast.18, ...), custom_call_target="tpu_custom_call" | custom-call | flops 1500000000 | bytes 6000000 | tf_op jit(solution)/shard_map/pallas_call | solution.py:392
  12.0 6.8 %collective-permute-start = (bf16[8,560,128]{2,1,0:T(8,128)(2,1)}, bf16[8,560,128]{2,1,0:T(8,128)(2,1)S(1)}, u32[]{:S(2)}, u32[]{:S(2)}) collective-permute-start(bf16[8,560,128]{2,1,0:T(8,128)(2,1)} %get-tuple-element.12), channel_id=1, source_target_pairs={{0,1},{1,0},{2,3},{3,2},{4,5},{5,4},{6,7},{7,6},{8,9},{9,8},{10,11... | collective-permute-start | bytes 3440648 | tf_op jit(solution)/shard_map/ppermute | solution.py:412
  18.8 0.0 collective-permute-done.1.qw_ref
  18.8 0.0 copy-done.1
  18.8 0.3 shard_map.84
  19.2 0.0 copy-start
  19.2 0.0 copy-start.3
  19.2 2.1 %collective-permute-start.2 = (bf16[8,128,128]{2,1,0:T(8,128)(2,1)S(1)}, bf16[8,128,128]{2,1,0:T(8,128)(2,1)S(1)}, u32[]{:S(2)}, u32[]{:S(2)}) collective-permute-start(bf16[8,128,128]{2,1,0:T(8,128)(2,1)S(1)} %shard_map.84), channel_id=1, source_target_pairs={{0,1},{1,0},{2,3},{3,2},{4,5},{5,4},{6,7},{7,6},{8,9},{9,8},{10,11... | collective-permute-start | bytes 786440 | tf_op jit(solution)/shard_map/ppermute | solution.py:421
  21.2 0.3 shard_map.85.own_ref
  21.6 1.2 %collective-permute-done.2.score_ref = bf16[8,128,128]{2,1,0:T(8,128)(2,1)S(1)} collective-permute-done((bf16[8,128,128]{2,1,0:T(8,128)(2,1)S(1)}, bf16[8,128,128]{2,1,0:T(8,128)(2,1)S(1)}, u32[]{:S(2)}, u32[]{:S(2)}) %collective-permute-start.2) | collective-permute-done | bytes 262176 | tf_op jit(solution)/shard_map/ppermute | solution.py:421
  22.7 0.0 collective-permute-done.got_ref
  22.7 0.0 copy-done
  22.7 0.0 copy-done.3
  22.8 0.8 %shard_map.86 = bf16[8,688,128]{2,1,0:T(8,128)(2,1)S(1)} custom-call(bf16[8,560,128]{2,1,0:T(8,128)(2,1)S(1)} %collective-permute-done.got_ref, bf16[8,128,128]{2,1,0:T(8,128)(2,1)S(1)} %collective-permute-done.2.score_ref, bf16[8,512,128]{2,1,0:T(8,128)(2,1)S(1)} %copy-done, f32[256,512]{1,0:T(8,128)S(1)} %shard_map.85.own_ref, ...), custom_call_target="tpu_custom_call" | custom-call | flops 10000000 | bytes 5000000 | tf_op jit(solution)/shard_map/pallas_call | solution.py:429
  23.5 0.0 copy-start.2
  23.5 0.0 copy-start.4
  23.5 23.4 %all_to_all.10.got_ref = bf16[8,688,128]{2,1,0:T(8,128)(2,1)S(1)} all-to-all(bf16[8,688,128]{2,1,0:T(8,128)(2,1)S(1)} %shard_map.86), channel_id=1, replica_groups=mesh['role'=2,'grp'=16,'yx'=8,'core'=2] {'yx'}, dimensions={0} | all-to-all | bytes 2818048 | tf_op jit(solution)/shard_map/all_to_all | solution.py:436
  46.9 0.0 copy-done.2
  46.9 0.6 shard_map.87
  47.5 15.3 %all_to_all.11 = bf16[32,48,128]{2,1,0:T(8,128)(2,1)S(1)} all-to-all(bf16[32,48,128]{2,1,0:T(8,128)(2,1)S(1)} %bitcast.17), channel_id=1, replica_groups=mesh['role'=2,'grp'=16,'yx'=8,'core'=2] {'role','yx','core'}, dimensions={0} | all-to-all | bytes 786432 | tf_op jit(solution)/shard_map/all_to_all | solution.py:445
  62.8 1.1 %shard_map.88 = bf16[2,8,32,128]{3,2,1,0:T(8,128)(2,1)} custom-call(s32[1,1]{1,0:T(1,128)S(6)} %copy.11.span_ref, bf16[2,16,48,128]{3,2,1,0:T(8,128)(2,1)S(1)} %bitcast.16), custom_call_target="tpu_custom_call" | custom-call | flops 10000000 | bytes 700000 | tf_op jit(solution)/shard_map/pallas_call | solution.py:449
  (1 shorter events, 0.0 us)
Async XLA Ops:
  3.2 15.6 %collective-permute-start.1 = (bf16[256,512]{1,0:T(8,128)(2,1)}, bf16[256,512]{1,0:T(8,128)(2,1)S(1)}, u32[]{:S(2)}, u32[]{:S(2)}) collective-permute-start(bf16[256,512]{1,0:T(8,128)(2,1)} %shard_map.82), channel_id=1, source_target_pairs={{0,256},{256,0},{1,257},{257,1},{2,258},{258,2},{3,259},{259,3},{4... | collective-permute-start | bytes 786440 | tf_op jit(solution)/shard_map/ppermute | solution.py:387
  7.2 11.6 %copy-start.1 = (bf16[1,1,1024,512]{3,2,1,0:T(8,128)(2,1)S(1)}, bf16[1,1,1024,512]{3,2,1,0:T(8,128)(2,1)}, u32[]{:S(2)}) copy-start(bf16[1,1,1024,512]{3,2,1,0:T(8,128)(2,1)} %param.8) | copy-start | bytes 3145732
  12.0 10.7 %collective-permute-start = (bf16[8,560,128]{2,1,0:T(8,128)(2,1)}, bf16[8,560,128]{2,1,0:T(8,128)(2,1)S(1)}, u32[]{:S(2)}, u32[]{:S(2)}) collective-permute-start(bf16[8,560,128]{2,1,0:T(8,128)(2,1)} %get-tuple-element.12), channel_id=1, source_target_pairs={{0,1},{1,0},{2,3},{3,2},{4,5},{5,4},{6,7},{7,6},{8,9},{9,8},{10,11... | collective-permute-start | bytes 3440648 | tf_op jit(solution)/shard_map/ppermute | solution.py:412
  19.2 3.6 %copy-start = (bf16[8,512,128]{2,1,0:T(8,128)(2,1)S(1)}, bf16[8,512,128]{2,1,0:T(8,128)(2,1)}, u32[]{:S(2)}) copy-start(bf16[8,512,128]{2,1,0:T(8,128)(2,1)} %get-tuple-element.15.value_ref) | copy-start | bytes 3145732
  19.2 3.6 %copy-start.3 = (bf16[8,48,128]{2,1,0:T(8,128)(2,1)S(1)}, bf16[8,48,128]{2,1,0:T(8,128)(2,1)}, u32[]{:S(2)}) copy-start(bf16[8,48,128]{2,1,0:T(8,128)(2,1)} %get-tuple-element.16.mine_ref) | copy-start | bytes 294916
  19.2 3.6 %collective-permute-start.2 = (bf16[8,128,128]{2,1,0:T(8,128)(2,1)S(1)}, bf16[8,128,128]{2,1,0:T(8,128)(2,1)S(1)}, u32[]{:S(2)}, u32[]{:S(2)}) collective-permute-start(bf16[8,128,128]{2,1,0:T(8,128)(2,1)S(1)} %shard_map.84), channel_id=1, source_target_pairs={{0,1},{1,0},{2,3},{3,2},{4,5},{5,4},{6,7},{7,6},{8,9},{9,8},{10,11... | collective-permute-start | bytes 786440 | tf_op jit(solution)/shard_map/ppermute | solution.py:421
  23.5 23.4 %copy-start.2 = (bf16[1,2,4,8192]{3,2,1,0:T(4,128)(2,1)S(1)}, bf16[1,2,4,8192]{3,2,1,0:T(4,128)(2,1)}, u32[]{:S(2)}) copy-start(bf16[1,2,4,8192]{3,2,1,0:T(4,128)(2,1)} %param.14) | copy-start | bytes 393220
  23.5 23.4 %copy-start.4 = (bf16[1,2,4,2048]{3,2,1,0:T(4,128)(2,1)S(1)}, bf16[1,2,4,2048]{3,2,1,0:T(4,128)(2,1)}, u32[]{:S(2)}) copy-start(bf16[1,2,4,2048]{3,2,1,0:T(4,128)(2,1)} %param.15) | copy-start | bytes 98308

commit v10 on v8

--- a/solution.py
+++ b/solution.py
@@ -117,12 +117,14 @@
     core = lax.axis_index("core")
     me = lax.axis_index("yx") * 2 + core
     slab = cache_ref.shape[1]
-    span = acts_ref.shape[0]
-    half = span // 2
+    half = acts_ref.shape[1]
     order = (1 - core, core)
-    early = [
-        pltpu.make_async_copy(acts_hbm, acts_ref, sems.at[5]),
-        pltpu.make_async_copy(w_hbm.at[:, COLS : 2 * COLS], w_ref, sems.at[6]),
+    early = [pltpu.make_async_copy(w_hbm.at[:, COLS : 2 * COLS], w_ref, sems.at[6])]
+    early += [
+        pltpu.make_async_copy(
+            acts_hbm.at[pl.ds(pl.multiple_of(row * half, half), half)], acts_ref.at[k], sems.at[at]
+        )
+        for k, (row, at) in enumerate(zip(order, (5, 11)))
     ]
     loads = [
         pltpu.make_async_copy(owner_hbm, owner_ref, sems.at[0]),
@@ -141,11 +143,10 @@
     ]
     for copy in (*early, *loads):
         copy.start()
-    for copy in early:
-        copy.wait()
-    for k, row in enumerate(order):
-        tokens = acts_ref[pl.ds(pl.multiple_of(row * half, half), half), :]
-        value = dot_nn(tokens, w_ref[...]).astype(bf16)
+    early[0].wait()
+    for k in range(2):
+        early[1 + k].wait()
+        value = dot_nn(acts_ref[k], w_ref[...]).astype(bf16)
         for head in range(KVH):
             value_ref[k, head] = value[:, head_cols(head)]
         stores[k].start()
@@ -188,22 +189,30 @@
         store.wait()
 
 
-def absorb_kernel(span_ref, q_hbm, w_hbm, out_ref, q_ref, w_ref, sems):
-    middle = COLS // 2
+def absorb_kernel(span_ref, q_hbm, w_hbm, out_hbm, q_ref, w_ref, out_ref, sems):
+    part = w_ref.shape[0] // 2
     row = span_ref[0, 0]
-    first = pltpu.make_async_copy(q_hbm.at[row], q_ref, sems.at[2])
+    first = pltpu.make_async_copy(q_hbm.at[row], q_ref, sems.at[0])
+    parts = [slice(k * part, (k + 1) * part) for k in range(2)]
     loads = [
-        pltpu.make_async_copy(w_hbm.at[:, cols], w_ref.at[:, cols], sems.at[k])
-        for k, cols in enumerate((slice(0, middle), slice(middle, COLS)))
+        pltpu.make_async_copy(w_hbm.at[rows, 0:COLS], w_ref.at[rows], sems.at[1 + k])
+        for k, rows in enumerate(parts)
+    ]
+    stores = [
+        pltpu.make_async_copy(out_ref.at[:, cols], out_hbm.at[:, cols], sems.at[3 + k])
+        for k, cols in enumerate(parts)
     ]
     for copy in (first, *loads):
         copy.start()
     first.wait()
-    for head in range(KVH):
-        if head * HD % middle == 0:
-            loads[head * HD // middle].wait()
-        rows = slice(head * QROWS, (head + 1) * QROWS)
-        out_ref[rows] = dot_nt(q_ref[head], w_ref[:, head_cols(head)]).astype(bf16)
+    for k, cols in enumerate(parts):
+        loads[k].wait()
+        for head in range(KVH):
+            rows = slice(head * QROWS, (head + 1) * QROWS)
+            out_ref[rows, cols] = dot_nt(q_ref[head], w_ref[cols, head_cols(head)]).astype(bf16)
+        stores[k].start()
+    for copy in stores:
+        copy.wait()
 
 
 def other_kernel(qw_ref, acts_ref, out_ref):
@@ -224,7 +233,7 @@
 def pack_kernel(got_ref, score_ref, value_ref, own_ref, mine_ref, out_ref):
     half = value_ref.shape[1]
     tiles = half // HD
-    out_ref[:, :half] = (value_ref[...].astype(f32) + got_ref[:, :half].astype(f32)).astype(bf16)
+    out_ref[:, :half] = value_ref[...] + got_ref[:, :half]
     shape = (KVH, QROWS, HD)
     for tile in range(tiles):
         at = tile * QROWS
@@ -374,10 +383,16 @@
         absorb_kernel,
         struct((KVH * QROWS, width), bf16),
         [S, H, H],
-        [V(query.shape[1:], bf16), V((width, COLS), bf16), dma((3,))],
+        [
+            V(query.shape[1:], bf16),
+            V((width, COLS), bf16),
+            V((KVH * QROWS, width), bf16),
+            dma((5,)),
+        ],
         flops=70_000_000,
         moved=1_500_000,
         limit=FRONT,
+        out_space=H,
     )(span_row, query, kv_weight)
     asked = lax.ppermute(absorbed, "role", swap)
     absorbed, own_query = lax.optimization_barrier((absorbed, query))
@@ -393,11 +408,11 @@
             S(cache_len.shape, jnp.int32),
             V(query.shape, bf16),
             V(cache_kv.shape[1:], bf16),
-            V(acts.shape, bf16),
+            V((2, half, width), bf16),
             V((width, COLS), bf16),
             V((2, KVH, half, HD), bf16),
             V((2, KVH, PAIR, HD), bf16),
-            dma((11,)),
+            dma((12,)),
         ],
         flops=1_500_000_000,
         moved=6_000_000,

time: 64.1 us -> 63.9 us (level)
  no operation moved by 1% of the time
where the time goes in v10:
time: 63.9 us; the launch traced here: 63.6 us
  blocking collectives  38.7 us (61%)
  starting transfers between devices  12.8 us (20%)
  Pallas kernels  10.2 us (16%)
  waiting for transfers between devices  1.16 us (2%)
  between operations  0.78 us (1%)
    all_to_all x1, blocking collectives, shards(): got = lax.all_to_all(sent, 'yx', 0, 0, tiled=True)  23 us
    all_to_all x1, blocking collectives, shards(): lax.all_to_all(parts.reshape(4 * n_yx, PAIR, HD), ('role', 'yx', 'core'),...  15.7 us
    ppermute x1, starting transfers between devices, shards(): theirs = lax.ppermute(away, 'core', swap)  6.76 us
    pallas_call x1, Pallas kernels, shards(): call(front_kernel, [away, struct((KVH, half, HD), bf16), struct((KVH, PAI...  4.68 us
    ppermute x1, starting transfers between devices, shards(): asked = lax.ppermute(absorbed, 'role', swap)  3.95 us
    pallas_call x1, Pallas kernels, shards(): call(absorb_kernel, struct((KVH * QROWS, width), bf16), [S, H, H], [V(que...  2.38 us
    ppermute x1, starting transfers between devices, shards(): score = lax.ppermute(score, 'core', swap)  2.05 us
  transfers between devices with their start and end apart: 3, of which 1 were waited for; matrix products, arithmetic and copies ran while one was open for 0% of the time, Pallas kernels for 8%

profile of v10, /device:TPU:1, one launch (start us, length us, event | category | flops | bytes accessed | tf_op | source)
XLA Modules:
  0.0 63.6 jit_solution(13232261925450442326)
XLA Ops:
  0.7 2.4 %shard_map.82 = bf16[256,512]{1,0:T(8,128)(2,1)} custom-call(s32[1,1]{1,0:T(1,128)S(6)} %copy.11.span_ref, bf16[2,8,32,128]{3,2,1,0:T(8,128)(2,1)} %bitcast.21, bf16[512,2048]{1,0:T(8,128)(2,1)} %w_hbm.3), custom_call_target="tpu_custom_call" | custom-call | flops 70000000 | bytes 1500000 | tf_op jit(solution)/shard_map/pallas_call | solution.py:382
  3.0 3.9 %collective-permute-start.1 = (bf16[256,512]{1,0:T(8,128)(2,1)}, bf16[256,512]{1,0:T(8,128)(2,1)S(1)}, u32[]{:S(2)}, u32[]{:S(2)}) collective-permute-start(bf16[256,512]{1,0:T(8,128)(2,1)} %shard_map.82), channel_id=1, source_target_pairs={{0,256},{256,0},{1,257},{257,1},{2,258},{258,2},{3,259},{259,3},{4... | collective-permute-start | bytes 786440 | tf_op jit(solution)/shard_map/ppermute | solution.py:397
  7.0 0.0 copy-start.1
  7.0 4.7 %shard_map.83 = (bf16[8,560,128]{2,1,0:T(8,128)(2,1)}, bf16[8,512,128]{2,1,0:T(8,128)(2,1)}, bf16[8,48,128]{2,1,0:T(8,128)(2,1)}) custom-call(s32[2,16]{1,0:T(2,128)} %bitcast.26, s32[1,2]{1,0:T(1,128)} %len_hbm.1, bf16[2,8,32,128]{3,2,1,0:T(8,128)(2,1)} %bitcast.22, bf16[2,192,2048]{2,1,0:T(8,128)(2,1)} %bitcast.25, bf16[1024,512]{1,0:T(8,128)(2,1)} %bitcast.18, ...), custom_call_target="tpu_custom_call" | custom-call | flops 1500000000 | bytes 6000000 | tf_op jit(solution)/shard_map/pallas_call | solution.py:402
  11.7 6.8 %collective-permute-start = (bf16[8,560,128]{2,1,0:T(8,128)(2,1)}, bf16[8,560,128]{2,1,0:T(8,128)(2,1)S(1)}, u32[]{:S(2)}, u32[]{:S(2)}) collective-permute-start(bf16[8,560,128]{2,1,0:T(8,128)(2,1)} %get-tuple-element.12), channel_id=1, source_target_pairs={{0,1},{1,0},{2,3},{3,2},{4,5},{5,4},{6,7},{7,6},{8,9},{9,8},{10,11... | collective-permute-start | bytes 3440648 | tf_op jit(solution)/shard_map/ppermute | solution.py:422
  18.5 0.0 collective-permute-done.1.qw_ref
  18.5 0.0 copy-done.1
  18.5 0.3 shard_map.84
  18.8 0.0 copy-start
  18.8 0.0 copy-start.3
  18.9 2.1 %collective-permute-start.2 = (bf16[8,128,128]{2,1,0:T(8,128)(2,1)S(1)}, bf16[8,128,128]{2,1,0:T(8,128)(2,1)S(1)}, u32[]{:S(2)}, u32[]{:S(2)}) collective-permute-start(bf16[8,128,128]{2,1,0:T(8,128)(2,1)S(1)} %shard_map.84), channel_id=1, source_target_pairs={{0,1},{1,0},{2,3},{3,2},{4,5},{5,4},{6,7},{7,6},{8,9},{9,8},{10,11... | collective-permute-start | bytes 786440 | tf_op jit(solution)/shard_map/ppermute | solution.py:431
  20.9 0.3 shard_map.85.own_ref
  21.3 1.2 %collective-permute-done.2.score_ref = bf16[8,128,128]{2,1,0:T(8,128)(2,1)S(1)} collective-permute-done((bf16[8,128,128]{2,1,0:T(8,128)(2,1)S(1)}, bf16[8,128,128]{2,1,0:T(8,128)(2,1)S(1)}, u32[]{:S(2)}, u32[]{:S(2)}) %collective-permute-start.2) | collective-permute-done | bytes 262176 | tf_op jit(solution)/shard_map/ppermute | solution.py:431
  22.4 0.0 collective-permute-done.got_ref
  22.4 0.0 copy-done
  22.4 0.0 copy-done.3
  22.4 0.8 %shard_map.86 = bf16[8,688,128]{2,1,0:T(8,128)(2,1)S(1)} custom-call(bf16[8,560,128]{2,1,0:T(8,128)(2,1)S(1)} %collective-permute-done.got_ref, bf16[8,128,128]{2,1,0:T(8,128)(2,1)S(1)} %collective-permute-done.2.score_ref, bf16[8,512,128]{2,1,0:T(8,128)(2,1)S(1)} %copy-done, f32[256,512]{1,0:T(8,128)S(1)} %shard_map.85.own_ref, ...), custom_call_target="tpu_custom_call" | custom-call | flops 10000000 | bytes 5000000 | tf_op jit(solution)/shard_map/pallas_call | solution.py:439
  23.2 0.0 copy-start.2
  23.2 0.0 copy-start.4
  23.2 23.0 %all_to_all.10.got_ref = bf16[8,688,128]{2,1,0:T(8,128)(2,1)S(1)} all-to-all(bf16[8,688,128]{2,1,0:T(8,128)(2,1)S(1)} %shard_map.86), channel_id=1, replica_groups=mesh['role'=2,'grp'=16,'yx'=8,'core'=2] {'yx'}, dimensions={0} | all-to-all | bytes 2818048 | tf_op jit(solution)/shard_map/all_to_all | solution.py:446
  46.2 0.0 copy-done.2
  46.2 0.6 shard_map.87
  46.8 15.7 %all_to_all.11 = bf16[32,48,128]{2,1,0:T(8,128)(2,1)S(1)} all-to-all(bf16[32,48,128]{2,1,0:T(8,128)(2,1)S(1)} %bitcast.17), channel_id=1, replica_groups=mesh['role'=2,'grp'=16,'yx'=8,'core'=2] {'role','yx','core'}, dimensions={0} | all-to-all | bytes 786432 | tf_op jit(solution)/shard_map/all_to_all | solution.py:455
  62.5 1.1 %shard_map.88 = bf16[2,8,32,128]{3,2,1,0:T(8,128)(2,1)} custom-call(s32[1,1]{1,0:T(1,128)S(6)} %copy.11.span_ref, bf16[2,16,48,128]{3,2,1,0:T(8,128)(2,1)S(1)} %bitcast.16), custom_call_target="tpu_custom_call" | custom-call | flops 10000000 | bytes 700000 | tf_op jit(solution)/shard_map/pallas_call | solution.py:459
  (1 shorter events, 0.0 us)
Async XLA Ops:
  3.0 15.4 %collective-permute-start.1 = (bf16[256,512]{1,0:T(8,128)(2,1)}, bf16[256,512]{1,0:T(8,128)(2,1)S(1)}, u32[]{:S(2)}, u32[]{:S(2)}) collective-permute-start(bf16[256,512]{1,0:T(8,128)(2,1)} %shard_map.82), channel_id=1, source_target_pairs={{0,256},{256,0},{1,257},{257,1},{2,258},{258,2},{3,259},{259,3},{4... | collective-permute-start | bytes 786440 | tf_op jit(solution)/shard_map/ppermute | solution.py:397
  7.0 11.5 %copy-start.1 = (bf16[1,1,1024,512]{3,2,1,0:T(8,128)(2,1)S(1)}, bf16[1,1,1024,512]{3,2,1,0:T(8,128)(2,1)}, u32[]{:S(2)}) copy-start(bf16[1,1,1024,512]{3,2,1,0:T(8,128)(2,1)} %param.8) | copy-start | bytes 3145732
  11.7 10.7 %collective-permute-start = (bf16[8,560,128]{2,1,0:T(8,128)(2,1)}, bf16[8,560,128]{2,1,0:T(8,128)(2,1)S(1)}, u32[]{:S(2)}, u32[]{:S(2)}) collective-permute-start(bf16[8,560,128]{2,1,0:T(8,128)(2,1)} %get-tuple-element.12), channel_id=1, source_target_pairs={{0,1},{1,0},{2,3},{3,2},{4,5},{5,4},{6,7},{7,6},{8,9},{9,8},{10,11... | collective-permute-start | bytes 3440648 | tf_op jit(solution)/shard_map/ppermute | solution.py:422
  18.8 3.6 %copy-start = (bf16[8,512,128]{2,1,0:T(8,128)(2,1)S(1)}, bf16[8,512,128]{2,1,0:T(8,128)(2,1)}, u32[]{:S(2)}) copy-start(bf16[8,512,128]{2,1,0:T(8,128)(2,1)} %get-tuple-element.15.value_ref) | copy-start | bytes 3145732
  18.8 3.6 %copy-start.3 = (bf16[8,48,128]{2,1,0:T(8,128)(2,1)S(1)}, bf16[8,48,128]{2,1,0:T(8,128)(2,1)}, u32[]{:S(2)}) copy-start(bf16[8,48,128]{2,1,0:T(8,128)(2,1)} %get-tuple-element.16.mine_ref) | copy-start | bytes 294916
  18.9 3.6 %collective-permute-start.2 = (bf16[8,128,128]{2,1,0:T(8,128)(2,1)S(1)}, bf16[8,128,128]{2,1,0:T(8,128)(2,1)S(1)}, u32[]{:S(2)}, u32[]{:S(2)}) collective-permute-start(bf16[8,128,128]{2,1,0:T(8,128)(2,1)S(1)} %shard_map.84), channel_id=1, source_target_pairs={{0,1},{1,0},{2,3},{3,2},{4,5},{5,4},{6,7},{7,6},{8,9},{9,8},{10,11... | collective-permute-start | bytes 786440 | tf_op jit(solution)/shard_map/ppermute | solution.py:431
  23.2 23.0 %copy-start.2 = (bf16[1,2,4,8192]{3,2,1,0:T(4,128)(2,1)S(1)}, bf16[1,2,4,8192]{3,2,1,0:T(4,128)(2,1)}, u32[]{:S(2)}) copy-start(bf16[1,2,4,8192]{3,2,1,0:T(4,128)(2,1)} %param.14) | copy-start | bytes 393220
  23.2 23.0 %copy-start.4 = (bf16[1,2,4,2048]{3,2,1,0:T(4,128)(2,1)S(1)}, bf16[1,2,4,2048]{3,2,1,0:T(4,128)(2,1)}, u32[]{:S(2)}) copy-start(bf16[1,2,4,2048]{3,2,1,0:T(4,128)(2,1)} %param.15) | copy-start | bytes 98308

commit v11 on v10

--- a/solution.py
+++ b/solution.py
@@ -48,6 +48,24 @@
     return jnp.concatenate([rows, jnp.zeros((STAT, HD - QROWS), f32)], axis=1).astype(bf16)
 
 
+def packed_stats(lse):
+    count = lse.shape[0] // QROWS
+    lane = lax.broadcasted_iota(jnp.int32, (QROWS, HD), 1)
+    tile = jnp.zeros((QROWS, HD), f32)
+    for head in range(count):
+        tile = jnp.where(lane >> 3 == head, lse[head * QROWS : (head + 1) * QROWS], tile)
+    term = lane & 7
+    packed = jnp.zeros((QROWS, HD), f32)
+    for at, part in enumerate(terms(tile)):
+        packed = jnp.where(term == at, part, packed)
+    rows = jnp.concatenate([packed.T, jnp.zeros((HD, HD - QROWS), f32)], axis=1)
+    spare = jnp.zeros((STAT - 8, HD), f32)
+    return [
+        jnp.concatenate([rows[head * 8 : head * 8 + 8], spare], axis=0).astype(bf16)
+        for head in range(count)
+    ]
+
+
 def stat_row(tile):
     rows = tile.astype(f32)
     return rows[0:1] + rows[1:2] + rows[2:3]
@@ -83,15 +101,6 @@
 
 def head_cols(head, start=0):
     return slice(start + head * HD, start + (head + 1) * HD)
-
-
-def put_pair(out_ref, start, out, lse):
-    middle = start + QROWS
-    out_ref[:, start:middle] = out.astype(bf16).reshape(KVH, QROWS, HD)
-    for head in range(KVH):
-        out_ref[head, middle : middle + STAT] = packed_stat(
-            lse[head * QROWS : (head + 1) * QROWS]
-        )
 
 
 def front_kernel(
@@ -180,9 +189,10 @@
     )
     out = out / safe
     lse = jnp.where(total > 0.0, top + jnp.log(safe), NEG)
-    middle = KVH * QROWS
-    put_pair(pair_ref.at[0], 0, out[:middle], lse[:middle])
-    put_pair(pair_ref.at[1], 0, out[middle:], lse[middle:])
+    packed = packed_stats(lse)
+    for at, (k, _, head) in enumerate(places):
+        pair_ref[k, head, :QROWS] = out[at * QROWS : (at + 1) * QROWS].astype(bf16)
+        pair_ref[k, head, QROWS:] = packed[at]
     for store in stores[2:]:
         store.start()
     for store in stores:

time: 63.9 us -> 63.9 us (level)
  no operation moved by 1% of the time
where the time goes in v11:
time: 63.9 us; the launch traced here: 63.6 us
  blocking collectives  38.7 us (61%)
  starting transfers between devices  12.8 us (20%)
  Pallas kernels  10.2 us (16%)
  waiting for transfers between devices  1.16 us (2%)
  between operations  0.78 us (1%)
    all_to_all x1, blocking collectives, shards(): got = lax.all_to_all(sent, 'yx', 0, 0, tiled=True)  23 us
    all_to_all x1, blocking collectives, shards(): lax.all_to_all(parts.reshape(4 * n_yx, PAIR, HD), ('role', 'yx', 'core'),...  15.7 us
    ppermute x1, starting transfers between devices, shards(): theirs = lax.ppermute(away, 'core', swap)  6.76 us
    pallas_call x1, Pallas kernels, shards(): call(front_kernel, [away, struct((KVH, half, HD), bf16), struct((KVH, PAI...  4.65 us
    ppermute x1, starting transfers between devices, shards(): asked = lax.ppermute(absorbed, 'role', swap)  3.95 us
    pallas_call x1, Pallas kernels, shards(): call(absorb_kernel, struct((KVH * QROWS, width), bf16), [S, H, H], [V(que...  2.38 us
    ppermute x1, starting transfers between devices, shards(): score = lax.ppermute(score, 'core', swap)  2.05 us
  transfers between devices with their start and end apart: 3, of which 1 were waited for; matrix products, arithmetic and copies ran while one was open for 0% of the time, Pallas kernels for 8%

profile of v11, /device:TPU:1, one launch (start us, length us, event | category | flops | bytes accessed | tf_op | source)
XLA Modules:
  0.0 63.6 jit_solution(7469277611328259319)
XLA Ops:
  0.7 2.4 %shard_map.82 = bf16[256,512]{1,0:T(8,128)(2,1)} custom-call(s32[1,1]{1,0:T(1,128)S(6)} %copy.11.span_ref, bf16[2,8,32,128]{3,2,1,0:T(8,128)(2,1)} %bitcast.21, bf16[512,2048]{1,0:T(8,128)(2,1)} %w_hbm.3), custom_call_target="tpu_custom_call" | custom-call | flops 70000000 | bytes 1500000 | tf_op jit(solution)/shard_map/pallas_call | solution.py:392
  3.0 3.9 %collective-permute-start.1 = (bf16[256,512]{1,0:T(8,128)(2,1)}, bf16[256,512]{1,0:T(8,128)(2,1)S(1)}, u32[]{:S(2)}, u32[]{:S(2)}) collective-permute-start(bf16[256,512]{1,0:T(8,128)(2,1)} %shard_map.82), channel_id=1, source_target_pairs={{0,256},{256,0},{1,257},{257,1},{2,258},{258,2},{3,259},{259,3},{4... | collective-permute-start | bytes 786440 | tf_op jit(solution)/shard_map/ppermute | solution.py:407
  7.0 0.0 copy-start.1
  7.0 4.7 %shard_map.83 = (bf16[8,560,128]{2,1,0:T(8,128)(2,1)}, bf16[8,512,128]{2,1,0:T(8,128)(2,1)}, bf16[8,48,128]{2,1,0:T(8,128)(2,1)}) custom-call(s32[2,16]{1,0:T(2,128)} %bitcast.26, s32[1,2]{1,0:T(1,128)} %len_hbm.1, bf16[2,8,32,128]{3,2,1,0:T(8,128)(2,1)} %bitcast.22, bf16[2,192,2048]{2,1,0:T(8,128)(2,1)} %bitcast.25, bf16[1024,512]{1,0:T(8,128)(2,1)} %bitcast.18, ...), custom_call_target="tpu_custom_call" | custom-call | flops 1500000000 | bytes 6000000 | tf_op jit(solution)/shard_map/pallas_call | solution.py:412
  11.7 6.8 %collective-permute-start = (bf16[8,560,128]{2,1,0:T(8,128)(2,1)}, bf16[8,560,128]{2,1,0:T(8,128)(2,1)S(1)}, u32[]{:S(2)}, u32[]{:S(2)}) collective-permute-start(bf16[8,560,128]{2,1,0:T(8,128)(2,1)} %get-tuple-element.12), channel_id=1, source_target_pairs={{0,1},{1,0},{2,3},{3,2},{4,5},{5,4},{6,7},{7,6},{8,9},{9,8},{10,11... | collective-permute-start | bytes 3440648 | tf_op jit(solution)/shard_map/ppermute | solution.py:432
  18.4 0.0 collective-permute-done.1.qw_ref
  18.4 0.0 copy-done.1
  18.5 0.3 shard_map.84
  18.8 0.0 copy-start
  18.8 0.0 copy-start.3
  18.8 2.1 %collective-permute-start.2 = (bf16[8,128,128]{2,1,0:T(8,128)(2,1)S(1)}, bf16[8,128,128]{2,1,0:T(8,128)(2,1)S(1)}, u32[]{:S(2)}, u32[]{:S(2)}) collective-permute-start(bf16[8,128,128]{2,1,0:T(8,128)(2,1)S(1)} %shard_map.84), channel_id=1, source_target_pairs={{0,1},{1,0},{2,3},{3,2},{4,5},{5,4},{6,7},{7,6},{8,9},{9,8},{10,11... | collective-permute-start | bytes 786440 | tf_op jit(solution)/shard_map/ppermute | solution.py:441
  20.9 0.3 shard_map.85.own_ref
  21.2 1.2 %collective-permute-done.2.score_ref = bf16[8,128,128]{2,1,0:T(8,128)(2,1)S(1)} collective-permute-done((bf16[8,128,128]{2,1,0:T(8,128)(2,1)S(1)}, bf16[8,128,128]{2,1,0:T(8,128)(2,1)S(1)}, u32[]{:S(2)}, u32[]{:S(2)}) %collective-permute-start.2) | collective-permute-done | bytes 262176 | tf_op jit(solution)/shard_map/ppermute | solution.py:441
  22.4 0.0 collective-permute-done.got_ref
  22.4 0.0 copy-done
  22.4 0.0 copy-done.3
  22.4 0.8 %shard_map.86 = bf16[8,688,128]{2,1,0:T(8,128)(2,1)S(1)} custom-call(bf16[8,560,128]{2,1,0:T(8,128)(2,1)S(1)} %collective-permute-done.got_ref, bf16[8,128,128]{2,1,0:T(8,128)(2,1)S(1)} %collective-permute-done.2.score_ref, bf16[8,512,128]{2,1,0:T(8,128)(2,1)S(1)} %copy-done, f32[256,512]{1,0:T(8,128)S(1)} %shard_map.85.own_ref, ...), custom_call_target="tpu_custom_call" | custom-call | flops 10000000 | bytes 5000000 | tf_op jit(solution)/shard_map/pallas_call | solution.py:449
  23.2 0.0 copy-start.2
  23.2 0.0 copy-start.4
  23.2 23.0 %all_to_all.10.got_ref = bf16[8,688,128]{2,1,0:T(8,128)(2,1)S(1)} all-to-all(bf16[8,688,128]{2,1,0:T(8,128)(2,1)S(1)} %shard_map.86), channel_id=1, replica_groups=mesh['role'=2,'grp'=16,'yx'=8,'core'=2] {'yx'}, dimensions={0} | all-to-all | bytes 2818048 | tf_op jit(solution)/shard_map/all_to_all | solution.py:456
  46.2 0.0 copy-done.2
  46.2 0.6 shard_map.87
  46.8 15.7 %all_to_all.11 = bf16[32,48,128]{2,1,0:T(8,128)(2,1)S(1)} all-to-all(bf16[32,48,128]{2,1,0:T(8,128)(2,1)S(1)} %bitcast.17), channel_id=1, replica_groups=mesh['role'=2,'grp'=16,'yx'=8,'core'=2] {'role','yx','core'}, dimensions={0} | all-to-all | bytes 786432 | tf_op jit(solution)/shard_map/all_to_all | solution.py:465
  62.5 1.1 %shard_map.88 = bf16[2,8,32,128]{3,2,1,0:T(8,128)(2,1)} custom-call(s32[1,1]{1,0:T(1,128)S(6)} %copy.11.span_ref, bf16[2,16,48,128]{3,2,1,0:T(8,128)(2,1)S(1)} %bitcast.16), custom_call_target="tpu_custom_call" | custom-call | flops 10000000 | bytes 700000 | tf_op jit(solution)/shard_map/pallas_call | solution.py:469
  (1 shorter events, 0.0 us)
Async XLA Ops:
  3.0 15.4 %collective-permute-start.1 = (bf16[256,512]{1,0:T(8,128)(2,1)}, bf16[256,512]{1,0:T(8,128)(2,1)S(1)}, u32[]{:S(2)}, u32[]{:S(2)}) collective-permute-start(bf16[256,512]{1,0:T(8,128)(2,1)} %shard_map.82), channel_id=1, source_target_pairs={{0,256},{256,0},{1,257},{257,1},{2,258},{258,2},{3,259},{259,3},{4... | collective-permute-start | bytes 786440 | tf_op jit(solution)/shard_map/ppermute | solution.py:407
  7.0 11.5 %copy-start.1 = (bf16[1,1,1024,512]{3,2,1,0:T(8,128)(2,1)S(1)}, bf16[1,1,1024,512]{3,2,1,0:T(8,128)(2,1)}, u32[]{:S(2)}) copy-start(bf16[1,1,1024,512]{3,2,1,0:T(8,128)(2,1)} %param.8) | copy-start | bytes 3145732
  11.7 10.7 %collective-permute-start = (bf16[8,560,128]{2,1,0:T(8,128)(2,1)}, bf16[8,560,128]{2,1,0:T(8,128)(2,1)S(1)}, u32[]{:S(2)}, u32[]{:S(2)}) collective-permute-start(bf16[8,560,128]{2,1,0:T(8,128)(2,1)} %get-tuple-element.12), channel_id=1, source_target_pairs={{0,1},{1,0},{2,3},{3,2},{4,5},{5,4},{6,7},{7,6},{8,9},{9,8},{10,11... | collective-permute-start | bytes 3440648 | tf_op jit(solution)/shard_map/ppermute | solution.py:432
  18.8 3.6 %copy-start = (bf16[8,512,128]{2,1,0:T(8,128)(2,1)S(1)}, bf16[8,512,128]{2,1,0:T(8,128)(2,1)}, u32[]{:S(2)}) copy-start(bf16[8,512,128]{2,1,0:T(8,128)(2,1)} %get-tuple-element.15.value_ref) | copy-start | bytes 3145732
  18.8 3.6 %copy-start.3 = (bf16[8,48,128]{2,1,0:T(8,128)(2,1)S(1)}, bf16[8,48,128]{2,1,0:T(8,128)(2,1)}, u32[]{:S(2)}) copy-start(bf16[8,48,128]{2,1,0:T(8,128)(2,1)} %get-tuple-element.16.mine_ref) | copy-start | bytes 294916
  18.8 3.6 %collective-permute-start.2 = (bf16[8,128,128]{2,1,0:T(8,128)(2,1)S(1)}, bf16[8,128,128]{2,1,0:T(8,128)(2,1)S(1)}, u32[]{:S(2)}, u32[]{:S(2)}) collective-permute-start(bf16[8,128,128]{2,1,0:T(8,128)(2,1)S(1)} %shard_map.84), channel_id=1, source_target_pairs={{0,1},{1,0},{2,3},{3,2},{4,5},{5,4},{6,7},{7,6},{8,9},{9,8},{10,11... | collective-permute-start | bytes 786440 | tf_op jit(solution)/shard_map/ppermute | solution.py:441
  23.2 23.0 %copy-start.2 = (bf16[1,2,4,8192]{3,2,1,0:T(4,128)(2,1)S(1)}, bf16[1,2,4,8192]{3,2,1,0:T(4,128)(2,1)}, u32[]{:S(2)}) copy-start(bf16[1,2,4,8192]{3,2,1,0:T(4,128)(2,1)} %param.14) | copy-start | bytes 393220
  23.2 23.0 %copy-start.4 = (bf16[1,2,4,2048]{3,2,1,0:T(4,128)(2,1)S(1)}, bf16[1,2,4,2048]{3,2,1,0:T(4,128)(2,1)}, u32[]{:S(2)}) copy-start(bf16[1,2,4,2048]{3,2,1,0:T(4,128)(2,1)} %param.15) | copy-start | bytes 98308
